TPU v7x, 256 devices: a whole 4x4x8 slice. The times are simulated.
256 devices in a mesh: dp: 8 (over y, core), row: 2 (over x_lo), col: 16 (over z, x_hi).
Axes of the slice: x: 4 (x_hi: 2, x_lo: 2; x = x_hi * 2 + x_lo), y: 4, z: 8, core: 2. Of those that a mesh axis runs over, the one named last changes fastest.
Arguments:
- activations: bfloat16 [4096, 53248], P('dp', ('row', 'col')), may hold values from -6 to 6
- weights: bfloat16 [53248, 8192], P(('row', 'col'), 'dp'), may hold values from -6 to 6
- codes: int32 [1024, 8192], P(None, 'dp'), may hold values from 0 to 15
- scale_index: int32 [8, 8192], P(None, 'dp'), may hold values from 0 to 15
- scale_table: float32 [16], replicated, may hold values from 0.1 to 0.3
- inverse_block: float32 [1024, 1024], P(('row', 'col')), may hold values from -0.1875 to 0.1875
- block_index: int32 [1], replicated, may hold values from 0 to 25
Outputs:
- updated: bfloat16 [53248, 8192], P(('row', 'col'), 'dp')
All inputs are finite; a program needn't handle non-finite values.
Results may differ from a plain program's by a relative error of at most 0.001.
Values may be sent and summed in bfloat16 or wider, within the bound.
No kernel may reach another device: no remote copies, remote signals or barrier semaphores. Data moves between devices by JAX's collectives and lax.ppermute only.
A program may use at most 128 MiB of HBM per device.

v0:
```python
import jax
import jax.numpy as jnp
from jax import lax
from jax.sharding import PartitionSpec as P

BLK = 1024
GROUP = 128
LEVELS = 16


def spread(value, axis, source):
    kept = jnp.where(lax.axis_index(axis) == source, value, 0).astype(value.dtype)
    return lax.psum(kept, axis)


def pad_slice(values, offset, length, along, margin):
    widths = [(0, 0)] * values.ndim
    widths[along] = (margin, margin)
    padded = jnp.pad(values, widths)
    begin_at = jnp.clip(offset + margin, 0, values.shape[along] + margin)
    return lax.dynamic_slice_in_dim(padded, begin_at, length, along)


def local(activations, weights, codes, scale_index, scale_table, inverse_block, block_index):
    tile_index = lax.axis_index(("row", "col"))
    shard_rows = weights.shape[0]
    token_total = activations.shape[0] * lax.axis_size("dp")
    first_row = block_index[0] * BLK
    local_start = first_row - tile_index * shard_rows
    own_w = pad_slice(weights, local_start, BLK, 0, BLK)
    own_x = pad_slice(activations, local_start, BLK, 1, BLK)
    first_owner = first_row // shard_rows
    last_owner = (first_row + BLK - 1) // shard_rows

    def from_owner(owner):
        return (spread(own_w, ("row", "col"), owner), spread(own_x, ("row", "col"), owner))

    w_head, x_head = from_owner(first_owner)
    w_tail, x_tail = from_owner(last_owner)
    boundary = last_owner * shard_rows - first_row
    block_pos = jnp.arange(BLK, dtype=jnp.int32)
    w_block = jnp.where((block_pos >= boundary)[:, None], w_tail, w_head)
    x_block = jnp.where((block_pos >= boundary)[None, :], x_tail, x_head)
    chosen = (scale_index[:, :, None] == jnp.arange(LEVELS, dtype=jnp.int32)).astype(jnp.float32)
    group_scale = jnp.sum(chosen * scale_table, axis=2)
    scale_rows = jnp.repeat(group_scale, GROUP, axis=0)
    quantized = scale_rows * (codes.astype(jnp.float32) - 7.5)
    deviation = w_block.astype(jnp.float32) - quantized
    error_part = jnp.dot(inverse_block, deviation, precision=lax.Precision.HIGHEST)
    block_error = lax.all_gather(error_part, ("row", "col"), axis=0, tiled=True)
    factor = 2.0 / token_total
    partial_panel = (
        lax.dot_general(
            activations, x_block, (((0,), (0,)), ((), ())), preferred_element_type=jnp.float32
        )
        * factor
    )
    hessian_panel = lax.psum(partial_panel, "dp")
    update = jnp.dot(hessian_panel, block_error, precision=lax.Precision.HIGHEST)
    global_rows = tile_index * shard_rows + jnp.arange(shard_rows, dtype=jnp.int32)
    global_rows = global_rows[:, None]
    quant_local = pad_slice(quantized, -local_start, shard_rows, 0, shard_rows)
    kept_values = weights.astype(jnp.float32)
    result = jnp.where(global_rows >= first_row + BLK, kept_values - update, kept_values)
    result = jnp.where(
        (global_rows >= first_row) & (global_rows < first_row + BLK), quant_local, result
    )
    return result.astype(jnp.bfloat16)


def solution(mesh):
    return jax.shard_map(
        local,
        mesh=mesh,
        in_specs=(
            P("dp", ("row", "col")),
            P(("row", "col"), "dp"),
            P(None, "dp"),
            P(None, "dp"),
            P(),
            P(("row", "col"), None),
            P(),
        ),
        out_specs=P(("row", "col"), "dp"),
        check_vma=False,
    )
```

profile of v0, /device:TPU:24, one launch (start us, length us, event | category | flops | bytes accessed | tf_op | source)
XLA Modules:
  0.0 516.1 jit_solution(14449988105496603214)
XLA Ops:
  6.5 0.0 copy-start
  6.5 0.0 copy-start.2
  6.5 0.0 all-reduce.9.cloned.1.call-start
  7.4 3.8 broadcast_select_fusion
  11.2 0.0 copy-done.2
  11.2 2.0 broadcast_select_fusion.2
  13.3 0.0 all-reduce.9.cloned.1.call-update
  13.3 0.0 all-reduce.7.cloned.1.call-start
  13.4 188.4 %all-reduce.9.cloned.1.call-done = (bf16[512,1024]{1,0:T(8,128)(2,1)}, bf16[512,1024]{1,0:T(8,128)(2,1)}, bf16[1024,1024]{1,0:T(8,128)(2,1)}, bf16[1024,1024]{1,0:T(8,128)(2,1)}) async-done(((bf16[512,1024]{1,0:T(8,128)(2,1)}, bf16[512,1024]{1,0:T(8,128)(2,1)}, bf16[1024,1024]{1,0:T(8,128)(2,1)}, bf16[1024,1024]{1,0:T(8,128)(2,1)}), (bf16[512,1024]{1,0:T(8,128)(2,1)}, bf16[512,1024]{1,0:T(8,128)(2,1)}, ...) | async-done | bytes 6291472 | tf_op jit(solution)/shard_map/psum | solution.py:13
  201.8 6.5 %multiply_bitcast_fusion = f32[1664,1024]{0,1:T(8,128)} fusion(bf16[512,1664]{1,0:T(8,128)(2,1)S(1)} %copy-done.2, bf16[512,1024]{1,0:T(8,128)(2,1)} %get-tuple-element.5, bf16[512,1024]{1,0:T(8,128)(2,1)} %get-tuple-element.6, pred[1024]{0:T(1024)(128)(4,1)S(1)} %iota_compare_fusion.1), kind=kOutput, calls=%fused_computation.5 | convolution fusion | flops 1747058688 | bytes 10617856 | tf_op jit(solution)/shard_map/dot_general | solution.py:53
  208.3 0.0 copy-start.5
  208.3 0.0 copy-start.6
  208.3 0.0 all-reduce.7.cloned.1.call-update
  208.4 0.0 all-gather.2.cloned.1.call-start
  208.4 0.7 copy-done.5
  209.1 0.0 copy-done.6
  209.1 0.2 select_reduce_fusion
  209.3 0.0 copy-start.3
  209.3 0.0 copy-start.4
  209.3 2.9 bitcast_multiply_fusion
  212.2 0.0 copy-start.1
  212.2 1.9 copy-done.1
  214.2 0.0 copy-done
  214.2 0.0 copy-done.3
  214.2 0.0 copy-done.4
  214.2 3.9 fusion.7
  218.1 0.0 all-gather.2.cloned.1.call-update
  218.1 81.4 %all-reduce.7.cloned.1.call-done = f32[1664,1024]{0,1:T(8,128)} async-done(((f32[1664,1024]{0,1:T(8,128)}), f32[1664,1024]{0,1:T(8,128)}) %all-reduce.7.cloned.1.call-update) | async-done | bytes 6815760 | tf_op jit(solution)/shard_map/psum | solution.py:58
  299.6 160.3 %all-gather.2.cloned.1.call-done = f32[1024,1024]{1,0:T(8,128)} async-done(((f32[32,1024]{1,0:T(8,128)}), f32[1024,1024]{1,0:T(8,128)}) %all-gather.2.cloned.1.call-update) | async-done | bytes 4194320 | tf_op jit(solution)/shard_map/all_gather | solution.py:50
  459.8 49.7 %fusion.1 = bf16[1664,1024]{1,0:T(8,128)(2,1)} fusion(s32[]{:T(128)S(6)} %min.8, f32[1024,1024]{1,0:T(8,128)} %copy-done.1, bf16[1664,1024]{1,0:T(8,128)(2,1)} %param.8, f32[1664,1024]{0,1:T(8,128)} %all-reduce.7.cloned.1.call-done, f32[1024,1024]{1,0:T(8,128)} %all-gather.2.cloned.1.call-done, pred[1664]{0:T(1024)(128)(4,1)S(1)} %get-tuple-element.13, ...), kind=kOutput, calls=%fused_computation.4 | convolution fusion | flops 20944781312 | bytes 22023428 | tf_op jit(solution)/shard_map/dot_general | solution.py:59
  (2 shorter events, 0.0 us)
Async XLA Ops:
  6.5 207.6 %copy-start = (f32[32,1024]{1,0:T(8,128)S(1)}, f32[32,1024]{1,0:T(8,128)}, u32[]{:S(2)}) copy-start(f32[32,1024]{1,0:T(8,128)} %param.12) | copy-start | bytes 393220
  6.5 4.7 copy-start.2
  6.5 195.3 %all-reduce.9.cloned.1.call-start = ((), (), s32[]{:S(2)}) async-start(), calls=%async_computation.2 | async-start | bytes 12582912 | tf_op jit(solution)/shard_map/psum | solution.py:13
  13.3 286.2 %all-reduce.7.cloned.1.call-start = ((), (), s32[]{:S(2)}) async-start(), calls=%async_computation | async-start | bytes 13631488 | tf_op jit(solution)/shard_map/psum | solution.py:58
  208.3 0.8 copy-start.5
  208.3 0.8 copy-start.6
  208.4 251.5 %all-gather.2.cloned.1.call-start = ((), (), s32[]{:S(2)}) async-start(), calls=%async_computation.1 | async-start | bytes 4325376 | tf_op jit(solution)/shard_map/all_gather | solution.py:50
  209.3 4.9 copy-start.3
  209.3 4.9 copy-start.4
  212.2 2.0 copy-start.1
Sparse Core Ops, SparseCore 0:
  13.4 188.3 all-reduce.8
  208.5 91.0 all-reduce.6
  301.5 158.3 all-gather.1
where the time goes:
time: 516 us
  waiting for transfers between devices  430 us (83%)
  matrix products  60.1 us (12%)
  between operations  14 us (3%)
  other arithmetic  9.01 us (2%)
    psum x1, waiting for transfers between devices, spread(): return lax.psum(kept, axis)  188 us
    all_gather x1, waiting for transfers between devices, local(): block_error = lax.all_gather(error_part, ('row', 'col'), axis=0, tiled=True)  160 us
    psum x1, waiting for transfers between devices, local(): hessian_panel = lax.psum(partial_panel, 'dp')  81.4 us
    dot_general x1, matrix products, local(): jnp.dot(hessian_panel, block_error, precision=lax.Precision.HIGHEST)  49.7 us
  transfers between devices with their start and end apart: 3, of which 3 were waited for; matrix products, arithmetic and copies ran while one was open for 1% of the time, Pallas kernels for 0%

commit v1 on v0

v1 whole, which is shorter than its diff:
```python
import functools
import jax
import jax.numpy as jnp
from jax import lax
from jax.experimental import pallas as pl
from jax.experimental.pallas import tpu as pltpu
from jax.sharding import Mesh, PartitionSpec as P

BLK = 1024
GROUP = 128
LEVELS = 16
UNIT = 128
UNITS = BLK // UNIT
STEPS_PER_OCTAVE = 128.0
F32, BF16, S16 = jnp.float32, jnp.bfloat16, jnp.int16
PLANE = ("xl", "z", "xh")


def tile_at(x, z):
    return (x % 2) * 16 + (z % 8) * 2 + (x % 4) // 2


def ring(axis, size, shift, value):
    return lax.ppermute(value, axis, [(i, (i + shift) % size) for i in range(size)])


def pick_kernel(index, x_ref, w_ref, x_out, w_out):
    x_out[...] = x_ref[...].reshape(4, 128, UNIT)
    w = w_ref[...]
    for p in range(4):
        w_out[p] = w[:, 256 * p : 256 * (p + 1)]


def pick_units(activations, weights, index):
    tokens, cols = activations.shape[0], weights.shape[1]
    return pl.pallas_call(
        pick_kernel,
        grid_spec=pltpu.PrefetchScalarGridSpec(
            num_scalar_prefetch=1,
            grid=(UNITS,),
            in_specs=[
                pl.BlockSpec((tokens, UNIT), lambda j, u: (0, u[j])),
                pl.BlockSpec((UNIT, cols), lambda j, u: (u[j], 0)),
            ],
            out_specs=[
                pl.BlockSpec((4, 128, UNIT), lambda j, u: (0, 0, j)),
                pl.BlockSpec((4, UNIT, 256), lambda j, u: (0, j, 0)),
            ],
        ),
        out_shape=[
            jax.ShapeDtypeStruct((4, 128, BLK), BF16),
            jax.ShapeDtypeStruct((4, BLK, 256), BF16),
        ],
        name="pick_units",
    )(index, activations, weights)


def scatter_x(pieces, x, xh, from_low):
    def to(shift):
        pairs = [(tile_at(s, z), tile_at(s + shift, z)) for s in (0, 2) for z in range(8)]
        return lax.ppermute(
            lax.dynamic_index_in_dim(pieces, (2 * xh + shift) % 4, 0, False), PLANE, pairs
        )

    up, down, across = to(1), to(3), to(2)
    even = x % 2 == 0
    own = lax.dynamic_index_in_dim(pieces, x, 0, False)
    near = jnp.where(even, own, up)
    far = jnp.where(even, across, down)
    return jnp.where(from_low, near, far)


def spread_z(piece, distance):
    up, down = ring("z", 8, 3, piece), ring("z", 8, -3, piece)
    piece = jnp.where(distance == 3, up, jnp.where(distance == 5, down, piece))
    up, down = ring("z", 8, 1, piece), ring("z", 8, -1, piece)
    from_below = (distance == 1) | (distance == 4) | (distance == 6)
    from_above = (distance == 7) | (distance == 2)
    return jnp.where(from_below, up, jnp.where(from_above, down, piece))


def quantize(values):
    rows = values.shape[-2]
    top = jnp.max(jnp.abs(values), axis=-1, keepdims=True)
    level = jnp.floor(jnp.log2(32700.0 / jnp.maximum(top, 1e-25)) * STEPS_PER_OCTAVE)
    scaled = jnp.round(values * jnp.exp2(level / STEPS_PER_OCTAVE)).astype(jnp.int32).astype(S16)
    levels = jnp.swapaxes(level, -1, -2).astype(jnp.int32).astype(S16)
    widths = [(0, 0)] * (values.ndim - 2) + [(0, 15), (0, values.shape[-1] - rows)]
    return jnp.concatenate([scaled, jnp.pad(levels, widths)], axis=-2)


def scales_of(message):
    rows = message.shape[-2] - 16
    level = message[..., rows : rows + 1, :rows].astype(F32)
    return jnp.swapaxes(jnp.exp2(-level / STEPS_PER_OCTAVE), -1, -2)


def dequantize(message):
    return message[..., :-16, :].astype(F32) * scales_of(message)


def split(values):
    high = values.astype(BF16)
    return high, (values - high.astype(F32)).astype(BF16)


def mm(a, b):
    return jnp.dot(a, b, preferred_element_type=F32)


def error_kernel(inv_ref, w_ref, q_ref, high_ref, low_ref):
    inv_high, inv_low = split(inv_ref[...])
    dev_high, dev_low = split(w_ref[...].astype(F32) - q_ref[...])
    error = mm(inv_high, dev_high) + (mm(inv_high, dev_low) + mm(inv_low, dev_high))
    high_ref[...], low_ref[...] = split(error)


def block_error(inverse, w_block, quantized):
    cols, wide = w_block.shape[1], 256
    stripe = pl.BlockSpec((BLK, wide), lambda i: (0, i))
    return pl.pallas_call(
        error_kernel,
        grid=(cols // wide,),
        in_specs=[pl.BlockSpec((BLK, BLK), lambda i: (0, 0)), stripe, stripe],
        out_specs=[stripe, stripe],
        out_shape=[jax.ShapeDtypeStruct((BLK, cols), BF16)] * 2,
        compiler_params=pltpu.CompilerParams(vmem_limit_bytes=40 << 20),
        cost_estimate=pl.CostEstimate(
            flops=6 * BLK * BLK * cols, bytes_accessed=BLK * cols * 14, transcendentals=0
        ),
        name="block_error",
    )(inverse, w_block, quantized)


def update_kernel(start_ref, h_ref, scale_ref, high_ref, low_ref, base_ref, out_ref):
    rows = out_ref.shape[0]
    h = h_ref[0, 0, :rows].astype(jnp.int32).astype(F32)
    h_high, h_low = split(h)
    update = mm(h_high, high_ref[...]) + (mm(h_high, low_ref[...]) + mm(h_low, high_ref[...]))
    base = base_ref[...].astype(F32)
    row = lax.broadcasted_iota(jnp.int32, base.shape, 0) + pl.program_id(0) * rows
    result = jnp.where(row >= start_ref[0], base - update * scale_ref[0, 0], base)
    out_ref[...] = result.astype(BF16)


def apply_update(start, panel, scales, high, low, base):
    rows, cols = panel.shape[2] - 16, base.shape[1]
    whole = pl.BlockSpec((BLK, cols), lambda i, s: (0, 0))
    stripe = pl.BlockSpec((rows, cols), lambda i, s: (i, 0))
    return pl.pallas_call(
        update_kernel,
        grid_spec=pltpu.PrefetchScalarGridSpec(
            num_scalar_prefetch=1,
            grid=(base.shape[0] // rows,),
            in_specs=[
                pl.BlockSpec((1, 1, rows + 16, BLK), lambda i, s: (i % 4, i // 4, 0, 0)),
                pl.BlockSpec((1, 1, rows, 1), lambda i, s: (i % 4, i // 4, 0, 0)),
                whole,
                whole,
                stripe,
            ],
            out_specs=stripe,
        ),
        out_shape=jax.ShapeDtypeStruct(base.shape, BF16),
        compiler_params=pltpu.CompilerParams(vmem_limit_bytes=40 << 20),
        cost_estimate=pl.CostEstimate(
            flops=6 * base.shape[0] * BLK * cols,
            bytes_accessed=base.shape[0] * cols * 6 + BLK * cols * 4,
            transcendentals=0,
        ),
        name="apply_update",
    )(start, panel, scales, high, low, base)


def local(activations, weights, codes, scale_index, scale_table, inverse_block, block_index):
    y, core = lax.axis_index("y"), lax.axis_index("core")
    xl, z, xh = (lax.axis_index(a) for a in PLANE)
    x = 2 * xh + xl
    tile = lax.axis_index(PLANE)
    shard_rows = weights.shape[0]
    tile_units = shard_rows // UNIT
    token_total = activations.shape[0] * 8
    first_unit = block_index[0] * UNITS
    units = first_unit + jnp.arange(UNITS, dtype=jnp.int32)
    owner = units // tile_units
    x_owner, z_owner = 2 * (owner % 2), (owner // 2) % 8
    distance = (z - z_owner) % 8
    from_low = x_owner == jnp.where(x % 2 == 0, x, (x + 3) % 4)

    own_rows = inverse_block.shape[0] // 2
    inverse_part = lax.dynamic_slice_in_dim(inverse_block, core * own_rows, own_rows, 0)
    inverse = lax.all_gather(inverse_part, ("xh", "xl", "z", "core"), axis=0)
    inverse = inverse.reshape(2, 2, 8, 2, own_rows, BLK).transpose(1, 2, 0, 3, 4, 5)
    inverse = inverse.reshape(BLK, BLK)

    index = jnp.clip(units - tile * tile_units, 0, tile_units - 1)
    x_pieces, w_pieces = pick_units(activations, weights, index)

    half = shard_rows // 2
    x_mine = lax.dynamic_slice_in_dim(activations, core * half, half, 1)
    x_theirs = lax.dynamic_slice_in_dim(activations, (1 - core) * half, half, 1)
    x_other = ring("core", 2, 1, x_theirs)
    x_low = jnp.where(core == 0, x_mine, x_other).reshape(4, 128, half)
    x_high = jnp.where(core == 0, x_other, x_mine).reshape(4, 128, half)
    x_rows = jnp.stack([x_low, x_high], axis=1).reshape(1024, half)

    lanes = lambda v: jnp.repeat(v, UNIT)[None, :]
    sublanes = lambda v: jnp.repeat(v, UNIT)[:, None]
    x_piece = scatter_x(x_pieces, x, xh, lanes(from_low))
    x_piece, w_pieces = lax.optimization_barrier((x_piece, w_pieces))
    w_piece = scatter_x(w_pieces, x, xh, sublanes(from_low))
    x_piece = spread_z(x_piece, lanes(distance))
    x_piece, w_piece = lax.optimization_barrier((x_piece, w_piece))
    w_piece = spread_z(w_piece, sublanes(distance))

    x_block = lax.all_gather(
        x_piece.astype(jnp.float16), ("xh", "xl", "core"), axis=0, tiled=True
    ).astype(BF16)

    partial_panel = lax.dot_general(
        x_rows, x_block, (((0,), (0,)), ((), ())), preferred_element_type=F32
    )
    quarter = half // 4
    parts = partial_panel.reshape(4, quarter, BLK)
    message = quantize(parts)
    total = lax.dynamic_index_in_dim(parts, y, 0, False)
    for shift in (1, 3, 2):
        sent = lax.dynamic_index_in_dim(message, (y + shift) % 4, 0, False)
        total = total + dequantize(ring("y", 4, shift, sent))
    panel = lax.all_gather(quantize(total), ("y", "core"), axis=0)
    panel = panel.reshape(4, 2, quarter + 16, BLK)
    scales = scales_of(panel) * (2.0 / token_total)

    chosen = (scale_index[:, :, None] == jnp.arange(LEVELS, dtype=jnp.int32)).astype(F32)
    group_scale = jnp.sum(chosen * scale_table, axis=2)
    quantized = jnp.repeat(group_scale, GROUP, axis=0) * (codes.astype(F32) - 7.5)

    w_all = lax.all_gather(w_piece.astype(jnp.float16), ("xh", "xl"), axis=0)
    w_block = w_all.transpose(1, 0, 2).reshape(BLK, 1024).astype(BF16)
    high, low = block_error(inverse, w_block, quantized)

    first_local = block_index[0] * BLK - tile * shard_rows
    padded = jnp.pad(quantized.astype(BF16), [(shard_rows, shard_rows), (0, 0)])
    begin = jnp.clip(shard_rows - first_local, 0, BLK + shard_rows)
    quant_rows = lax.dynamic_slice_in_dim(padded, begin, shard_rows, 0)
    row = jnp.arange(shard_rows, dtype=jnp.int32)[:, None] - first_local
    base = jnp.where((row >= 0) & (row < BLK), quant_rows, weights)
    start = (first_local + BLK).reshape(1)
    return apply_update(start, panel, scales, high, low, base)


def solution(mesh):
    cube = Mesh(mesh.devices.reshape(4, 2, 2, 8, 2), ("y", "core") + PLANE)
    return jax.shard_map(
        local,
        mesh=cube,
        in_specs=(
            P(("y", "core"), PLANE),
            P(PLANE, ("y", "core")),
            P(None, ("y", "core")),
            P(None, ("y", "core")),
            P(),
            P(PLANE, None),
            P(),
        ),
        out_specs=P(PLANE, ("y", "core")),
        check_vma=False,
    )
```

time: 516 us -> 223 us (0.43)
  waiting for transfers between devices: 430 us -> 23.8 us
  blocking collectives: 0 us -> 61 us
  matrix products: 60.1 us -> 3.61 us
  starting transfers between devices: 0.09 us -> 43.9 us
  Pallas kernels: 0 us -> 27.7 us
  local copies, waits for them, and re-layouts: 2.65 us -> 22.9 us
  other arithmetic: 9.01 us -> 22.3 us
    psum x2 -> x0, waiting for transfers between devices: 270 us -> none  [the longest x1 188 us: spread(): return lax.psum(kept, axis)]
    all_gather x1, waiting for transfers between devices: 160 us -> 0.01 us  [local(): inverse = lax.all_gather(inverse_part, ('xh', 'xl', 'z', 'core'), axis=0)]
    all_gather x0 -> x3, blocking collectives: none -> 61 us  [the longest x1 21.7 us: local(): w_all = lax.all_gather(w_piece.astype(jnp.float16), ('xh', 'xl'), axis=0)]
    dot_general x3 -> x1, matrix products: 60.1 us -> 3.61 us  [local(): lax.dot_general(x_rows, x_block, (((0,), (0,)), ((), ())), preferred_elem...]
    ppermute x0 -> x18, starting transfers between devices: none -> 43.9 us  [the longest x12 25.8 us: ring(): lax.ppermute(value, axis, [(i, (i + shift) % size) for i in range(size)])]
    pallas_call x0 -> x3, Pallas kernels: none -> 27.7 us  [the longest x1 13.3 us: apply_update(): pl.pallas_call(update_kernel, grid_spec=pltpu.PrefetchScalarGridSpec(num_...]
    ppermute x0 -> x18, waiting for transfers between devices: none -> 23.8 us  [the longest x12 14.3 us: ring(): lax.ppermute(value, axis, [(i, (i + shift) % size) for i in range(size)])]
    convert_element_type x0 -> x8, other arithmetic: none -> 7.38 us  [the longest x1 5.99 us: local(): padded = jnp.pad(quantized.astype(BF16), [(shard_rows, shard_rows), (0, 0)])]
  transfers between devices with their start and end apart: 3 -> 19, of which waited for: 3 -> 6; matrix products, arithmetic and copies ran while one was open for 1% -> 18% of each run, Pallas kernels for 0% -> 0%
where the time goes in v1:
time: 223 us; the launch traced here: 220 us
  blocking collectives  61 us (27%)
  starting transfers between devices  43.9 us (20%)
  Pallas kernels  27.7 us (12%)
  waiting for transfers between devices  23.8 us (11%)
  local copies, waits for them, and re-layouts  22.9 us (10%)
  other arithmetic  22.3 us (10%)
  between operations  14.5 us (7%)
  matrix products  3.61 us (2%)
    ppermute x12, starting transfers between devices, ring(): lax.ppermute(value, axis, [(i, (i + shift) % size) for i in range(size)])  25.8 us
    all_gather x1, blocking collectives, local(): w_all = lax.all_gather(w_piece.astype(jnp.float16), ('xh', 'xl'), axis=0)  21.7 us
    all_gather x1, blocking collectives, local(): panel = lax.all_gather(quantize(total), ('y', 'core'), axis=0)  19.7 us
    all_gather x1, blocking collectives, local(): lax.all_gather(x_piece.astype(jnp.float16), ('xh', 'xl', 'core'), axis=0,...  19.7 us
    ppermute x6, starting transfers between devices, to(): lax.ppermute(lax.dynamic_index_in_dim(pieces, (2 * xh + shift) % 4, 0, Fa...  18.1 us
    ppermute x12, waiting for transfers between devices, ring(): lax.ppermute(value, axis, [(i, (i + shift) % size) for i in range(size)])  14.3 us
    pallas_call x1, Pallas kernels, apply_update(): pl.pallas_call(update_kernel, grid_spec=pltpu.PrefetchScalarGridSpec(num_...  13.3 us
    ppermute x6, waiting for transfers between devices, to(): lax.ppermute(lax.dynamic_index_in_dim(pieces, (2 * xh + shift) % 4, 0, Fa...  9.52 us
  transfers between devices with their start and end apart: 19, of which 6 were waited for; matrix products, arithmetic and copies ran while one was open for 18% of the time, Pallas kernels for 0%

profile of v1, /device:TPU:24, one launch (start us, length us, event | category | flops | bytes accessed | tf_op | source)
XLA Modules:
  0.0 219.8 jit_solution(1367163557006252138)
XLA Ops:
  7.2 0.6 subtract_clamp_fusion.index
  7.8 4.9 %pick_units.1 = (bf16[4,128,1024]{2,1,0:T(8,128)(2,1)}, bf16[4,1024,256]{2,1,0:T(8,128)(2,1)}) custom-call(s32[8]{0:T(128)} %subtract_clamp_fusion.index, bf16[512,1664]{1,0:T(8,128)(2,1)} %x_ref.1, bf16[1664,1024]{1,0:T(8,128)(2,1)} %w_ref.1), custom_call_target="tpu_custom_call" | custom-call | tf_op jit(solution)/shard_map/pick_units/pallas_call | solution.py:36
  12.7 2.1 dynamic-slice_bitcast_fusion.3
  14.8 3.5 %collective-permute-start.1 = (bf16[128,1024]{1,0:T(8,128)(2,1)}, bf16[128,1024]{1,0:T(8,128)(2,1)S(1)}, u32[]{:S(2)}, u32[]{:S(2)}) collective-permute-start(bf16[128,1024]{1,0:T(8,128)(2,1)} %get-tuple-element.41), channel_id=1, source_target_pairs={{0,16},{2,18},{4,20},{6,22},{8,24},{10,26},{12,28},{14,30},{1,17},... | collective-permute-start | bytes 786440 | tf_op jit(solution)/shard_map/ppermute | solution.py:61
  18.3 4.6 %collective-permute-start.2 = (bf16[128,1024]{1,0:T(8,128)(2,1)}, bf16[128,1024]{1,0:T(8,128)(2,1)S(1)}, u32[]{:S(2)}, u32[]{:S(2)}) collective-permute-start(bf16[128,1024]{1,0:T(8,128)(2,1)} %get-tuple-element.40), channel_id=1, source_target_pairs={{0,1},{2,3},{4,5},{6,7},{8,9},{10,11},{12,13},{14,15},{1,0},{3,2},... | collective-permute-start | bytes 786440 | tf_op jit(solution)/shard_map/ppermute | solution.py:61
  23.0 2.0 collective-permute-start.3
  25.0 0.6 constant_dynamic-slice_fusion
  25.8 0.1 broadcast_bitcast_fusion.2
  25.9 1.9 constant_dynamic-slice_fusion.2
  27.7 0.9 select_reduce_fusion
  28.7 0.1 broadcast_bitcast_fusion.1
  28.7 4.2 %collective-permute-done.2 = bf16[128,1024]{1,0:T(8,128)(2,1)S(1)} collective-permute-done((bf16[128,1024]{1,0:T(8,128)(2,1)}, bf16[128,1024]{1,0:T(8,128)(2,1)S(1)}, u32[]{:S(2)}, u32[]{:S(2)}) %collective-permute-start.2) | collective-permute-done | bytes 262176 | tf_op jit(solution)/shard_map/ppermute | solution.py:61
  32.9 1.0 fusion.13
  33.9 4.7 %collective-permute-start.4 = (bf16[128,1024]{1,0:T(8,128)(2,1)S(1)}, bf16[128,1024]{1,0:T(8,128)(2,1)S(1)}, u32[]{:S(2)}, u32[]{:S(2)}) collective-permute-start(bf16[128,1024]{1,0:T(8,128)(2,1)S(1)} %fusion.13), channel_id=1, source_target_pairs={{0,6},{2,8},{4,10},{6,12},{8,14},{10,0},{12,2},{14,4},{1,7},{3,9},... | collective-permute-start | bytes 786440 | tf_op jit(solution)/shard_map/ppermute | solution.py:24
  38.6 2.2 %collective-permute-start.5 = (bf16[128,1024]{1,0:T(8,128)(2,1)S(1)}, bf16[128,1024]{1,0:T(8,128)(2,1)}, u32[]{:S(2)}, u32[]{:S(2)}) collective-permute-start(bf16[128,1024]{1,0:T(8,128)(2,1)S(1)} %fusion.13), channel_id=1, source_target_pairs={{0,10},{2,12},{4,14},{6,0},{8,2},{10,4},{12,6},{14,8},{1,11},{3,13... | collective-permute-start | bytes 786440 | tf_op jit(solution)/shard_map/ppermute | solution.py:24
  40.8 2.5 %dynamic-slice_bitcast_fusion = (bf16[1024,256]{1,0:T(8,128)(2,1)}, bf16[1024,256]{1,0:T(8,128)(2,1)}, bf16[1024,256]{1,0:T(8,128)(2,1)}) fusion(bf16[4,1024,256]{2,1,0:T(8,128)(2,1)} %get-tuple-element.16, s32[]{:T(128)S(6)} %select_n.205, s32[]{:T(128)S(6)} %select_n.203, s32[]{:T(128)S(6)} %select_n.200), kind=kLoop, calls=%fused_computation.28 | loop fusion | bytes 3145740 | tf_op jit(solution)/shard_map/jit(dynamic_index_in_dim)/squeeze | solution.py:62
  43.3 3.3 %collective-permute-start.10 = (bf16[1024,256]{1,0:T(8,128)(2,1)}, bf16[1024,256]{1,0:T(8,128)(2,1)}, u32[]{:S(2)}, u32[]{:S(2)}) collective-permute-start(bf16[1024,256]{1,0:T(8,128)(2,1)} %get-tuple-element.29), channel_id=1, source_target_pairs={{0,17},{2,19},{4,21},{6,23},{8,25},{10,27},{12,29},{14,31},{1,16},... | collective-permute-start | bytes 1572872 | tf_op jit(solution)/shard_map/ppermute | solution.py:61
  46.6 2.1 collective-permute-start.8
  48.7 2.6 %collective-permute-start.9 = (bf16[1024,256]{1,0:T(8,128)(2,1)}, bf16[1024,256]{1,0:T(8,128)(2,1)}, u32[]{:S(2)}, u32[]{:S(2)}) collective-permute-start(bf16[1024,256]{1,0:T(8,128)(2,1)} %get-tuple-element.30), channel_id=1, source_target_pairs={{0,1},{2,3},{4,5},{6,7},{8,9},{10,11},{12,13},{14,15},{1,0},{3,2},... | collective-permute-start | bytes 1572872 | tf_op jit(solution)/shard_map/ppermute | solution.py:61
  51.3 0.5 copy.31
  51.8 0.5 copy.30
  52.4 6.0 %fusion.37 = (bf16[1024,1024]{1,0:T(8,128)(2,1)}, f32[1024,1024]{1,0:T(8,128)}) fusion(s32[1024,1024]{1,0:T(8,128)} %param.9, f32[8,1024]{1,0:T(8,128)S(1)} %select_reduce_fusion), kind=kLoop, calls=%fused_computation.105 | loop fusion | flops 4194304 | bytes 10518528 | tf_op jit(solution)/shard_map/convert_element_type | solution.py:243
  58.5 1.2 collective-permute-done.5
  59.7 1.0 select_select_fusion.2
  60.7 4.8 %collective-permute-start.6 = (bf16[128,1024]{1,0:T(8,128)(2,1)S(1)}, bf16[128,1024]{1,0:T(8,128)(2,1)S(1)}, u32[]{:S(2)}, u32[]{:S(2)}) collective-permute-start(bf16[128,1024]{1,0:T(8,128)(2,1)S(1)} %select_select_fusion.2), channel_id=1, source_target_pairs={{0,2},{2,4},{4,6},{6,8},{8,10},{10,12},{12,14},{14,0},{1,3},{3,5},... | collective-permute-start | bytes 786440 | tf_op jit(solution)/shard_map/ppermute | solution.py:24
  65.5 5.4 %collective-permute-done.9 = bf16[1024,256]{1,0:T(8,128)(2,1)} collective-permute-done((bf16[1024,256]{1,0:T(8,128)(2,1)}, bf16[1024,256]{1,0:T(8,128)(2,1)}, u32[]{:S(2)}, u32[]{:S(2)}) %collective-permute-start.9) | collective-permute-done | bytes 524320 | tf_op jit(solution)/shard_map/ppermute | solution.py:61
  70.9 2.2 fusion.6
  73.1 2.5 %collective-permute-start.14 = (bf16[1024,256]{1,0:T(8,128)(2,1)}, bf16[1024,256]{1,0:T(8,128)(2,1)}, u32[]{:S(2)}, u32[]{:S(2)}) collective-permute-start(bf16[1024,256]{1,0:T(8,128)(2,1)} %fusion.6), channel_id=1, source_target_pairs={{0,6},{2,8},{4,10},{6,12},{8,14},{10,0},{12,2},{14,4},{1,7},{3,9},... | collective-permute-start | bytes 1572872 | tf_op jit(solution)/shard_map/ppermute | solution.py:24
  75.6 2.6 %collective-permute-start.15 = (bf16[1024,256]{1,0:T(8,128)(2,1)}, bf16[1024,256]{1,0:T(8,128)(2,1)}, u32[]{:S(2)}, u32[]{:S(2)}) collective-permute-start(bf16[1024,256]{1,0:T(8,128)(2,1)} %fusion.6), channel_id=1, source_target_pairs={{0,10},{2,12},{4,14},{6,0},{8,2},{10,4},{12,6},{14,8},{1,11},{3,13... | collective-permute-start | bytes 1572872 | tf_op jit(solution)/shard_map/ppermute | solution.py:24
  78.3 19.7 %all-gather.10 = f16[1024,1024]{1,0:T(8,128)(2,1)} all-gather(f16[128,1024]{1,0:T(8,128)(2,1)S(1)} %convert_element_type.106), channel_id=1, replica_groups=mesh['y'=4,'core'=2,'xl'=2,'z'=8,'xh'=2] {'xh','xl','core'}, dimensions={0}, use_global_device_ids=true | all-gather | bytes 2359296 | tf_op jit(solution)/shard_map/all_gather | solution.py:216
  98.0 0.1 broadcast_select_fusion.1
  98.1 0.2 stack_reshape.6
  98.3 0.2 stack_reshape.7
  98.5 1.2 pad_maximum_fusion
  99.7 2.6 %copy.25 = bf16[4,2,128,832]{2,1,0,3:T(2,128)(2,1)S(1)} copy(bf16[4,2,128,832]{2,0,3,1:T(4,128)(2,1)S(1)} %pad_maximum_fusion) | data formatting | bytes 3407872 | tf_op jit(solution)/shard_map/stack | solution.py:205
  102.3 1.2 reshape.290
  103.6 3.6 %abs_reduce_fusion = (f32[4,208]{1,0:T(4,128)S(1)}, f32[4,208,1024]{2,1,0:T(8,128)S(1)}) fusion(bf16[4,208,1024]{2,1,0:T(8,128)(2,1)S(1)} %bitcast.85, f16[1024,1024]{1,0:T(8,128)(2,1)} %all-gather.10), kind=kOutput, calls=%fused_computation.4 | convolution fusion | flops 1747582208 | bytes 7212288 | tf_op jit(solution)/shard_map/dot_general | solution.py:220
  107.3 0.3 convert_convert_fusion
  107.6 1.3 copy-done.9
  109.0 1.1 fusion.10
  110.1 0.3 collective-permute-start.11
  110.4 0.6 copy-done.6
  111.0 0.8 copy-done.7
  111.8 2.1 fusion.base_ref
  113.9 0.9 collective-permute-start.12
  114.7 1.1 collective-permute-start.13
  115.8 1.1 collective-permute-done.14
  116.9 1.8 collective-permute-done.15
  118.7 1.7 select_select_fusion
  120.4 6.7 %collective-permute-start.16 = (bf16[1024,256]{1,0:T(8,128)(2,1)S(1)}, bf16[1024,256]{1,0:T(8,128)(2,1)S(1)}, u32[]{:S(2)}, u32[]{:S(2)}) collective-permute-start(bf16[1024,256]{1,0:T(8,128)(2,1)S(1)} %select_select_fusion), channel_id=1, source_target_pairs={{0,2},{2,4},{4,6},{6,8},{8,10},{10,12},{12,14},{14,0},{1,3},{3,5},... | collective-permute-start | bytes 1572872 | tf_op jit(solution)/shard_map/ppermute | solution.py:24
  127.1 0.7 fusion.31
  127.8 10.2 %collective-permute-done.12 = s16[224,1024]{1,0:T(8,128)(2,1)S(1)} collective-permute-done((s16[224,1024]{1,0:T(8,128)(2,1)}, s16[224,1024]{1,0:T(8,128)(2,1)S(1)}, u32[]{:S(2)}, u32[]{:S(2)}) %collective-permute-start.12) | collective-permute-done | bytes 458784 | tf_op jit(solution)/shard_map/ppermute | solution.py:24
  138.0 2.0 abs_reduce_fusion.1
  140.0 0.1 convert_convert_fusion.1
  140.2 19.7 %all-gather.11 = s16[1792,1024]{1,0:T(8,128)(2,1)S(1)} all-gather(s16[224,1024]{1,0:T(8,128)(2,1)S(1)} %pad_add_fusion), channel_id=2, replica_groups=mesh['y'=4,'core'=2,'xl'=2,'z'=8,'xh'=2] {'y','core'}, dimensions={0}, use_global_device_ids=true | all-gather | bytes 4128768 | tf_op jit(solution)/shard_map/all_gather | solution.py:230
  160.0 1.8 copy-done.2
  161.8 1.3 mul.192.scale_ref
  163.0 0.3 select_convert_fusion
  163.4 21.7 %all-gather.9 = f16[4096,256]{1,0:T(8,128)(2,1)S(1)} all-gather(f16[1024,256]{1,0:T(8,128)(2,1)S(1)} %select_convert_fusion), channel_id=4, replica_groups=mesh['y'=4,'core'=2,'xl'=2,'z'=8,'xh'=2] {'xh','xl'}, dimensions={0}, use_global_device_ids=true | all-gather | bytes 2621440 | tf_op jit(solution)/shard_map/all_gather | solution.py:238
  185.1 0.5 convert_element_type.133
  185.6 1.6 copy.32
  187.2 2.9 %copy.27 = f32[2,2,8,2,16,1024]{5,4,3,0,2,1:T(8,128)S(1)} copy(f32[2,2,8,2,16,1024]{5,4,3,2,1,0:T(8,128)} %bitcast.84) | data formatting | bytes 8388608 | tf_op jit(solution)/shard_map/reshape | solution.py:193
  190.1 9.5 %block_error.1 = (bf16[1024,1024]{1,0:T(8,128)(2,1)S(1)}, bf16[1024,1024]{1,0:T(8,128)(2,1)S(1)}) custom-call(f32[1024,1024]{1,0:T(8,128)S(1)} %bitcast.79, bf16[1024,1024]{1,0:T(8,128)(2,1)S(1)} %bitcast.82, f32[1024,1024]{1,0:T(8,128)} %get-tuple-element.22.q_ref), custom_call_target="tpu_custom_call" | custom-call | flops 6442450944 | bytes 14680064 | tf_op jit(solution)/shard_map/block_error/pallas_call | solution.py:121
  199.7 13.3 %apply_update.1 = bf16[1664,1024]{1,0:T(8,128)(2,1)} custom-call(s32[1]{0:T(128)} %bitcast.1.start_ref, s16[4,2,224,1024]{3,2,1,0:T(8,128)(2,1)S(1)} %bitcast.81, f32[4,2,208,1]{3,2,1,0:T(8,128)S(1)} %copy-done.5, bf16[1024,1024]{1,0:T(8,128)(2,1)S(1)} %get-tuple-element.19.high_ref, bf16[1024,1024]{1,0:T(8,128)(2,1)S(1)} %get-tuple-element.20.low_ref, ...), custom_call_target="tpu_custom_call" | custom-call | flops 10468982784 | bytes 14417920 | tf_op jit(solution)/shard_map/apply_update/pallas_call | solution.py:150
  (54 shorter events, 0.6 us)
Async XLA Ops:
  6.5 18.5 %copy-start = (f32[32,1024]{1,0:T(8,128)S(1)}, f32[32,1024]{1,0:T(8,128)}, u32[]{:S(2)}) copy-start(f32[32,1024]{1,0:T(8,128)} %param.12) | copy-start | bytes 393220
  6.5 180.6 %all-gather.8.cloned.1.call-start = ((), (), s32[]{:S(2)}) async-start(), calls=%async_computation | async-start | bytes 4259840 | tf_op jit(solution)/shard_map/all_gather | solution.py:192
  12.7 13.1 %copy-start.8 = (bf16[512,1664]{1,0:T(8,128)(2,1)S(1)}, bf16[512,1664]{1,0:T(8,128)(2,1)}, u32[]{:S(2)}) copy-start(bf16[512,1664]{1,0:T(8,128)(2,1)} %x_ref.1) | copy-start | bytes 5111812
  14.8 12.9 %copy-start.11 = (f32[16]{0:T(128)S(1)}, f32[16]{0:T(128)}, u32[]{:S(2)}) copy-start(f32[16]{0:T(128)} %param.11) | copy-start | bytes 196
  14.8 13.9 %collective-permute-start.1 = (bf16[128,1024]{1,0:T(8,128)(2,1)}, bf16[128,1024]{1,0:T(8,128)(2,1)S(1)}, u32[]{:S(2)}, u32[]{:S(2)}) collective-permute-start(bf16[128,1024]{1,0:T(8,128)(2,1)} %get-tuple-element.41), channel_id=1, source_target_pairs={{0,16},{2,18},{4,20},{6,22},{8,24},{10,26},{12,28},{14,30},{1,17},... | collective-permute-start | bytes 786440 | tf_op jit(solution)/shard_map/ppermute | solution.py:61
  18.3 14.5 %collective-permute-start.2 = (bf16[128,1024]{1,0:T(8,128)(2,1)}, bf16[128,1024]{1,0:T(8,128)(2,1)S(1)}, u32[]{:S(2)}, u32[]{:S(2)}) collective-permute-start(bf16[128,1024]{1,0:T(8,128)(2,1)} %get-tuple-element.40), channel_id=1, source_target_pairs={{0,1},{2,3},{4,5},{6,7},{8,9},{10,11},{12,13},{14,15},{1,0},{3,2},... | collective-permute-start | bytes 786440 | tf_op jit(solution)/shard_map/ppermute | solution.py:61
  23.0 9.9 %collective-permute-start.3 = (bf16[128,1024]{1,0:T(8,128)(2,1)S(1)}, bf16[128,1024]{1,0:T(8,128)(2,1)}, u32[]{:S(2)}, u32[]{:S(2)}) collective-permute-start(bf16[128,1024]{1,0:T(8,128)(2,1)S(1)} %get-tuple-element.39), channel_id=1, source_target_pairs={{0,17},{2,19},{4,21},{6,23},{8,25},{10,27},{12,29},{14,31},{1,16},... | collective-permute-start | bytes 786440 | tf_op jit(solution)/shard_map/ppermute | solution.py:61
  28.7 22.6 %copy-start.10 = (bf16[512,832]{1,0:T(8,128)(2,1)S(1)}, bf16[512,832]{1,0:T(8,128)(2,1)}, u32[]{:S(2)}) copy-start(bf16[512,832]{1,0:T(8,128)(2,1)} %get-tuple-element.38) | copy-start | bytes 2555908
  33.9 24.5 %collective-permute-start.4 = (bf16[128,1024]{1,0:T(8,128)(2,1)S(1)}, bf16[128,1024]{1,0:T(8,128)(2,1)S(1)}, u32[]{:S(2)}, u32[]{:S(2)}) collective-permute-start(bf16[128,1024]{1,0:T(8,128)(2,1)S(1)} %fusion.13), channel_id=1, source_target_pairs={{0,6},{2,8},{4,10},{6,12},{8,14},{10,0},{12,2},{14,4},{1,7},{3,9},... | collective-permute-start | bytes 786440 | tf_op jit(solution)/shard_map/ppermute | solution.py:24
  38.6 21.1 %collective-permute-start.5 = (bf16[128,1024]{1,0:T(8,128)(2,1)S(1)}, bf16[128,1024]{1,0:T(8,128)(2,1)}, u32[]{:S(2)}, u32[]{:S(2)}) collective-permute-start(bf16[128,1024]{1,0:T(8,128)(2,1)S(1)} %fusion.13), channel_id=1, source_target_pairs={{0,10},{2,12},{4,14},{6,0},{8,2},{10,4},{12,6},{14,8},{1,11},{3,13... | collective-permute-start | bytes 786440 | tf_op jit(solution)/shard_map/ppermute | solution.py:24
  43.3 22.2 %collective-permute-start.10 = (bf16[1024,256]{1,0:T(8,128)(2,1)}, bf16[1024,256]{1,0:T(8,128)(2,1)}, u32[]{:S(2)}, u32[]{:S(2)}) collective-permute-start(bf16[1024,256]{1,0:T(8,128)(2,1)} %get-tuple-element.29), channel_id=1, source_target_pairs={{0,17},{2,19},{4,21},{6,23},{8,25},{10,27},{12,29},{14,31},{1,16},... | collective-permute-start | bytes 1572872 | tf_op jit(solution)/shard_map/ppermute | solution.py:61
  46.6 18.9 %collective-permute-start.8 = (bf16[1024,256]{1,0:T(8,128)(2,1)}, bf16[1024,256]{1,0:T(8,128)(2,1)}, u32[]{:S(2)}, u32[]{:S(2)}) collective-permute-start(bf16[1024,256]{1,0:T(8,128)(2,1)} %get-tuple-element.31), channel_id=1, source_target_pairs={{0,16},{2,18},{4,20},{6,22},{8,24},{10,26},{12,28},{14,30},{1,17},... | collective-permute-start | bytes 1572872 | tf_op jit(solution)/shard_map/ppermute | solution.py:61
  48.7 22.2 %collective-permute-start.9 = (bf16[1024,256]{1,0:T(8,128)(2,1)}, bf16[1024,256]{1,0:T(8,128)(2,1)}, u32[]{:S(2)}, u32[]{:S(2)}) collective-permute-start(bf16[1024,256]{1,0:T(8,128)(2,1)} %get-tuple-element.30), channel_id=1, source_target_pairs={{0,1},{2,3},{4,5},{6,7},{8,9},{10,11},{12,13},{14,15},{1,0},{3,2},... | collective-permute-start | bytes 1572872 | tf_op jit(solution)/shard_map/ppermute | solution.py:61
  58.4 39.5 %collective-permute-start = (bf16[512,832]{0,1:T(8,128)(2,1)S(1)}, bf16[512,832]{0,1:T(8,128)(2,1)S(1)}, u32[]{:S(2)}, u32[]{:S(2)}) collective-permute-start(bf16[512,832]{0,1:T(8,128)(2,1)S(1)} %copy.31), channel_id=1, source_target_pairs={{0,32},{32,0},{1,33},{33,1},{2,34},{34,2},{3,35},{35,3},{4,36},{36... | collective-permute-start | bytes 2555912 | tf_op jit(solution)/shard_map/ppermute | solution.py:24
  60.7 12.4 %collective-permute-start.6 = (bf16[128,1024]{1,0:T(8,128)(2,1)S(1)}, bf16[128,1024]{1,0:T(8,128)(2,1)S(1)}, u32[]{:S(2)}, u32[]{:S(2)}) collective-permute-start(bf16[128,1024]{1,0:T(8,128)(2,1)S(1)} %select_select_fusion.2), channel_id=1, source_target_pairs={{0,2},{2,4},{4,6},{6,8},{8,10},{10,12},{12,14},{14,0},{1,3},{3,5},... | collective-permute-start | bytes 786440 | tf_op jit(solution)/shard_map/ppermute | solution.py:24
  65.5 7.6 %collective-permute-start.7 = (bf16[128,1024]{1,0:T(8,128)(2,1)S(1)}, bf16[128,1024]{1,0:T(8,128)(2,1)S(1)}, u32[]{:S(2)}, u32[]{:S(2)}) collective-permute-start(bf16[128,1024]{1,0:T(8,128)(2,1)S(1)} %select_select_fusion.2), channel_id=1, source_target_pairs={{0,14},{2,0},{4,2},{6,4},{8,6},{10,8},{12,10},{14,12},{1,15},{3,1}... | collective-permute-start | bytes 786440 | tf_op jit(solution)/shard_map/ppermute | solution.py:24
  73.1 43.8 %collective-permute-start.14 = (bf16[1024,256]{1,0:T(8,128)(2,1)}, bf16[1024,256]{1,0:T(8,128)(2,1)}, u32[]{:S(2)}, u32[]{:S(2)}) collective-permute-start(bf16[1024,256]{1,0:T(8,128)(2,1)} %fusion.6), channel_id=1, source_target_pairs={{0,6},{2,8},{4,10},{6,12},{8,14},{10,0},{12,2},{14,4},{1,7},{3,9},... | collective-permute-start | bytes 1572872 | tf_op jit(solution)/shard_map/ppermute | solution.py:24
  75.6 43.1 %collective-permute-start.15 = (bf16[1024,256]{1,0:T(8,128)(2,1)}, bf16[1024,256]{1,0:T(8,128)(2,1)}, u32[]{:S(2)}, u32[]{:S(2)}) collective-permute-start(bf16[1024,256]{1,0:T(8,128)(2,1)} %fusion.6), channel_id=1, source_target_pairs={{0,10},{2,12},{4,14},{6,0},{8,2},{10,4},{12,6},{14,8},{1,11},{3,13... | collective-permute-start | bytes 1572872 | tf_op jit(solution)/shard_map/ppermute | solution.py:24
  107.2 1.8 copy-start.9
  107.3 3.7 %copy-start.6 = (bf16[1664,1024]{1,0:T(8,128)(2,1)S(1)}, bf16[1664,1024]{1,0:T(8,128)(2,1)}, u32[]{:S(2)}) copy-start(bf16[1664,1024]{1,0:T(8,128)(2,1)} %w_ref.1) | copy-start | bytes 10223620
  109.0 2.8 %copy-start.7 = (bf16[1024,1024]{1,0:T(8,128)(2,1)S(1)}, bf16[1024,1024]{1,0:T(8,128)(2,1)}, u32[]{:S(2)}) copy-start(bf16[1024,1024]{1,0:T(8,128)(2,1)} %get-tuple-element.21) | copy-start | bytes 6291460
  110.1 17.0 %collective-permute-start.11 = (s16[224,1024]{1,0:T(8,128)(2,1)}, s16[224,1024]{1,0:T(8,128)(2,1)}, u32[]{:S(2)}, u32[]{:S(2)}) collective-permute-start(s16[224,1024]{1,0:T(8,128)(2,1)} %get-tuple-element.32), channel_id=1, source_target_pairs={{0,64},{64,128},{128,192},{192,0},{1,65},{65,129},{129,193},{193,1... | collective-permute-start | bytes 1376264 | tf_op jit(solution)/shard_map/ppermute | solution.py:24
  113.9 24.1 %collective-permute-start.12 = (s16[224,1024]{1,0:T(8,128)(2,1)}, s16[224,1024]{1,0:T(8,128)(2,1)S(1)}, u32[]{:S(2)}, u32[]{:S(2)}) collective-permute-start(s16[224,1024]{1,0:T(8,128)(2,1)} %get-tuple-element.33), channel_id=1, source_target_pairs={{0,192},{64,0},{128,64},{192,128},{1,193},{65,1},{129,65},{193,129... | collective-permute-start | bytes 1376264 | tf_op jit(solution)/shard_map/ppermute | solution.py:24
  114.7 23.3 %collective-permute-start.13 = (s16[224,1024]{1,0:T(8,128)(2,1)}, s16[224,1024]{1,0:T(8,128)(2,1)S(1)}, u32[]{:S(2)}, u32[]{:S(2)}) collective-permute-start(s16[224,1024]{1,0:T(8,128)(2,1)} %get-tuple-element.34), channel_id=1, source_target_pairs={{0,128},{64,192},{128,0},{192,64},{1,129},{65,193},{129,1},{193,65... | collective-permute-start | bytes 1376264 | tf_op jit(solution)/shard_map/ppermute | solution.py:24
  120.4 42.7 %collective-permute-start.16 = (bf16[1024,256]{1,0:T(8,128)(2,1)S(1)}, bf16[1024,256]{1,0:T(8,128)(2,1)S(1)}, u32[]{:S(2)}, u32[]{:S(2)}) collective-permute-start(bf16[1024,256]{1,0:T(8,128)(2,1)S(1)} %select_select_fusion), channel_id=1, source_target_pairs={{0,2},{2,4},{4,6},{6,8},{8,10},{10,12},{12,14},{14,0},{1,3},{3,5},... | collective-permute-start | bytes 1572872 | tf_op jit(solution)/shard_map/ppermute | solution.py:24
  127.1 35.9 %collective-permute-start.17 = (bf16[1024,256]{1,0:T(8,128)(2,1)S(1)}, bf16[1024,256]{1,0:T(8,128)(2,1)S(1)}, u32[]{:S(2)}, u32[]{:S(2)}) collective-permute-start(bf16[1024,256]{1,0:T(8,128)(2,1)S(1)} %select_select_fusion), channel_id=1, source_target_pairs={{0,14},{2,0},{4,2},{6,4},{8,6},{10,8},{12,10},{14,12},{1,15},{3,1}... | collective-permute-start | bytes 1572872 | tf_op jit(solution)/shard_map/ppermute | solution.py:24
  160.0 1.8 copy-start.2
  187.2 2.9 %copy-start.4 = (bf16[4,128,8,256]{3,2,0,1:T(8,128)(2,1)S(1)}, bf16[4,128,8,256]{3,2,0,1:T(8,128)(2,1)}, u32[]{:S(2)}) copy-start(bf16[4,128,8,256]{3,2,0,1:T(8,128)(2,1)} %copy.32) | copy-start | bytes 6291460
  190.1 9.5 %copy-start.3 = (s16[1792,1024]{1,0:T(8,128)(2,1)S(1)}, s16[1792,1024]{1,0:T(8,128)(2,1)}, u32[]{:S(2)}) copy-start(s16[1792,1024]{1,0:T(8,128)(2,1)} %copy-done.2) | copy-start | bytes 11010052
  190.1 9.5 %copy-start.5 = (f32[4,2,208,1]{3,2,1,0:T(8,128)S(1)}, f32[4,2,208,1]{3,2,1,0:T(8,128)}, u32[]{:S(2)}) copy-start(f32[4,2,208,1]{3,2,1,0:T(8,128)} %mul.192.scale_ref) | copy-start | bytes 19972
  199.6 13.3 %copy-start.1 = (f32[32,1024]{1,0:T(8,128)S(1)}, f32[32,1024]{1,0:T(8,128)}, u32[]{:S(2)}) copy-start(f32[32,1024]{1,0:T(8,128)} %param.12) | copy-start | bytes 393220
Sparse Core Ops, SparseCore 0:
  25.8 97.5 all-gather.7

commit v2 on v1

v2 whole, which is shorter than its diff:
```python
import functools
import jax
import jax.numpy as jnp
from jax import lax
from jax.experimental import pallas as pl
from jax.experimental.pallas import tpu as pltpu
from jax.sharding import Mesh, PartitionSpec as P

BLK = 1024
GROUP = 128
LEVELS = 16
UNIT = 128
UNITS = BLK // UNIT
STEPS_PER_OCTAVE = 128.0
F32, BF16, S16 = jnp.float32, jnp.bfloat16, jnp.int16
PLANE = ("xl", "z", "xh")


def tile_at(x, z):
    return (x % 2) * 16 + (z % 8) * 2 + (x % 4) // 2


def ring(axis, size, shift, value):
    return lax.ppermute(value, axis, [(i, (i + shift) % size) for i in range(size)])


def pick_kernel(rows, cols, scalars, src_ref, *out_refs):
    x = scalars[UNITS]
    for k, out_ref in enumerate(out_refs):
        p = (x + k) % 4
        if rows is not None:
            out_ref[...] = src_ref[pl.ds(pl.multiple_of(p * rows, rows), rows), :]
        else:
            out_ref[...] = src_ref[:, pl.ds(pl.multiple_of(p * cols, cols), cols)]


def pick(source, along, scalars, name):
    other = source.shape[1 - along]
    part = other // 4
    if along == 1:
        in_spec = pl.BlockSpec((other, UNIT), lambda j, u: (0, u[j]))
        out_spec = pl.BlockSpec((part, UNIT), lambda j, u: (0, j))
        shape, rows, cols = (part, BLK), part, None
    else:
        in_spec = pl.BlockSpec((UNIT, other), lambda j, u: (u[j], 0))
        out_spec = pl.BlockSpec((UNIT, part), lambda j, u: (j, 0))
        shape, rows, cols = (BLK, part), None, part
    return pl.pallas_call(
        functools.partial(pick_kernel, rows, cols),
        grid_spec=pltpu.PrefetchScalarGridSpec(
            num_scalar_prefetch=1, grid=(UNITS,), in_specs=[in_spec], out_specs=[out_spec] * 4
        ),
        out_shape=[jax.ShapeDtypeStruct(shape, BF16)] * 4,
        name=name,
    )(scalars, source)


def plane_pairs(columns, shift):
    return [(tile_at(s, z), tile_at(s + shift, z)) for s in columns for z in range(8)]


def scatter_x(pieces, x, from_low):
    own, *others = pieces
    up, across, down = (
        lax.ppermute(piece, PLANE, plane_pairs((0, 2), shift))
        for shift, piece in zip((1, 2, 3), others)
    )
    even = x % 2 == 0
    near = jnp.where(even, own, up)
    far = jnp.where(even, across, down)
    return jnp.where(from_low, near, far)


def spread_z(piece, distance, beside=None):
    up, down = ring("z", 8, 3, piece), ring("z", 8, -3, piece)
    if beside is not None:
        up, down, beside = lax.optimization_barrier((up, down, beside))
    piece = jnp.where(distance == 3, up, jnp.where(distance == 5, down, piece))
    up, down = ring("z", 8, 1, piece), ring("z", 8, -1, piece)
    from_below = (distance == 1) | (distance == 4) | (distance == 6)
    from_above = (distance == 7) | (distance == 2)
    return jnp.where(from_below, up, jnp.where(from_above, down, piece)), beside


def quantize(values):
    rows = values.shape[-2]
    top = jnp.max(jnp.abs(values), axis=-1, keepdims=True)
    level = jnp.floor(jnp.log2(32700.0 / jnp.maximum(top, 1e-25)) * STEPS_PER_OCTAVE)
    scaled = jnp.round(values * jnp.exp2(level / STEPS_PER_OCTAVE)).astype(jnp.int32).astype(S16)
    levels = jnp.swapaxes(level, -1, -2).astype(jnp.int32).astype(S16)
    widths = [(0, 0)] * (values.ndim - 2) + [(0, 15), (0, values.shape[-1] - rows)]
    return jnp.concatenate([scaled, jnp.pad(levels, widths)], axis=-2)


def scales_of(message):
    rows = message.shape[-2] - 16
    level = message[..., rows : rows + 1, :rows].astype(F32)
    return jnp.swapaxes(jnp.exp2(-level / STEPS_PER_OCTAVE), -1, -2)


def dequantize(message):
    return message[..., :-16, :].astype(F32) * scales_of(message)


def split(values):
    high = values.astype(BF16)
    return high, (values - high.astype(F32)).astype(BF16)


def mm(a, b):
    return jnp.dot(a, b, preferred_element_type=F32)


def error_kernel(inv_ref, w_ref, q_ref, out_ref):
    inv_high, inv_low = split(inv_ref[...])
    dev_high, dev_low = split(w_ref[...].astype(F32) - q_ref[...])
    error = mm(inv_high, dev_high) + (mm(inv_high, dev_low) + mm(inv_low, dev_high))
    i = pl.program_id(0)
    first = ((i % 2) * 16 + i // 2) * 32
    for z in range(8):
        at = pl.multiple_of(first + z * 64, 32)
        out_ref[pl.ds(at, 32), :] = error[z * 32 : (z + 1) * 32]


def block_error(inverse, w_piece, quantized):
    wide = w_piece.shape[1]
    whole = pl.BlockSpec((BLK, wide), lambda i: (0, 0))
    return pl.pallas_call(
        error_kernel,
        grid=(4,),
        in_specs=[pl.BlockSpec((BLK // 4, BLK), lambda i: (i, 0)), whole, whole],
        out_specs=whole,
        out_shape=jax.ShapeDtypeStruct((BLK, wide), F32),
        compiler_params=pltpu.CompilerParams(vmem_limit_bytes=32 << 20),
        cost_estimate=pl.CostEstimate(
            flops=6 * BLK * BLK * wide, bytes_accessed=BLK * BLK * 4, transcendentals=0
        ),
        name="block_error",
    )(inverse, w_piece, quantized)


def quantize_columns(error):
    top = jnp.max(jnp.abs(error), axis=0, keepdims=True)
    level = jnp.floor(jnp.log2(32700.0 / jnp.maximum(top, 1e-25)) * STEPS_PER_OCTAVE)
    scaled = jnp.round(error * jnp.exp2(level / STEPS_PER_OCTAVE))
    levels = jnp.broadcast_to(level, (16, error.shape[1]))
    return jnp.concatenate([scaled, levels], axis=0).astype(jnp.int32).astype(S16)


def update_kernel(scalars, h_ref, scale_ref, e0, e1, e2, e3, base_ref, out_ref, high_ref, low_ref, factor_ref):
    rows, wide = out_ref.shape[0], e0.shape[1]

    @pl.when(pl.program_id(0) == 0)
    def _():
        for k, e in enumerate((e0, e1, e2, e3)):
            high_ref[k], low_ref[k] = split(e[:BLK].astype(jnp.int32).astype(F32))
            level = e[BLK : BLK + 16].astype(jnp.int32).astype(F32)
            factor_ref[k] = jnp.exp2(level * (-1.0 / STEPS_PER_OCTAVE))

    h_high, h_low = split(h_ref[0, 0, :rows].astype(jnp.int32).astype(F32))
    row = lax.broadcasted_iota(jnp.int32, (rows, wide), 0) + pl.program_id(0) * rows
    for k in range(4):
        cols = pl.ds(pl.multiple_of(((scalars[1] + 4 - k) % 4) * wide, wide), wide)
        update = mm(h_high, high_ref[k]) + (mm(h_high, low_ref[k]) + mm(h_low, high_ref[k]))
        update = update * scale_ref[0, 0] * factor_ref[k, 0:1]
        base = base_ref[:, cols].astype(F32)
        out_ref[:, cols] = jnp.where(row >= scalars[0], base - update, base).astype(BF16)


def apply_update(scalars, panel, scales, errors, base):
    rows, cols = panel.shape[2] - 16, base.shape[1]
    wide = cols // 4
    whole = pl.BlockSpec((BLK + 16, wide), lambda i, s: (0, 0))
    stripe = pl.BlockSpec((rows, cols), lambda i, s: (i, 0))
    return pl.pallas_call(
        update_kernel,
        grid_spec=pltpu.PrefetchScalarGridSpec(
            num_scalar_prefetch=1,
            grid=(base.shape[0] // rows,),
            in_specs=[
                pl.BlockSpec((1, 1, rows + 16, BLK), lambda i, s: (i % 4, i // 4, 0, 0)),
                pl.BlockSpec((1, 1, rows, 1), lambda i, s: (i % 4, i // 4, 0, 0)),
                whole,
                whole,
                whole,
                whole,
                stripe,
            ],
            out_specs=stripe,
            scratch_shapes=[
                pltpu.VMEM((4, BLK, wide), BF16),
                pltpu.VMEM((4, BLK, wide), BF16),
                pltpu.VMEM((4, 16, wide), F32),
            ],
        ),
        out_shape=jax.ShapeDtypeStruct(base.shape, BF16),
        compiler_params=pltpu.CompilerParams(vmem_limit_bytes=32 << 20),
        cost_estimate=pl.CostEstimate(
            flops=6 * base.shape[0] * BLK * cols,
            bytes_accessed=base.shape[0] * cols * 6 + BLK * cols * 2,
            transcendentals=0,
        ),
        name="apply_update",
    )(scalars, panel, scales, *errors, base)


def local(activations, weights, codes, scale_index, scale_table, inverse_block, block_index):
    y, core = lax.axis_index("y"), lax.axis_index("core")
    xl, z, xh = (lax.axis_index(a) for a in PLANE)
    x = 2 * xh + xl
    tile = lax.axis_index(PLANE)
    shard_rows = weights.shape[0]
    tile_units = shard_rows // UNIT
    token_total = activations.shape[0] * 8
    first_unit = block_index[0] * UNITS
    units = first_unit + jnp.arange(UNITS, dtype=jnp.int32)
    owner = units // tile_units
    x_owner, z_owner = 2 * (owner % 2), (owner // 2) % 8
    distance = (z - z_owner) % 8
    from_low = x_owner == jnp.where(x % 2 == 0, x, (x + 3) % 4)

    own_rows = inverse_block.shape[0] // 2
    inverse_part = lax.dynamic_slice_in_dim(inverse_block, core * own_rows, own_rows, 0)
    inverse = lax.all_gather(inverse_part, ("xh", "xl", "z", "core"), axis=0)
    inverse = inverse.reshape(BLK, BLK)

    index = jnp.clip(units - tile * tile_units, 0, tile_units - 1)
    picks = jnp.append(index, x)
    x_pieces = pick(activations, 1, picks, "pick_columns")
    w_pieces = pick(weights, 0, picks, "pick_rows")

    half = shard_rows // 2
    x_mine = lax.dynamic_slice_in_dim(activations, core * half, half, 1)
    x_theirs = lax.dynamic_slice_in_dim(activations, (1 - core) * half, half, 1)
    x_other = ring("core", 2, 1, x_theirs)
    x_low = jnp.where(core == 0, x_mine, x_other).reshape(4, 128, half)
    x_high = jnp.where(core == 0, x_other, x_mine).reshape(4, 128, half)
    x_rows = jnp.stack([x_low, x_high], axis=1).reshape(1024, half).T

    lanes = lambda v: jnp.repeat(v, UNIT)[None, :]
    sublanes = lambda v: jnp.repeat(v, UNIT)[:, None]
    x_piece = scatter_x(x_pieces, x, lanes(from_low))
    x_piece, w_pieces = lax.optimization_barrier((x_piece, w_pieces))
    w_piece = scatter_x(w_pieces, x, sublanes(from_low))
    x_piece, x_rows = spread_z(x_piece, lanes(distance), x_rows)
    x_piece, w_piece = lax.optimization_barrier((x_piece, w_piece))
    w_piece, _ = spread_z(w_piece, sublanes(distance))

    x_block = lax.all_gather(
        x_piece.astype(jnp.float16), ("xh", "xl", "core"), axis=0, tiled=True
    ).astype(BF16)

    partial_panel = lax.dot_general(
        x_rows, x_block, (((1,), (0,)), ((), ())), preferred_element_type=F32
    )
    quarter = half // 4
    parts = partial_panel.reshape(4, quarter, BLK)
    message = quantize(parts)
    total = lax.dynamic_index_in_dim(parts, y, 0, False)
    for shift in (1, 3, 2):
        sent = lax.dynamic_index_in_dim(message, (y + shift) % 4, 0, False)
        total = total + dequantize(ring("y", 4, shift, sent))
    panel = lax.all_gather(quantize(total), ("y", "core"), axis=0)
    panel = panel.reshape(4, 2, quarter + 16, BLK)
    scales = scales_of(panel) * (2.0 / token_total)

    chosen = (scale_index[:, :, None] == jnp.arange(LEVELS, dtype=jnp.int32)).astype(F32)
    group_scale = jnp.sum(chosen * scale_table, axis=2)
    quantized = jnp.repeat(group_scale, GROUP, axis=0) * (codes.astype(F32) - 7.5)

    wide = w_piece.shape[1]
    own_columns = lax.dynamic_slice_in_dim(quantized, x * wide, wide, 1)
    error = quantize_columns(block_error(inverse, w_piece, own_columns))
    errors = [error]
    for shift in (1, 2, 3):
        errors.append(lax.ppermute(error, PLANE, plane_pairs(range(4), shift)))

    first_local = block_index[0] * BLK - tile * shard_rows
    padded = jnp.pad(quantized.astype(BF16), [(shard_rows, shard_rows), (0, 0)])
    begin = jnp.clip(shard_rows - first_local, 0, BLK + shard_rows)
    quant_rows = lax.dynamic_slice_in_dim(padded, begin, shard_rows, 0)
    row = jnp.arange(shard_rows, dtype=jnp.int32)[:, None] - first_local
    base = jnp.where((row >= 0) & (row < BLK), quant_rows, weights)
    scalars = jnp.stack([first_local + BLK, x])
    return apply_update(scalars, panel, scales, errors, base)


def solution(mesh):
    cube = Mesh(mesh.devices.reshape(4, 2, 2, 8, 2), ("y", "core") + PLANE)
    return jax.shard_map(
        local,
        mesh=cube,
        in_specs=(
            P(("y", "core"), PLANE),
            P(PLANE, ("y", "core")),
            P(None, ("y", "core")),
            P(None, ("y", "core")),
            P(),
            P(PLANE, None),
            P(),
        ),
        out_specs=P(PLANE, ("y", "core")),
        check_vma=False,
    )
```

time: 223 us -> 236 us (1.058)
  waiting for transfers between devices: 23.8 us -> 52.2 us
  blocking collectives: 61 us -> 37.7 us
  other arithmetic: 22.3 us -> 31.3 us
    ppermute x12, waiting for transfers between devices: 14.3 us -> 51.2 us  [ring(): lax.ppermute(value, axis, [(i, (i + shift) % size) for i in range(size)])]
    all_gather x1 -> x0, blocking collectives: 21.7 us -> none  [local(): w_all = lax.all_gather(w_piece.astype(jnp.float16), ('xh', 'xl'), axis=0)]
    ppermute x6 -> x9, waiting for transfers between devices: 9.52 us -> 0.97 us  [the longest x3 0.95 us: local(): errors.append(lax.ppermute(error, PLANE, plane_pairs(range(4), shift)))]
    another operation x1 -> x2, other arithmetic: 1.2 us -> 6.74 us  [the longest x1 6.66 us: local(): x_rows = jnp.stack([x_low, x_high], axis=1).reshape(1024, half).T]
    another operation x3 -> x2, local copies, waits for them, and re-layouts: 3.02 us -> 7.79 us  [local(): x_rows = jnp.stack([x_low, x_high], axis=1).reshape(1024, half).T]
    squeeze x2 -> x0, local copies, waits for them, and re-layouts: 4.59 us -> none  [to(): lax.dynamic_index_in_dim(pieces, (2 * xh + shift) % 4, 0, False)]
    ppermute x12, starting transfers between devices: 25.8 us -> 22.9 us  [ring(): lax.ppermute(value, axis, [(i, (i + shift) % size) for i in range(size)])]
    pallas_call x2 -> x3, Pallas kernels: 14.4 us -> 11.7 us  [the longest x2 9.08 us: pick(): pl.pallas_call(functools.partial(pick_kernel, rows, cols), grid_spec=pltp...]
  transfers between devices with their start and end apart: 19 -> 22, of which waited for: 6 -> 9; matrix products, arithmetic and copies ran while one was open for 18% -> 23% of each run, Pallas kernels for 0% -> 2%
where the time goes in v2:
time: 236 us; the launch traced here: 234 us
  waiting for transfers between devices  52.2 us (22%)
  starting transfers between devices  43.2 us (18%)
  blocking collectives  37.7 us (16%)
  other arithmetic  31.3 us (13%)
  Pallas kernels  26.8 us (11%)
  local copies, waits for them, and re-layouts  24.2 us (10%)
  between operations  14.6 us (6%)
  matrix products  3.68 us (2%)
    ppermute x12, waiting for transfers between devices, ring(): lax.ppermute(value, axis, [(i, (i + shift) % size) for i in range(size)])  51.2 us
    ppermute x12, starting transfers between devices, ring(): lax.ppermute(value, axis, [(i, (i + shift) % size) for i in range(size)])  22.9 us
    all_gather x1, blocking collectives, local(): panel = lax.all_gather(quantize(total), ('y', 'core'), axis=0)  19.8 us
    all_gather x1, blocking collectives, local(): lax.all_gather(x_piece.astype(jnp.float16), ('xh', 'xl', 'core'), axis=0,...  17.8 us
    ppermute x6, starting transfers between devices, scatter_x(): lax.ppermute(piece, PLANE, plane_pairs((0, 2), shift))  16.2 us
    pallas_call x1, Pallas kernels, apply_update(): pl.pallas_call(update_kernel, grid_spec=pltpu.PrefetchScalarGridSpec(num_...  15.1 us
    pallas_call x2, Pallas kernels, pick(): pl.pallas_call(functools.partial(pick_kernel, rows, cols), grid_spec=pltp...  9.08 us
    another operation x2, local copies, waits for them, and re-layouts, local(): x_rows = jnp.stack([x_low, x_high], axis=1).reshape(1024, half).T  7.79 us
  transfers between devices with their start and end apart: 22, of which 9 were waited for; matrix products, arithmetic and copies ran while one was open for 23% of the time, Pallas kernels for 2%

profile of v2, /device:TPU:24, one launch (start us, length us, event | category | flops | bytes accessed | tf_op | source)
XLA Modules:
  0.0 233.7 jit_solution(14141196488569129705)
XLA Ops:
  7.3 0.7 pad_add_fusion.2.scalars
  8.0 4.4 %pick_columns.1 = (bf16[128,1024]{1,0:T(8,128)(2,1)}, bf16[128,1024]{1,0:T(8,128)(2,1)}, bf16[128,1024]{1,0:T(8,128)(2,1)}, bf16[128,1024]{1,0:T(8,128)(2,1)}) custom-call(s32[9]{0:T(128)} %pad_add_fusion.2.scalars, bf16[512,1664]{1,0:T(8,128)(2,1)} %src_ref.2), custom_call_target="tpu_custom_call" | custom-call | tf_op jit(solution)/shard_map/pick_columns/pallas_call | solution.py:48
  12.4 3.4 %collective-permute-start = (bf16[128,1024]{1,0:T(8,128)(2,1)}, bf16[128,1024]{1,0:T(8,128)(2,1)S(1)}, u32[]{:S(2)}, u32[]{:S(2)}) collective-permute-start(bf16[128,1024]{1,0:T(8,128)(2,1)} %get-tuple-element.24), channel_id=1, source_target_pairs={{0,16},{2,18},{4,20},{6,22},{8,24},{10,26},{12,28},{14,30},{1,17},... | collective-permute-start | bytes 786440 | tf_op jit(solution)/shard_map/ppermute | solution.py:65
  15.8 4.6 %collective-permute-start.1 = (bf16[128,1024]{1,0:T(8,128)(2,1)}, bf16[128,1024]{1,0:T(8,128)(2,1)S(1)}, u32[]{:S(2)}, u32[]{:S(2)}) collective-permute-start(bf16[128,1024]{1,0:T(8,128)(2,1)} %get-tuple-element.25), channel_id=1, source_target_pairs={{0,1},{2,3},{4,5},{6,7},{8,9},{10,11},{12,13},{14,15},{1,0},{3,2},... | collective-permute-start | bytes 786440 | tf_op jit(solution)/shard_map/ppermute | solution.py:65
  20.4 1.3 collective-permute-start.2
  21.8 1.8 constant_dynamic-slice_fusion.3
  23.6 2.2 copy.26
  25.8 0.6 constant_dynamic-slice_fusion.1
  26.6 0.9 select_reduce_fusion
  27.7 4.7 %pick_rows.1 = (bf16[1024,256]{1,0:T(8,128)(2,1)}, bf16[1024,256]{1,0:T(8,128)(2,1)}, bf16[1024,256]{1,0:T(8,128)(2,1)}, bf16[1024,256]{1,0:T(8,128)(2,1)}) custom-call(s32[9]{0:T(128)} %pad_add_fusion.2.scalars, bf16[1664,1024]{1,0:T(8,128)(2,1)} %src_ref.3), custom_call_target="tpu_custom_call" | custom-call | tf_op jit(solution)/shard_map/pick_rows/pallas_call | solution.py:48
  32.4 1.2 copy.25
  33.6 5.3 %fusion.34 = (bf16[1024,1024]{1,0:T(8,128)(2,1)S(1)}, f32[1024,1024]{1,0:T(8,128)}) fusion(s32[1024,1024]{1,0:T(8,128)} %param.9, f32[8,1024]{1,0:T(8,128)S(1)} %select_reduce_fusion), kind=kLoop, calls=%fused_computation.104 | loop fusion | flops 4194304 | bytes 10518528 | tf_op jit(solution)/shard_map/convert_element_type | solution.py:279
  39.0 0.7 copy-done.8
  39.7 0.7 copy-done.9
  40.4 1.0 select_select_fusion.5
  41.5 4.7 %collective-permute-start.3 = (bf16[128,1024]{1,0:T(8,128)(2,1)S(1)}, bf16[128,1024]{1,0:T(8,128)(2,1)}, u32[]{:S(2)}, u32[]{:S(2)}) collective-permute-start(bf16[128,1024]{1,0:T(8,128)(2,1)S(1)} %select_select_fusion.5), channel_id=1, source_target_pairs={{0,6},{2,8},{4,10},{6,12},{8,14},{10,0},{12,2},{14,4},{1,7},{3,9},... | collective-permute-start | bytes 786440 | tf_op jit(solution)/shard_map/ppermute | solution.py:24
  46.2 2.2 collective-permute-start.4
  48.4 2.1 collective-permute-start.10
  50.5 2.1 collective-permute-start.8
  52.5 2.7 %collective-permute-start.9 = (bf16[1024,256]{1,0:T(8,128)(2,1)}, bf16[1024,256]{1,0:T(8,128)(2,1)}, u32[]{:S(2)}, u32[]{:S(2)}) collective-permute-start(bf16[1024,256]{1,0:T(8,128)(2,1)} %get-tuple-element.37), channel_id=1, source_target_pairs={{0,1},{2,3},{4,5},{6,7},{8,9},{10,11},{12,13},{14,15},{1,0},{3,2},... | collective-permute-start | bytes 1572872 | tf_op jit(solution)/shard_map/ppermute | solution.py:65
  55.2 2.4 %broadcast_select_fusion.1 = (bf16[512,832]{0,1:T(8,128)(2,1)}, bf16[512,832]{0,1:T(8,128)(2,1)S(1)}) fusion(bf16[512,832]{0,1:T(8,128)(2,1)} %copy.25, bf16[512,832]{0,1:T(8,128)(2,1)} %collective-permute-done.5, pred[]{:T(512)S(6)} %eq.181), kind=kLoop, calls=%fused_computation.24 | loop fusion | flops 851968 | bytes 3407873 | tf_op jit(solution)/shard_map/jit(_where)/select_n | solution.py:236
  57.7 5.9 %stack_reshape.8 = bf16[4,1,128,832]{2,1,0,3:T(2,128)(2,1)} reshape(bf16[512,832]{0,1:T(8,128)(2,1)} %get-tuple-element.54) | data formatting | bytes 1703936 | tf_op jit(solution)/shard_map/stack;reshape | solution.py:238
  63.6 1.9 stack_reshape.9
  65.5 6.7 %pad_maximum_fusion = bf16[4,2,128,832]{2,1,0,3:T(2,128)(2,1)} fusion(bf16[4,1,128,832]{2,1,0,3:T(2,128)(2,1)} %stack_reshape.9, bf16[4,1,128,832]{2,1,0,3:T(2,128)(2,1)} %stack_reshape.8), kind=kLoop, calls=%fused_computation.10 | loop fusion | flops 3407872 | bytes 3407872 | tf_op jit(solution)/shard_map/stack | solution.py:238
  72.1 5.0 %reshape.317 = bf16[1024,832]{0,1:T(8,128)(2,1)} reshape(bf16[4,2,128,832]{2,1,0,3:T(2,128)(2,1)} %pad_maximum_fusion) | data formatting | bytes 3407872 | tf_op jit(solution)/shard_map/reshape | solution.py:238
  77.2 1.1 select_select_fusion.4
  78.2 2.0 collective-permute-start.6
  80.2 1.5 collective-permute-start.7
  81.7 1.4 select_select_fusion.2
  83.2 5.4 %collective-permute-done.6 = bf16[128,1024]{1,0:T(8,128)(2,1)S(1)} collective-permute-done((bf16[128,1024]{1,0:T(8,128)(2,1)S(1)}, bf16[128,1024]{1,0:T(8,128)(2,1)S(1)}, u32[]{:S(2)}, u32[]{:S(2)}) %collective-permute-start.6) | collective-permute-done | bytes 262176 | tf_op jit(solution)/shard_map/ppermute | solution.py:24
  88.6 1.1 collective-permute-done.7
  89.8 17.8 %all-gather.7 = f16[1024,1024]{1,0:T(8,128)(2,1)S(1)} all-gather(f16[128,1024]{1,0:T(8,128)(2,1)S(1)} %convert_element_type.102), channel_id=1, replica_groups=mesh['y'=4,'core'=2,'xl'=2,'z'=8,'xh'=2] {'xh','xl','core'}, dimensions={0}, use_global_device_ids=true | all-gather | bytes 2359296 | tf_op jit(solution)/shard_map/all_gather | solution.py:249
  107.7 3.7 %abs_reduce_fusion = (f32[832]{0:T(1024)S(1)}, f32[832,1024]{1,0:T(8,128)}) fusion(bf16[832,1024]{1,0:T(8,128)(2,1)S(1)} %bitcast.47, f16[1024,1024]{1,0:T(8,128)(2,1)S(1)} %all-gather.7), kind=kOutput, calls=%fused_computation.4 | convolution fusion | flops 1747582208 | bytes 7212288 | tf_op jit(solution)/shard_map/dot_general | solution.py:253
  111.4 0.1 reshape.336
  111.5 2.5 %convert_convert_fusion = s16[4,208,1024]{2,1,0:T(8,128)(2,1)S(1)} fusion(f32[4,208,1024]{2,1,0:T(8,128)} %bitcast.45, f32[4,208]{1,0:T(4,128)S(1)} %reshape.329), kind=kLoop, calls=%fused_computation.3 | loop fusion | flops 3407872 | bytes 5115136 | tf_op jit(solution)/shard_map/convert_element_type | solution.py:89
  114.1 1.1 fusion.9
  115.2 3.3 %fusion.base_ref = bf16[1664,1024]{1,0:T(8,128)(2,1)} fusion(bf16[1664,1024]{1,0:T(8,128)(2,1)S(1)} %copy-done.4, s32[]{:T(128)S(6)} %min.14, bf16[1024,1024]{1,0:T(8,128)(2,1)S(1)} %get-tuple-element.41, pred[1664]{0:T(1024)(128)(4,1)S(1)} %fusion.19), kind=kLoop, calls=%fused_computation.2 | loop fusion | flops 1703936 | bytes 8914564 | tf_op jit(solution)/shard_map/jit(_where)/select_n | solution.py:283
  118.4 2.0 collective-permute-start.12
  120.5 1.3 constant_dynamic-slice_fusion.q_ref
  121.8 1.4 collective-permute-start.13
  123.3 5.7 %collective-permute-start.14 = (bf16[1024,256]{1,0:T(8,128)(2,1)S(1)}, bf16[1024,256]{1,0:T(8,128)(2,1)S(1)}, u32[]{:S(2)}, u32[]{:S(2)}) collective-permute-start(bf16[1024,256]{1,0:T(8,128)(2,1)S(1)} %select_select_fusion.2), channel_id=1, source_target_pairs={{0,6},{2,8},{4,10},{6,12},{8,14},{10,0},{12,2},{14,4},{1,7},{3,9},... | collective-permute-start | bytes 1572872 | tf_op jit(solution)/shard_map/ppermute | solution.py:24
  128.9 0.7 fusion.28
  129.6 12.8 %collective-permute-done.12 = s16[224,1024]{1,0:T(8,128)(2,1)S(1)} collective-permute-done((s16[224,1024]{1,0:T(8,128)(2,1)}, s16[224,1024]{1,0:T(8,128)(2,1)S(1)}, u32[]{:S(2)}, u32[]{:S(2)}) %collective-permute-start.12) | collective-permute-done | bytes 458784 | tf_op jit(solution)/shard_map/ppermute | solution.py:24
  142.5 0.7 fusion.22
  143.1 2.1 abs_reduce_fusion.2
  145.2 16.5 %collective-permute-done.14 = bf16[1024,256]{1,0:T(8,128)(2,1)S(1)} collective-permute-done((bf16[1024,256]{1,0:T(8,128)(2,1)S(1)}, bf16[1024,256]{1,0:T(8,128)(2,1)S(1)}, u32[]{:S(2)}, u32[]{:S(2)}) %collective-permute-start.14) | collective-permute-done | bytes 524320 | tf_op jit(solution)/shard_map/ppermute | solution.py:24
  161.7 3.3 %collective-permute-done.15 = bf16[1024,256]{1,0:T(8,128)(2,1)S(1)} collective-permute-done((bf16[1024,256]{1,0:T(8,128)(2,1)S(1)}, bf16[1024,256]{1,0:T(8,128)(2,1)S(1)}, u32[]{:S(2)}, u32[]{:S(2)}) %collective-permute-start.15) | collective-permute-done | bytes 524320 | tf_op jit(solution)/shard_map/ppermute | solution.py:24
  165.0 0.3 select_select_fusion.1
  165.3 3.0 %collective-permute-start.16 = (bf16[1024,256]{1,0:T(8,128)(2,1)S(1)}, bf16[1024,256]{1,0:T(8,128)(2,1)S(1)}, u32[]{:S(2)}, u32[]{:S(2)}) collective-permute-start(bf16[1024,256]{1,0:T(8,128)(2,1)S(1)} %select_select_fusion.1), channel_id=1, source_target_pairs={{0,2},{2,4},{4,6},{6,8},{8,10},{10,12},{12,14},{14,0},{1,3},{3,5},... | collective-permute-start | bytes 1572872 | tf_op jit(solution)/shard_map/ppermute | solution.py:24
  168.3 0.4 collective-permute-start.17
  168.6 0.1 convert_convert_fusion.1
  168.8 9.9 %collective-permute-done.16 = bf16[1024,256]{1,0:T(8,128)(2,1)S(1)} collective-permute-done((bf16[1024,256]{1,0:T(8,128)(2,1)S(1)}, bf16[1024,256]{1,0:T(8,128)(2,1)S(1)}, u32[]{:S(2)}, u32[]{:S(2)}) %collective-permute-start.16) | collective-permute-done | bytes 524320 | tf_op jit(solution)/shard_map/ppermute | solution.py:24
  178.8 2.2 collective-permute-done.17
  181.0 0.3 select_select_fusion.w_ref
  181.4 2.2 copy-done.2
  183.5 2.6 %block_error.1 = f32[1024,256]{1,0:T(8,128)S(1)} custom-call(f32[1024,1024]{1,0:T(8,128)S(1)} %copy-done.2, bf16[1024,256]{1,0:T(8,128)(2,1)S(1)} %select_select_fusion.w_ref, f32[1024,256]{1,0:T(8,128)S(1)} %constant_dynamic-slice_fusion.q_ref), custom_call_target="tpu_custom_call" | custom-call | flops 1610612736 | bytes 4194304 | tf_op jit(solution)/shard_map/block_error/pallas_call | solution.py:128
  186.3 0.1 fusion.3.e0
  186.5 2.5 %collective-permute-start.19 = (s16[1040,256]{1,0:T(8,128)(2,1)S(1)}, s16[1040,256]{1,0:T(8,128)(2,1)S(1)}, u32[]{:S(2)}, u32[]{:S(2)}) collective-permute-start(s16[1040,256]{1,0:T(8,128)(2,1)S(1)} %fusion.3.e0), channel_id=1, source_target_pairs={{0,1},{2,3},{4,5},{6,7},{8,9},{10,11},{12,13},{14,15},{16,17},{18,... | collective-permute-start | bytes 1597448 | tf_op jit(solution)/shard_map/ppermute | solution.py:276
  189.0 1.6 collective-permute-start.20
  190.6 19.8 %all-gather.8 = s16[1792,1024]{1,0:T(8,128)(2,1)S(1)} all-gather(s16[224,1024]{1,0:T(8,128)(2,1)S(1)} %pad_add_fusion), channel_id=2, replica_groups=mesh['y'=4,'core'=2,'xl'=2,'z'=8,'xh'=2] {'y','core'}, dimensions={0}, use_global_device_ids=true | all-gather | bytes 4128768 | tf_op jit(solution)/shard_map/all_gather | solution.py:263
  210.5 0.3 mul.219.scale_ref
  210.7 0.3 collective-permute-done.18.e1
  211.1 0.6 collective-permute-done.20.e3
  211.7 15.1 %apply_update.1 = bf16[1664,1024]{1,0:T(8,128)(2,1)} custom-call(s32[2]{0:T(128)S(1)} %pad_add_fusion.1.scalars, s16[4,2,224,1024]{3,2,1,0:T(8,128)(2,1)S(1)} %bitcast.44, f32[4,2,208,1]{3,2,1,0:T(8,128)S(1)} %mul.219.scale_ref, s16[1040,256]{1,0:T(8,128)(2,1)S(1)} %fusion.3.e0, s16[1040,256]{1,0:T(8,128)(2,1)S(1)} %collective-permute-done.18.e1, ...), custom_call_target="tpu_custom_call" | custom-call | flops 10468982784 | bytes 12320768 | tf_op jit(solution)/shard_map/apply_update/pallas_call | solution.py:175
  (61 shorter events, 1.1 us)
Async XLA Ops:
  6.5 19.2 %copy-start = (f32[32,1024]{1,0:T(8,128)S(1)}, f32[32,1024]{1,0:T(8,128)}, u32[]{:S(2)}) copy-start(f32[32,1024]{1,0:T(8,128)} %param.12) | copy-start | bytes 393220
  6.5 15.2 %copy-start.5 = (bf16[512,1664]{1,0:T(8,128)(2,1)S(1)}, bf16[512,1664]{1,0:T(8,128)(2,1)}, u32[]{:S(2)}) copy-start(bf16[512,1664]{1,0:T(8,128)(2,1)} %src_ref.2) | copy-start | bytes 5111812
  6.5 174.8 %all-gather.6.cloned.1.call-start = ((), (), s32[]{:S(2)}) async-start(), calls=%async_computation | async-start | bytes 4259840 | tf_op jit(solution)/shard_map/all_gather | solution.py:224
  12.4 26.6 %collective-permute-start = (bf16[128,1024]{1,0:T(8,128)(2,1)}, bf16[128,1024]{1,0:T(8,128)(2,1)S(1)}, u32[]{:S(2)}, u32[]{:S(2)}) collective-permute-start(bf16[128,1024]{1,0:T(8,128)(2,1)} %get-tuple-element.24), channel_id=1, source_target_pairs={{0,16},{2,18},{4,20},{6,22},{8,24},{10,26},{12,28},{14,30},{1,17},... | collective-permute-start | bytes 786440 | tf_op jit(solution)/shard_map/ppermute | solution.py:65
  15.8 23.2 %collective-permute-start.1 = (bf16[128,1024]{1,0:T(8,128)(2,1)}, bf16[128,1024]{1,0:T(8,128)(2,1)S(1)}, u32[]{:S(2)}, u32[]{:S(2)}) collective-permute-start(bf16[128,1024]{1,0:T(8,128)(2,1)} %get-tuple-element.25), channel_id=1, source_target_pairs={{0,1},{2,3},{4,5},{6,7},{8,9},{10,11},{12,13},{14,15},{1,0},{3,2},... | collective-permute-start | bytes 786440 | tf_op jit(solution)/shard_map/ppermute | solution.py:65
  20.4 18.6 %collective-permute-start.2 = (bf16[128,1024]{1,0:T(8,128)(2,1)}, bf16[128,1024]{1,0:T(8,128)(2,1)S(1)}, u32[]{:S(2)}, u32[]{:S(2)}) collective-permute-start(bf16[128,1024]{1,0:T(8,128)(2,1)} %get-tuple-element.26), channel_id=1, source_target_pairs={{0,17},{2,19},{4,21},{6,23},{8,25},{10,27},{12,29},{14,31},{1,16},... | collective-permute-start | bytes 786440 | tf_op jit(solution)/shard_map/ppermute | solution.py:65
  21.8 4.8 %copy-start.10 = (f32[16]{0:T(128)S(1)}, f32[16]{0:T(128)}, u32[]{:S(2)}) copy-start(f32[16]{0:T(128)} %param.11) | copy-start | bytes 196
  25.8 26.8 %collective-permute-start.5 = (bf16[512,832]{0,1:T(8,128)(2,1)}, bf16[512,832]{0,1:T(8,128)(2,1)}, u32[]{:S(2)}, u32[]{:S(2)}) collective-permute-start(bf16[512,832]{0,1:T(8,128)(2,1)} %copy.26), channel_id=1, source_target_pairs={{0,32},{32,0},{1,33},{33,1},{2,34},{34,2},{3,35},{35,3},{4,36},{36... | collective-permute-start | bytes 2555912 | tf_op jit(solution)/shard_map/ppermute | solution.py:24
  33.6 6.8 %copy-start.7 = (bf16[128,1024]{1,0:T(8,128)(2,1)S(1)}, bf16[128,1024]{1,0:T(8,128)(2,1)}, u32[]{:S(2)}) copy-start(bf16[128,1024]{1,0:T(8,128)(2,1)} %get-tuple-element.23) | copy-start | bytes 786436
  39.0 0.7 copy-start.8
  39.7 0.7 copy-start.9
  41.5 35.7 %collective-permute-start.3 = (bf16[128,1024]{1,0:T(8,128)(2,1)S(1)}, bf16[128,1024]{1,0:T(8,128)(2,1)}, u32[]{:S(2)}, u32[]{:S(2)}) collective-permute-start(bf16[128,1024]{1,0:T(8,128)(2,1)S(1)} %select_select_fusion.5), channel_id=1, source_target_pairs={{0,6},{2,8},{4,10},{6,12},{8,14},{10,0},{12,2},{14,4},{1,7},{3,9},... | collective-permute-start | bytes 786440 | tf_op jit(solution)/shard_map/ppermute | solution.py:24
  46.2 31.0 %collective-permute-start.4 = (bf16[128,1024]{1,0:T(8,128)(2,1)S(1)}, bf16[128,1024]{1,0:T(8,128)(2,1)}, u32[]{:S(2)}, u32[]{:S(2)}) collective-permute-start(bf16[128,1024]{1,0:T(8,128)(2,1)S(1)} %select_select_fusion.5), channel_id=1, source_target_pairs={{0,10},{2,12},{4,14},{6,0},{8,2},{10,4},{12,6},{14,8},{1,11},{3,13... | collective-permute-start | bytes 786440 | tf_op jit(solution)/shard_map/ppermute | solution.py:24
  48.4 33.4 %collective-permute-start.10 = (bf16[1024,256]{1,0:T(8,128)(2,1)}, bf16[1024,256]{1,0:T(8,128)(2,1)}, u32[]{:S(2)}, u32[]{:S(2)}) collective-permute-start(bf16[1024,256]{1,0:T(8,128)(2,1)} %get-tuple-element.38), channel_id=1, source_target_pairs={{0,17},{2,19},{4,21},{6,23},{8,25},{10,27},{12,29},{14,31},{1,16},... | collective-permute-start | bytes 1572872 | tf_op jit(solution)/shard_map/ppermute | solution.py:65
  50.5 31.3 %collective-permute-start.8 = (bf16[1024,256]{1,0:T(8,128)(2,1)}, bf16[1024,256]{1,0:T(8,128)(2,1)}, u32[]{:S(2)}, u32[]{:S(2)}) collective-permute-start(bf16[1024,256]{1,0:T(8,128)(2,1)} %get-tuple-element.36), channel_id=1, source_target_pairs={{0,16},{2,18},{4,20},{6,22},{8,24},{10,26},{12,28},{14,30},{1,17},... | collective-permute-start | bytes 1572872 | tf_op jit(solution)/shard_map/ppermute | solution.py:65
  52.5 29.2 %collective-permute-start.9 = (bf16[1024,256]{1,0:T(8,128)(2,1)}, bf16[1024,256]{1,0:T(8,128)(2,1)}, u32[]{:S(2)}, u32[]{:S(2)}) collective-permute-start(bf16[1024,256]{1,0:T(8,128)(2,1)} %get-tuple-element.37), channel_id=1, source_target_pairs={{0,1},{2,3},{4,5},{6,7},{8,9},{10,11},{12,13},{14,15},{1,0},{3,2},... | collective-permute-start | bytes 1572872 | tf_op jit(solution)/shard_map/ppermute | solution.py:65
  78.2 10.3 %collective-permute-start.6 = (bf16[128,1024]{1,0:T(8,128)(2,1)S(1)}, bf16[128,1024]{1,0:T(8,128)(2,1)S(1)}, u32[]{:S(2)}, u32[]{:S(2)}) collective-permute-start(bf16[128,1024]{1,0:T(8,128)(2,1)S(1)} %select_select_fusion.4), channel_id=1, source_target_pairs={{0,2},{2,4},{4,6},{6,8},{8,10},{10,12},{12,14},{14,0},{1,3},{3,5},... | collective-permute-start | bytes 786440 | tf_op jit(solution)/shard_map/ppermute | solution.py:24
  80.2 9.5 %collective-permute-start.7 = (bf16[128,1024]{1,0:T(8,128)(2,1)S(1)}, bf16[128,1024]{1,0:T(8,128)(2,1)S(1)}, u32[]{:S(2)}, u32[]{:S(2)}) collective-permute-start(bf16[128,1024]{1,0:T(8,128)(2,1)S(1)} %select_select_fusion.4), channel_id=1, source_target_pairs={{0,14},{2,0},{4,2},{6,4},{8,6},{10,8},{12,10},{14,12},{1,15},{3,1}... | collective-permute-start | bytes 786440 | tf_op jit(solution)/shard_map/ppermute | solution.py:24
  83.2 24.5 %copy-start.6 = (bf16[1024,832]{0,1:T(8,128)(2,1)S(1)}, bf16[1024,832]{0,1:T(8,128)(2,1)}, u32[]{:S(2)}) copy-start(bf16[1024,832]{0,1:T(8,128)(2,1)} %reshape.317) | copy-start | bytes 5111812
  111.5 3.6 %copy-start.4 = (bf16[1664,1024]{1,0:T(8,128)(2,1)S(1)}, bf16[1664,1024]{1,0:T(8,128)(2,1)}, u32[]{:S(2)}) copy-start(bf16[1664,1024]{1,0:T(8,128)(2,1)} %src_ref.3) | copy-start | bytes 10223620
  115.2 13.8 %collective-permute-start.11 = (s16[224,1024]{1,0:T(8,128)(2,1)}, s16[224,1024]{1,0:T(8,128)(2,1)}, u32[]{:S(2)}, u32[]{:S(2)}) collective-permute-start(s16[224,1024]{1,0:T(8,128)(2,1)} %get-tuple-element.51), channel_id=1, source_target_pairs={{0,64},{64,128},{128,192},{192,0},{1,65},{65,129},{129,193},{193,1... | collective-permute-start | bytes 1376264 | tf_op jit(solution)/shard_map/ppermute | solution.py:24
  118.4 24.0 %collective-permute-start.12 = (s16[224,1024]{1,0:T(8,128)(2,1)}, s16[224,1024]{1,0:T(8,128)(2,1)S(1)}, u32[]{:S(2)}, u32[]{:S(2)}) collective-permute-start(s16[224,1024]{1,0:T(8,128)(2,1)} %get-tuple-element.52), channel_id=1, source_target_pairs={{0,192},{64,0},{128,64},{192,128},{1,193},{65,1},{129,65},{193,129... | collective-permute-start | bytes 1376264 | tf_op jit(solution)/shard_map/ppermute | solution.py:24
  121.8 20.7 %collective-permute-start.13 = (s16[224,1024]{1,0:T(8,128)(2,1)S(1)}, s16[224,1024]{1,0:T(8,128)(2,1)}, u32[]{:S(2)}, u32[]{:S(2)}) collective-permute-start(s16[224,1024]{1,0:T(8,128)(2,1)S(1)} %get-tuple-element.53), channel_id=1, source_target_pairs={{0,128},{64,192},{128,0},{192,64},{1,129},{65,193},{129,1},{193,65... | collective-permute-start | bytes 1376264 | tf_op jit(solution)/shard_map/ppermute | solution.py:24
  123.3 38.4 %collective-permute-start.14 = (bf16[1024,256]{1,0:T(8,128)(2,1)S(1)}, bf16[1024,256]{1,0:T(8,128)(2,1)S(1)}, u32[]{:S(2)}, u32[]{:S(2)}) collective-permute-start(bf16[1024,256]{1,0:T(8,128)(2,1)S(1)} %select_select_fusion.2), channel_id=1, source_target_pairs={{0,6},{2,8},{4,10},{6,12},{8,14},{10,0},{12,2},{14,4},{1,7},{3,9},... | collective-permute-start | bytes 1572872 | tf_op jit(solution)/shard_map/ppermute | solution.py:24
  128.9 36.0 %collective-permute-start.15 = (bf16[1024,256]{1,0:T(8,128)(2,1)S(1)}, bf16[1024,256]{1,0:T(8,128)(2,1)S(1)}, u32[]{:S(2)}, u32[]{:S(2)}) collective-permute-start(bf16[1024,256]{1,0:T(8,128)(2,1)S(1)} %select_select_fusion.2), channel_id=1, source_target_pairs={{0,10},{2,12},{4,14},{6,0},{8,2},{10,4},{12,6},{14,8},{1,11},{3,13... | collective-permute-start | bytes 1572872 | tf_op jit(solution)/shard_map/ppermute | solution.py:24
  165.3 13.5 %collective-permute-start.16 = (bf16[1024,256]{1,0:T(8,128)(2,1)S(1)}, bf16[1024,256]{1,0:T(8,128)(2,1)S(1)}, u32[]{:S(2)}, u32[]{:S(2)}) collective-permute-start(bf16[1024,256]{1,0:T(8,128)(2,1)S(1)} %select_select_fusion.1), channel_id=1, source_target_pairs={{0,2},{2,4},{4,6},{6,8},{8,10},{10,12},{12,14},{14,0},{1,3},{3,5},... | collective-permute-start | bytes 1572872 | tf_op jit(solution)/shard_map/ppermute | solution.py:24
  168.3 12.7 %collective-permute-start.17 = (bf16[1024,256]{1,0:T(8,128)(2,1)S(1)}, bf16[1024,256]{1,0:T(8,128)(2,1)S(1)}, u32[]{:S(2)}, u32[]{:S(2)}) collective-permute-start(bf16[1024,256]{1,0:T(8,128)(2,1)S(1)} %select_select_fusion.1), channel_id=1, source_target_pairs={{0,14},{2,0},{4,2},{6,4},{8,6},{10,8},{12,10},{14,12},{1,15},{3,1}... | collective-permute-start | bytes 1572872 | tf_op jit(solution)/shard_map/ppermute | solution.py:24
  181.4 2.2 copy-start.2
  186.4 25.3 %copy-start.3 = (bf16[1664,1024]{1,0:T(8,128)(2,1)S(1)}, bf16[1664,1024]{1,0:T(8,128)(2,1)}, u32[]{:S(2)}) copy-start(bf16[1664,1024]{1,0:T(8,128)(2,1)} %fusion.base_ref) | copy-start | bytes 10223620
  186.4 24.6 %collective-permute-start.18 = (s16[1040,256]{1,0:T(8,128)(2,1)S(1)}, s16[1040,256]{1,0:T(8,128)(2,1)S(1)}, u32[]{:S(2)}, u32[]{:S(2)}) collective-permute-start(s16[1040,256]{1,0:T(8,128)(2,1)S(1)} %fusion.3.e0), channel_id=1, source_target_pairs={{0,16},{2,18},{4,20},{6,22},{8,24},{10,26},{12,28},{14,30},{16,1},... | collective-permute-start | bytes 1597448 | tf_op jit(solution)/shard_map/ppermute | solution.py:276
  186.5 24.6 %collective-permute-start.19 = (s16[1040,256]{1,0:T(8,128)(2,1)S(1)}, s16[1040,256]{1,0:T(8,128)(2,1)S(1)}, u32[]{:S(2)}, u32[]{:S(2)}) collective-permute-start(s16[1040,256]{1,0:T(8,128)(2,1)S(1)} %fusion.3.e0), channel_id=1, source_target_pairs={{0,1},{2,3},{4,5},{6,7},{8,9},{10,11},{12,13},{14,15},{16,17},{18,... | collective-permute-start | bytes 1597448 | tf_op jit(solution)/shard_map/ppermute | solution.py:276
  189.0 22.7 %collective-permute-start.20 = (s16[1040,256]{1,0:T(8,128)(2,1)S(1)}, s16[1040,256]{1,0:T(8,128)(2,1)S(1)}, u32[]{:S(2)}, u32[]{:S(2)}) collective-permute-start(s16[1040,256]{1,0:T(8,128)(2,1)S(1)} %fusion.3.e0), channel_id=1, source_target_pairs={{0,17},{2,19},{4,21},{6,23},{8,25},{10,27},{12,29},{14,31},{16,0},... | collective-permute-start | bytes 1597448 | tf_op jit(solution)/shard_map/ppermute | solution.py:276
  211.7 15.1 %copy-start.1 = (f32[32,1024]{1,0:T(8,128)S(1)}, f32[32,1024]{1,0:T(8,128)}, u32[]{:S(2)}) copy-start(f32[32,1024]{1,0:T(8,128)} %param.12) | copy-start | bytes 393220
Sparse Core Ops, SparseCore 0:
  26.5 86.9 all-gather.5

commit v3 on v2

--- a/solution.py
+++ b/solution.py
@@ -71,15 +71,17 @@
     return jnp.where(from_low, near, far)
 
 
-def spread_z(piece, distance, beside=None):
+def reach_far(piece, distance, beside=()):
     up, down = ring("z", 8, 3, piece), ring("z", 8, -3, piece)
-    if beside is not None:
-        up, down, beside = lax.optimization_barrier((up, down, beside))
-    piece = jnp.where(distance == 3, up, jnp.where(distance == 5, down, piece))
+    up, down, *beside = lax.optimization_barrier((up, down, *beside))
+    return jnp.where(distance == 3, up, jnp.where(distance == 5, down, piece)), *beside
+
+
+def reach_near(piece, distance):
     up, down = ring("z", 8, 1, piece), ring("z", 8, -1, piece)
     from_below = (distance == 1) | (distance == 4) | (distance == 6)
     from_above = (distance == 7) | (distance == 2)
-    return jnp.where(from_below, up, jnp.where(from_above, down, piece)), beside
+    return jnp.where(from_below, up, jnp.where(from_above, down, piece))
 
 
 def quantize(values):
@@ -221,6 +223,7 @@
 
     own_rows = inverse_block.shape[0] // 2
     inverse_part = lax.dynamic_slice_in_dim(inverse_block, core * own_rows, own_rows, 0)
+    inverse_part, activations = lax.optimization_barrier((inverse_part, activations))
     inverse = lax.all_gather(inverse_part, ("xh", "xl", "z", "core"), axis=0)
     inverse = inverse.reshape(BLK, BLK)
 
@@ -233,18 +236,20 @@
     x_mine = lax.dynamic_slice_in_dim(activations, core * half, half, 1)
     x_theirs = lax.dynamic_slice_in_dim(activations, (1 - core) * half, half, 1)
     x_other = ring("core", 2, 1, x_theirs)
-    x_low = jnp.where(core == 0, x_mine, x_other).reshape(4, 128, half)
-    x_high = jnp.where(core == 0, x_other, x_mine).reshape(4, 128, half)
-    x_rows = jnp.stack([x_low, x_high], axis=1).reshape(1024, half).T
+    x_low = jnp.where(core == 0, x_mine, x_other)
+    x_high = jnp.where(core == 0, x_other, x_mine)
+    x_rows = jnp.concatenate(
+        [v[128 * p : 128 * (p + 1)] for p in range(4) for v in (x_low, x_high)], axis=0
+    ).T
 
     lanes = lambda v: jnp.repeat(v, UNIT)[None, :]
     sublanes = lambda v: jnp.repeat(v, UNIT)[:, None]
     x_piece = scatter_x(x_pieces, x, lanes(from_low))
     x_piece, w_pieces = lax.optimization_barrier((x_piece, w_pieces))
     w_piece = scatter_x(w_pieces, x, sublanes(from_low))
-    x_piece, x_rows = spread_z(x_piece, lanes(distance), x_rows)
+    x_piece, x_rows = reach_far(x_piece, lanes(distance), (x_rows,))
     x_piece, w_piece = lax.optimization_barrier((x_piece, w_piece))
-    w_piece, _ = spread_z(w_piece, sublanes(distance))
+    x_piece = reach_near(x_piece, lanes(distance))
 
     x_block = lax.all_gather(
         x_piece.astype(jnp.float16), ("xh", "xl", "core"), axis=0, tiled=True
@@ -253,24 +258,28 @@
     partial_panel = lax.dot_general(
         x_rows, x_block, (((1,), (0,)), ((), ())), preferred_element_type=F32
     )
+    w_piece, partial_panel = reach_far(w_piece, sublanes(distance), (partial_panel,))
+    w_piece = reach_near(w_piece, sublanes(distance))
     quarter = half // 4
     parts = partial_panel.reshape(4, quarter, BLK)
     message = quantize(parts)
+    message, codes, scale_index = lax.optimization_barrier((message, codes, scale_index))
     total = lax.dynamic_index_in_dim(parts, y, 0, False)
     for shift in (1, 3, 2):
         sent = lax.dynamic_index_in_dim(message, (y + shift) % 4, 0, False)
         total = total + dequantize(ring("y", 4, shift, sent))
+    chosen = (scale_index[:, :, None] == jnp.arange(LEVELS, dtype=jnp.int32)).astype(F32)
+    group_scale = jnp.sum(chosen * scale_table, axis=2)
+    quantized = jnp.repeat(group_scale, GROUP, axis=0) * (codes.astype(F32) - 7.5)
+
+    wide = w_piece.shape[1]
+    own_columns = lax.dynamic_slice_in_dim(quantized, x * wide, wide, 1)
+    error = quantize_columns(block_error(inverse, w_piece, own_columns))
+    total, error = lax.optimization_barrier((total, error))
     panel = lax.all_gather(quantize(total), ("y", "core"), axis=0)
     panel = panel.reshape(4, 2, quarter + 16, BLK)
     scales = scales_of(panel) * (2.0 / token_total)
 
-    chosen = (scale_index[:, :, None] == jnp.arange(LEVELS, dtype=jnp.int32)).astype(F32)
-    group_scale = jnp.sum(chosen * scale_table, axis=2)
-    quantized = jnp.repeat(group_scale, GROUP, axis=0) * (codes.astype(F32) - 7.5)
-
-    wide = w_piece.shape[1]
-    own_columns = lax.dynamic_slice_in_dim(quantized, x * wide, wide, 1)
-    error = quantize_columns(block_error(inverse, w_piece, own_columns))
     errors = [error]
     for shift in (1, 2, 3):
         errors.append(lax.ppermute(error, PLANE, plane_pairs(range(4), shift)))

time: 236 us -> 209 us (0.89)
  local copies, waits for them, and re-layouts: 24.2 us -> 7.62 us
  other arithmetic: 31.3 us -> 17.1 us
  starting transfers between devices: 43.2 us -> 46.4 us
  waiting for transfers between devices: 52.2 us -> 54.6 us
    ppermute x12, waiting for transfers between devices: 51.2 us -> 40.2 us  [ring(): lax.ppermute(value, axis, [(i, (i + shift) % size) for i in range(size)])]
    ppermute x6, waiting for transfers between devices: 0.02 us -> 9.47 us  [scatter_x(): lax.ppermute(piece, PLANE, plane_pairs((0, 2), shift))]
    another operation x2 -> x0, local copies, waits for them, and re-layouts: 7.79 us -> none  [local(): x_rows = jnp.stack([x_low, x_high], axis=1).reshape(1024, half).T]
    another operation x1 -> x0, other arithmetic: 6.66 us -> none  [local(): x_rows = jnp.stack([x_low, x_high], axis=1).reshape(1024, half).T]
    reshape x1 -> x0, local copies, waits for them, and re-layouts: 5.01 us -> none  [local(): x_rows = jnp.stack([x_low, x_high], axis=1).reshape(1024, half).T]
    convert_element_type x1, other arithmetic: 5.31 us -> 1.05 us  [local(): padded = jnp.pad(quantized.astype(BF16), [(shard_rows, shard_rows), (0, 0)])]
    ppermute x3, waiting for transfers between devices: 0.95 us -> 4.87 us  [local(): errors.append(lax.ppermute(error, PLANE, plane_pairs(range(4), shift)))]
    unnamed x24 -> x31, local copies, waits for them, and re-layouts: 7.04 us -> 4.55 us
  transfers between devices with their start and end apart: 22 -> 22, of which waited for: 9 -> 12; matrix products, arithmetic and copies ran while one was open for 23% -> 11% of each run, Pallas kernels for 2% -> 4%
where the time goes in v3:
time: 209 us; the launch traced here: 207 us
  waiting for transfers between devices  54.6 us (26%)
  starting transfers between devices  46.4 us (22%)
  blocking collectives  37 us (18%)
  Pallas kernels  26.7 us (13%)
  other arithmetic  17.1 us (8%)
  between operations  14.5 us (7%)
  local copies, waits for them, and re-layouts  7.62 us (4%)
  matrix products  3.39 us (2%)
    ppermute x12, waiting for transfers between devices, ring(): lax.ppermute(value, axis, [(i, (i + shift) % size) for i in range(size)])  40.2 us
    ppermute x12, starting transfers between devices, ring(): lax.ppermute(value, axis, [(i, (i + shift) % size) for i in range(size)])  23.7 us
    all_gather x1, blocking collectives, local(): panel = lax.all_gather(quantize(total), ('y', 'core'), axis=0)  19.9 us
    ppermute x6, starting transfers between devices, scatter_x(): lax.ppermute(piece, PLANE, plane_pairs((0, 2), shift))  18.7 us
    all_gather x1, blocking collectives, local(): lax.all_gather(x_piece.astype(jnp.float16), ('xh', 'xl', 'core'), axis=0,...  17 us
    pallas_call x1, Pallas kernels, apply_update(): pl.pallas_call(update_kernel, grid_spec=pltpu.PrefetchScalarGridSpec(num_...  15.1 us
    ppermute x6, waiting for transfers between devices, scatter_x(): lax.ppermute(piece, PLANE, plane_pairs((0, 2), shift))  9.47 us
    pallas_call x2, Pallas kernels, pick(): pl.pallas_call(functools.partial(pick_kernel, rows, cols), grid_spec=pltp...  8.95 us
  transfers between devices with their start and end apart: 22, of which 12 were waited for; matrix products, arithmetic and copies ran while one was open for 11% of the time, Pallas kernels for 4%

profile of v3, /device:TPU:24, one launch (start us, length us, event | category | flops | bytes accessed | tf_op | source)
XLA Modules:
  0.0 207.3 jit_solution(17516957957196993295)
XLA Ops:
  6.5 0.9 copy-done
  7.4 0.6 constant_dynamic-slice_fusion.2
  8.8 0.6 pad_add_fusion.3.scalars
  9.4 4.4 %pick_columns.1 = (bf16[128,1024]{1,0:T(8,128)(2,1)}, bf16[128,1024]{1,0:T(8,128)(2,1)}, bf16[128,1024]{1,0:T(8,128)(2,1)}, bf16[128,1024]{1,0:T(8,128)(2,1)}) custom-call(s32[9]{0:T(128)} %pad_add_fusion.3.scalars, bf16[512,1664]{1,0:T(8,128)(2,1)} %src_ref.1), custom_call_target="tpu_custom_call" | custom-call | tf_op jit(solution)/shard_map/pick_columns/pallas_call | solution.py:48
  13.7 4.1 %collective-permute-start = (bf16[128,1024]{1,0:T(8,128)(2,1)}, bf16[128,1024]{1,0:T(8,128)(2,1)}, u32[]{:S(2)}, u32[]{:S(2)}) collective-permute-start(bf16[128,1024]{1,0:T(8,128)(2,1)} %get-tuple-element.35), channel_id=1, source_target_pairs={{0,16},{2,18},{4,20},{6,22},{8,24},{10,26},{12,28},{14,30},{1,17},... | collective-permute-start | bytes 786440 | tf_op jit(solution)/shard_map/ppermute | solution.py:65
  17.8 4.6 %collective-permute-start.1 = (bf16[128,1024]{1,0:T(8,128)(2,1)}, bf16[128,1024]{1,0:T(8,128)(2,1)}, u32[]{:S(2)}, u32[]{:S(2)}) collective-permute-start(bf16[128,1024]{1,0:T(8,128)(2,1)} %get-tuple-element.36), channel_id=1, source_target_pairs={{0,1},{2,3},{4,5},{6,7},{8,9},{10,11},{12,13},{14,15},{1,0},{3,2},... | collective-permute-start | bytes 786440 | tf_op jit(solution)/shard_map/ppermute | solution.py:65
  22.4 2.0 collective-permute-start.2
  24.5 1.4 copy.15
  25.9 0.1 collective-permute-start.5
  26.1 4.6 %pick_rows.1 = (bf16[1024,256]{1,0:T(8,128)(2,1)}, bf16[1024,256]{1,0:T(8,128)(2,1)}, bf16[1024,256]{1,0:T(8,128)(2,1)}, bf16[1024,256]{1,0:T(8,128)(2,1)}) custom-call(s32[9]{0:T(128)} %pad_add_fusion.3.scalars, bf16[1664,1024]{1,0:T(8,128)(2,1)} %src_ref.2), custom_call_target="tpu_custom_call" | custom-call | tf_op jit(solution)/shard_map/pick_rows/pallas_call | solution.py:48
  30.8 1.4 collective-permute-done.1
  32.2 1.0 select_select_fusion.4
  33.2 1.3 collective-permute-start.6
  34.5 5.3 %collective-permute-start.7 = (bf16[1024,256]{1,0:T(8,128)(2,1)}, bf16[1024,256]{1,0:T(8,128)(2,1)S(1)}, u32[]{:S(2)}, u32[]{:S(2)}) collective-permute-start(bf16[1024,256]{1,0:T(8,128)(2,1)} %get-tuple-element.47), channel_id=1, source_target_pairs={{0,1},{2,3},{4,5},{6,7},{8,9},{10,11},{12,13},{14,15},{1,0},{3,2},... | collective-permute-start | bytes 1572872 | tf_op jit(solution)/shard_map/ppermute | solution.py:65
  39.8 1.3 collective-permute-start.8
  41.2 7.1 %collective-permute-start.4 = (bf16[128,1024]{1,0:T(8,128)(2,1)S(1)}, bf16[128,1024]{1,0:T(8,128)(2,1)S(1)}, u32[]{:S(2)}, u32[]{:S(2)}) collective-permute-start(bf16[128,1024]{1,0:T(8,128)(2,1)S(1)} %select_select_fusion.4), channel_id=1, source_target_pairs={{0,10},{2,12},{4,14},{6,0},{8,2},{10,4},{12,6},{14,8},{1,11},{3,13... | collective-permute-start | bytes 786440 | tf_op jit(solution)/shard_map/ppermute | solution.py:24
  48.3 3.6 %collective-permute-start.3 = (bf16[128,1024]{1,0:T(8,128)(2,1)S(1)}, bf16[128,1024]{1,0:T(8,128)(2,1)S(1)}, u32[]{:S(2)}, u32[]{:S(2)}) collective-permute-start(bf16[128,1024]{1,0:T(8,128)(2,1)S(1)} %select_select_fusion.4), channel_id=1, source_target_pairs={{0,6},{2,8},{4,10},{6,12},{8,14},{10,0},{12,2},{14,4},{1,7},{3,9},... | collective-permute-start | bytes 786440 | tf_op jit(solution)/shard_map/ppermute | solution.py:24
  51.9 8.1 %collective-permute-done.7 = bf16[1024,256]{1,0:T(8,128)(2,1)S(1)} collective-permute-done((bf16[1024,256]{1,0:T(8,128)(2,1)}, bf16[1024,256]{1,0:T(8,128)(2,1)S(1)}, u32[]{:S(2)}, u32[]{:S(2)}) %collective-permute-start.7) | collective-permute-done | bytes 524320 | tf_op jit(solution)/shard_map/ppermute | solution.py:65
  60.0 2.1 %select_select_fusion.2 = bf16[1024,256]{1,0:T(8,128)(2,1)} fusion(bf16[1024,256]{1,0:T(8,128)(2,1)S(1)} %collective-permute-done.7, bf16[1024,256]{1,0:T(8,128)(2,1)S(1)} %collective-permute-done.8, bf16[1024,256]{1,0:T(8,128)(2,1)} %get-tuple-element.45, bf16[1024,256]{1,0:T(8,128)(2,1)S(1)} %collective-permute-done.6, ...), kind=kLoop, calls=%fused_computation.23 | loop fusion | flops 786432 | bytes 2622465 | tf_op jit(solution)/shard_map/jit(_where)/select_n | solution.py:71
  62.1 1.5 broadcast_select_fusion
  64.3 3.2 %collective-permute-done.3 = bf16[128,1024]{1,0:T(8,128)(2,1)S(1)} collective-permute-done((bf16[128,1024]{1,0:T(8,128)(2,1)S(1)}, bf16[128,1024]{1,0:T(8,128)(2,1)S(1)}, u32[]{:S(2)}, u32[]{:S(2)}) %collective-permute-start.3) | collective-permute-done | bytes 262176 | tf_op jit(solution)/shard_map/ppermute | solution.py:24
  67.5 4.1 %collective-permute-start.12 = (bf16[128,1024]{1,0:T(8,128)(2,1)S(1)}, bf16[128,1024]{1,0:T(8,128)(2,1)S(1)}, u32[]{:S(2)}, u32[]{:S(2)}) collective-permute-start(bf16[128,1024]{1,0:T(8,128)(2,1)S(1)} %select_select_fusion.3), channel_id=1, source_target_pairs={{0,14},{2,0},{4,2},{6,4},{8,6},{10,8},{12,10},{14,12},{1,15},{3,1}... | collective-permute-start | bytes 786440 | tf_op jit(solution)/shard_map/ppermute | solution.py:24
  71.8 2.9 %collective-permute-start.10 = (bf16[1024,256]{1,0:T(8,128)(2,1)}, bf16[1024,256]{1,0:T(8,128)(2,1)S(1)}, u32[]{:S(2)}, u32[]{:S(2)}) collective-permute-start(bf16[1024,256]{1,0:T(8,128)(2,1)} %select_select_fusion.2), channel_id=1, source_target_pairs={{0,10},{2,12},{4,14},{6,0},{8,2},{10,4},{12,6},{14,8},{1,11},{3,13... | collective-permute-start | bytes 1572872 | tf_op jit(solution)/shard_map/ppermute | solution.py:24
  74.7 0.9 collective-permute-start.9
  75.6 6.9 %collective-permute-done.12 = bf16[128,1024]{1,0:T(8,128)(2,1)S(1)} collective-permute-done((bf16[128,1024]{1,0:T(8,128)(2,1)S(1)}, bf16[128,1024]{1,0:T(8,128)(2,1)S(1)}, u32[]{:S(2)}, u32[]{:S(2)}) %collective-permute-start.12) | collective-permute-done | bytes 262176 | tf_op jit(solution)/shard_map/ppermute | solution.py:24
  82.5 11.4 %collective-permute-done.11 = bf16[128,1024]{1,0:T(8,128)(2,1)S(1)} collective-permute-done((bf16[128,1024]{1,0:T(8,128)(2,1)S(1)}, bf16[128,1024]{1,0:T(8,128)(2,1)S(1)}, u32[]{:S(2)}, u32[]{:S(2)}) %collective-permute-start.11) | collective-permute-done | bytes 262176 | tf_op jit(solution)/shard_map/ppermute | solution.py:24
  94.0 17.0 %all-gather.7 = f16[1024,1024]{1,0:T(8,128)(2,1)S(1)} all-gather(f16[128,1024]{1,0:T(8,128)(2,1)S(1)} %select_convert_fusion), channel_id=1, replica_groups=mesh['y'=4,'core'=2,'xl'=2,'z'=8,'xh'=2] {'xh','xl','core'}, dimensions={0}, use_global_device_ids=true | all-gather | bytes 2359296 | tf_op jit(solution)/shard_map/all_gather | solution.py:254
  111.0 3.4 %fusion.1 = f32[832,1024]{1,0:T(8,128)S(1)} fusion(bf16[832,1024]{1,0:T(8,128)(2,1)} %bitcast.40, f16[1024,1024]{1,0:T(8,128)(2,1)S(1)} %all-gather.7), kind=kOutput, calls=%fused_computation.5 | convolution fusion | flops 1745879040 | bytes 7208960 | tf_op jit(solution)/shard_map/dot_general | solution.py:258
  114.4 1.1 collective-permute-done.10
  115.5 6.0 %collective-permute-done.9 = bf16[1024,256]{1,0:T(8,128)(2,1)S(1)} collective-permute-done((bf16[1024,256]{1,0:T(8,128)(2,1)}, bf16[1024,256]{1,0:T(8,128)(2,1)S(1)}, u32[]{:S(2)}, u32[]{:S(2)}) %collective-permute-start.9) | collective-permute-done | bytes 524320 | tf_op jit(solution)/shard_map/ppermute | solution.py:24
  121.5 2.2 %select_select_fusion.1 = bf16[1024,256]{1,0:T(8,128)(2,1)} fusion(bf16[1024,256]{1,0:T(8,128)(2,1)S(1)} %collective-permute-done.9, bf16[1024,256]{1,0:T(8,128)(2,1)S(1)} %collective-permute-done.10, bf16[1024,256]{1,0:T(8,128)(2,1)} %select_select_fusion.2, pred[1024]{0:T(1024)(128)(4,1)S(1)} %get-tuple-element.79, pred[1024]{0:T(1024)(128)(4,1)S(1)} %get-tuple-element.80), kind=kLoop, calls=%fused_computation.22 | loop fusion | flops 524288 | bytes 2099200 | tf_op jit(solution)/shard_map/jit(_where)/select_n | solution.py:77
  123.7 1.5 collective-permute-start.17
  125.2 0.5 collective-permute-start.16
  125.7 0.3 abs_reduce_fusion
  126.1 0.1 reshape.325
  126.2 0.1 reshape.332
  126.3 0.3 convert_convert_fusion
  126.6 0.2 pad_add_fusion
  126.8 0.1 dynamic-slice_bitcast_fusion.2
  126.9 0.5 collective-permute-start.13
  127.4 2.5 %collective-permute-start.15 = (s16[224,1024]{1,0:T(8,128)(2,1)S(1)}, s16[224,1024]{1,0:T(8,128)(2,1)S(1)}, u32[]{:S(2)}, u32[]{:S(2)}) collective-permute-start(s16[224,1024]{1,0:T(8,128)(2,1)S(1)} %get-tuple-element.72), channel_id=1, source_target_pairs={{0,128},{64,192},{128,0},{192,64},{1,129},{65,193},{129,1},{193,65... | collective-permute-start | bytes 1376264 | tf_op jit(solution)/shard_map/ppermute | solution.py:24
  129.9 0.2 select_reduce_fusion
  130.1 1.0 fusion.28
  131.2 0.9 copy-done.5
  132.1 3.3 %fusion.base_ref = bf16[1664,1024]{1,0:T(8,128)(2,1)} fusion(bf16[1664,1024]{1,0:T(8,128)(2,1)S(1)} %copy-done.5, s32[]{:T(128)S(6)} %min.14, bf16[1024,1024]{1,0:T(8,128)(2,1)S(1)} %get-tuple-element.61, pred[1664]{0:T(1024)(128)(4,1)S(1)} %fusion.13), kind=kLoop, calls=%fused_computation.2 | loop fusion | flops 1703936 | bytes 8914564 | tf_op jit(solution)/shard_map/jit(_where)/select_n | solution.py:292
  135.4 0.1 constant_dynamic-slice_fusion.q_ref
  135.5 4.9 %collective-permute-done.13 = s16[224,1024]{1,0:T(8,128)(2,1)S(1)} collective-permute-done((s16[224,1024]{1,0:T(8,128)(2,1)S(1)}, s16[224,1024]{1,0:T(8,128)(2,1)S(1)}, u32[]{:S(2)}, u32[]{:S(2)}) %collective-permute-start.13) | collective-permute-done | bytes 458784 | tf_op jit(solution)/shard_map/ppermute | solution.py:24
  140.4 1.9 collective-permute-done.15
  142.3 4.9 %collective-permute-done.14 = s16[224,1024]{1,0:T(8,128)(2,1)S(1)} collective-permute-done((s16[224,1024]{1,0:T(8,128)(2,1)S(1)}, s16[224,1024]{1,0:T(8,128)(2,1)S(1)}, u32[]{:S(2)}, u32[]{:S(2)}) %collective-permute-start.14) | collective-permute-done | bytes 458784 | tf_op jit(solution)/shard_map/ppermute | solution.py:24
  147.2 1.7 fusion.5
  148.9 1.7 select_select_fusion.w_ref
  150.6 2.2 %copy-done.2 = f32[1024,1024]{1,0:T(8,128)S(1)} copy-done((f32[1024,1024]{1,0:T(8,128)S(1)}, f32[1024,1024]{1,0:T(8,128)}, u32[]{:S(2)}) %copy-start.2) | copy-done | bytes 4194328
  152.8 2.6 %block_error.1 = f32[1024,256]{1,0:T(8,128)S(1)} custom-call(f32[1024,1024]{1,0:T(8,128)S(1)} %copy-done.2, bf16[1024,256]{1,0:T(8,128)(2,1)S(1)} %select_select_fusion.w_ref, f32[1024,256]{1,0:T(8,128)S(1)} %constant_dynamic-slice_fusion.q_ref), custom_call_target="tpu_custom_call" | custom-call | flops 1610612736 | bytes 4194304 | tf_op jit(solution)/shard_map/block_error/pallas_call | solution.py:130
  155.5 0.1 multiply_round-nearest-even_fusion
  155.6 0.1 fusion.3.e0
  155.7 3.0 %collective-permute-start.20 = (s16[1040,256]{1,0:T(8,128)(2,1)S(1)}, s16[1040,256]{1,0:T(8,128)(2,1)S(1)}, u32[]{:S(2)}, u32[]{:S(2)}) collective-permute-start(s16[1040,256]{1,0:T(8,128)(2,1)S(1)} %fusion.3.e0), channel_id=1, source_target_pairs={{0,17},{2,19},{4,21},{6,23},{8,25},{10,27},{12,29},{14,31},{16,0},... | collective-permute-start | bytes 1597448 | tf_op jit(solution)/shard_map/ppermute | solution.py:285
  158.7 1.1 collective-permute-start.19
  159.8 0.1 abs_reduce_fusion.2
  159.9 0.2 convert_convert_fusion.1
  160.2 19.9 %all-gather.8 = s16[1792,1024]{1,0:T(8,128)(2,1)S(1)} all-gather(s16[224,1024]{1,0:T(8,128)(2,1)S(1)} %pad_add_fusion.1), channel_id=3, replica_groups=mesh['y'=4,'core'=2,'xl'=2,'z'=8,'xh'=2] {'y','core'}, dimensions={0}, use_global_device_ids=true | all-gather | bytes 4128768 | tf_op jit(solution)/shard_map/all_gather | solution.py:279
  180.2 0.3 mul.219.scale_ref
  180.4 1.2 collective-permute-done.20.e3
  181.6 3.7 %collective-permute-done.18.e1 = s16[1040,256]{1,0:T(8,128)(2,1)S(1)} collective-permute-done((s16[1040,256]{1,0:T(8,128)(2,1)S(1)}, s16[1040,256]{1,0:T(8,128)(2,1)S(1)}, u32[]{:S(2)}, u32[]{:S(2)}) %collective-permute-start.18) | collective-permute-done | bytes 532512 | tf_op jit(solution)/shard_map/ppermute | solution.py:285
  185.3 15.1 %apply_update.1 = bf16[1664,1024]{1,0:T(8,128)(2,1)} custom-call(s32[2]{0:T(128)S(1)} %pad_add_fusion.2.scalars, s16[4,2,224,1024]{3,2,1,0:T(8,128)(2,1)S(1)} %bitcast.37, f32[4,2,208,1]{3,2,1,0:T(8,128)S(1)} %mul.219.scale_ref, s16[1040,256]{1,0:T(8,128)(2,1)S(1)} %fusion.3.e0, s16[1040,256]{1,0:T(8,128)(2,1)S(1)} %collective-permute-done.18.e1, ...), custom_call_target="tpu_custom_call" | custom-call | flops 10468982784 | bytes 12320768 | tf_op jit(solution)/shard_map/apply_update/pallas_call | solution.py:177
  (68 shorter events, 1.5 us)
Async XLA Ops:
  6.5 0.9 copy-start
  6.5 17.9 %copy-start.6 = (bf16[512,1664]{1,0:T(8,128)(2,1)S(1)}, bf16[512,1664]{1,0:T(8,128)(2,1)}, u32[]{:S(2)}) copy-start(bf16[512,1664]{1,0:T(8,128)(2,1)} %src_ref.1) | copy-start | bytes 5111812
  6.5 144.1 %all-gather.6.cloned.1.call-start = ((), (), s32[]{:S(2)}) async-start(), calls=%async_computation | async-start | bytes 4259840 | tf_op jit(solution)/shard_map/all_gather | solution.py:227
  13.7 17.1 %collective-permute-start = (bf16[128,1024]{1,0:T(8,128)(2,1)}, bf16[128,1024]{1,0:T(8,128)(2,1)}, u32[]{:S(2)}, u32[]{:S(2)}) collective-permute-start(bf16[128,1024]{1,0:T(8,128)(2,1)} %get-tuple-element.35), channel_id=1, source_target_pairs={{0,16},{2,18},{4,20},{6,22},{8,24},{10,26},{12,28},{14,30},{1,17},... | collective-permute-start | bytes 786440 | tf_op jit(solution)/shard_map/ppermute | solution.py:65
  17.8 14.4 %collective-permute-start.1 = (bf16[128,1024]{1,0:T(8,128)(2,1)}, bf16[128,1024]{1,0:T(8,128)(2,1)}, u32[]{:S(2)}, u32[]{:S(2)}) collective-permute-start(bf16[128,1024]{1,0:T(8,128)(2,1)} %get-tuple-element.36), channel_id=1, source_target_pairs={{0,1},{2,3},{4,5},{6,7},{8,9},{10,11},{12,13},{14,15},{1,0},{3,2},... | collective-permute-start | bytes 786440 | tf_op jit(solution)/shard_map/ppermute | solution.py:65
  22.4 9.7 %collective-permute-start.2 = (bf16[128,1024]{1,0:T(8,128)(2,1)}, bf16[128,1024]{1,0:T(8,128)(2,1)}, u32[]{:S(2)}, u32[]{:S(2)}) collective-permute-start(bf16[128,1024]{1,0:T(8,128)(2,1)} %get-tuple-element.37), channel_id=1, source_target_pairs={{0,17},{2,19},{4,21},{6,23},{8,25},{10,27},{12,29},{14,31},{1,16},... | collective-permute-start | bytes 786440 | tf_op jit(solution)/shard_map/ppermute | solution.py:65
  25.9 6.2 %copy-start.8 = (bf16[128,1024]{1,0:T(8,128)(2,1)S(1)}, bf16[128,1024]{1,0:T(8,128)(2,1)}, u32[]{:S(2)}) copy-start(bf16[128,1024]{1,0:T(8,128)(2,1)} %get-tuple-element.34) | copy-start | bytes 786436
  25.9 36.2 %collective-permute-start.5 = (bf16[512,832]{0,1:T(8,128)(2,1)S(1)}, bf16[512,832]{0,1:T(8,128)(2,1)}, u32[]{:S(2)}, u32[]{:S(2)}) collective-permute-start(bf16[512,832]{0,1:T(8,128)(2,1)S(1)} %constant_dynamic-slice_fusion.1), channel_id=1, source_target_pairs={{0,32},{32,0},{1,33},{33,1},{2,34},{34,2},{3,35},{35,3},{4,36},{36... | collective-permute-start | bytes 2555912 | tf_op jit(solution)/shard_map/ppermute | solution.py:24
  33.2 15.1 %collective-permute-start.6 = (bf16[1024,256]{1,0:T(8,128)(2,1)}, bf16[1024,256]{1,0:T(8,128)(2,1)S(1)}, u32[]{:S(2)}, u32[]{:S(2)}) collective-permute-start(bf16[1024,256]{1,0:T(8,128)(2,1)} %get-tuple-element.46), channel_id=1, source_target_pairs={{0,16},{2,18},{4,20},{6,22},{8,24},{10,26},{12,28},{14,30},{1,17},... | collective-permute-start | bytes 1572872 | tf_op jit(solution)/shard_map/ppermute | solution.py:65
  34.5 25.5 %collective-permute-start.7 = (bf16[1024,256]{1,0:T(8,128)(2,1)}, bf16[1024,256]{1,0:T(8,128)(2,1)S(1)}, u32[]{:S(2)}, u32[]{:S(2)}) collective-permute-start(bf16[1024,256]{1,0:T(8,128)(2,1)} %get-tuple-element.47), channel_id=1, source_target_pairs={{0,1},{2,3},{4,5},{6,7},{8,9},{10,11},{12,13},{14,15},{1,0},{3,2},... | collective-permute-start | bytes 1572872 | tf_op jit(solution)/shard_map/ppermute | solution.py:65
  39.8 20.2 %collective-permute-start.8 = (bf16[1024,256]{1,0:T(8,128)(2,1)}, bf16[1024,256]{1,0:T(8,128)(2,1)S(1)}, u32[]{:S(2)}, u32[]{:S(2)}) collective-permute-start(bf16[1024,256]{1,0:T(8,128)(2,1)} %get-tuple-element.48), channel_id=1, source_target_pairs={{0,17},{2,19},{4,21},{6,23},{8,25},{10,27},{12,29},{14,31},{1,16},... | collective-permute-start | bytes 1572872 | tf_op jit(solution)/shard_map/ppermute | solution.py:65
  41.2 23.0 %collective-permute-start.4 = (bf16[128,1024]{1,0:T(8,128)(2,1)S(1)}, bf16[128,1024]{1,0:T(8,128)(2,1)S(1)}, u32[]{:S(2)}, u32[]{:S(2)}) collective-permute-start(bf16[128,1024]{1,0:T(8,128)(2,1)S(1)} %select_select_fusion.4), channel_id=1, source_target_pairs={{0,10},{2,12},{4,14},{6,0},{8,2},{10,4},{12,6},{14,8},{1,11},{3,13... | collective-permute-start | bytes 786440 | tf_op jit(solution)/shard_map/ppermute | solution.py:24
  48.3 19.1 %collective-permute-start.3 = (bf16[128,1024]{1,0:T(8,128)(2,1)S(1)}, bf16[128,1024]{1,0:T(8,128)(2,1)S(1)}, u32[]{:S(2)}, u32[]{:S(2)}) collective-permute-start(bf16[128,1024]{1,0:T(8,128)(2,1)S(1)} %select_select_fusion.4), channel_id=1, source_target_pairs={{0,6},{2,8},{4,10},{6,12},{8,14},{10,0},{12,2},{14,4},{1,7},{3,9},... | collective-permute-start | bytes 786440 | tf_op jit(solution)/shard_map/ppermute | solution.py:24
  64.3 3.2 %copy-start.10 = (bf16[1024,832]{0,1:T(8,128)(2,1)}, bf16[1024,832]{0,1:T(8,128)(2,1)S(1)}, u32[]{:S(2)}) copy-start(bf16[1024,832]{0,1:T(8,128)(2,1)S(1)} %slice_dynamic-update-slice_fusion) | copy-start | bytes 5111812
  67.5 15.0 %collective-permute-start.12 = (bf16[128,1024]{1,0:T(8,128)(2,1)S(1)}, bf16[128,1024]{1,0:T(8,128)(2,1)S(1)}, u32[]{:S(2)}, u32[]{:S(2)}) collective-permute-start(bf16[128,1024]{1,0:T(8,128)(2,1)S(1)} %select_select_fusion.3), channel_id=1, source_target_pairs={{0,14},{2,0},{4,2},{6,4},{8,6},{10,8},{12,10},{14,12},{1,15},{3,1}... | collective-permute-start | bytes 786440 | tf_op jit(solution)/shard_map/ppermute | solution.py:24
  71.6 22.4 %collective-permute-start.11 = (bf16[128,1024]{1,0:T(8,128)(2,1)S(1)}, bf16[128,1024]{1,0:T(8,128)(2,1)S(1)}, u32[]{:S(2)}, u32[]{:S(2)}) collective-permute-start(bf16[128,1024]{1,0:T(8,128)(2,1)S(1)} %select_select_fusion.3), channel_id=1, source_target_pairs={{0,2},{2,4},{4,6},{6,8},{8,10},{10,12},{12,14},{14,0},{1,3},{3,5},... | collective-permute-start | bytes 786440 | tf_op jit(solution)/shard_map/ppermute | solution.py:24
  71.8 43.8 %collective-permute-start.10 = (bf16[1024,256]{1,0:T(8,128)(2,1)}, bf16[1024,256]{1,0:T(8,128)(2,1)S(1)}, u32[]{:S(2)}, u32[]{:S(2)}) collective-permute-start(bf16[1024,256]{1,0:T(8,128)(2,1)} %select_select_fusion.2), channel_id=1, source_target_pairs={{0,10},{2,12},{4,14},{6,0},{8,2},{10,4},{12,6},{14,8},{1,11},{3,13... | collective-permute-start | bytes 1572872 | tf_op jit(solution)/shard_map/ppermute | solution.py:24
  74.7 46.8 %collective-permute-start.9 = (bf16[1024,256]{1,0:T(8,128)(2,1)}, bf16[1024,256]{1,0:T(8,128)(2,1)S(1)}, u32[]{:S(2)}, u32[]{:S(2)}) collective-permute-start(bf16[1024,256]{1,0:T(8,128)(2,1)} %select_select_fusion.2), channel_id=1, source_target_pairs={{0,6},{2,8},{4,10},{6,12},{8,14},{10,0},{12,2},{14,4},{1,7},{3,9},... | collective-permute-start | bytes 1572872 | tf_op jit(solution)/shard_map/ppermute | solution.py:24
  114.4 11.8 %copy-start.4 = (f32[832,1024]{1,0:T(8,128)}, f32[832,1024]{1,0:T(8,128)S(1)}, u32[]{:S(2)}) copy-start(f32[832,1024]{1,0:T(8,128)S(1)} %fusion.1) | copy-start | bytes 10223620
  123.7 25.2 %collective-permute-start.17 = (bf16[1024,256]{1,0:T(8,128)(2,1)}, bf16[1024,256]{1,0:T(8,128)(2,1)}, u32[]{:S(2)}, u32[]{:S(2)}) collective-permute-start(bf16[1024,256]{1,0:T(8,128)(2,1)} %select_select_fusion.1), channel_id=1, source_target_pairs={{0,14},{2,0},{4,2},{6,4},{8,6},{10,8},{12,10},{14,12},{1,15},{3,1}... | collective-permute-start | bytes 1572872 | tf_op jit(solution)/shard_map/ppermute | solution.py:24
  125.2 23.6 %collective-permute-start.16 = (bf16[1024,256]{1,0:T(8,128)(2,1)}, bf16[1024,256]{1,0:T(8,128)(2,1)}, u32[]{:S(2)}, u32[]{:S(2)}) collective-permute-start(bf16[1024,256]{1,0:T(8,128)(2,1)} %select_select_fusion.1), channel_id=1, source_target_pairs={{0,2},{2,4},{4,6},{6,8},{8,10},{10,12},{12,14},{14,0},{1,3},{3,5},... | collective-permute-start | bytes 1572872 | tf_op jit(solution)/shard_map/ppermute | solution.py:24
  126.6 3.5 %copy-start.7 = (s32[1024,1024]{1,0:T(8,128)S(1)}, s32[1024,1024]{1,0:T(8,128)}, u32[]{:S(2)}) copy-start(s32[1024,1024]{1,0:T(8,128)} %param.9) | copy-start | bytes 12582916
  126.8 3.1 %copy-start.9 = (s32[8,1024]{1,0:T(8,128)S(1)}, s32[8,1024]{1,0:T(8,128)}, u32[]{:S(2)}) copy-start(s32[8,1024]{1,0:T(8,128)} %param.10) | copy-start | bytes 98308
  126.8 3.1 %copy-start.11 = (f32[16]{0:T(128)S(1)}, f32[16]{0:T(128)}, u32[]{:S(2)}) copy-start(f32[16]{0:T(128)} %param.11) | copy-start | bytes 196
  126.9 13.5 %collective-permute-start.13 = (s16[224,1024]{1,0:T(8,128)(2,1)S(1)}, s16[224,1024]{1,0:T(8,128)(2,1)S(1)}, u32[]{:S(2)}, u32[]{:S(2)}) collective-permute-start(s16[224,1024]{1,0:T(8,128)(2,1)S(1)} %get-tuple-element.71), channel_id=1, source_target_pairs={{0,64},{64,128},{128,192},{192,0},{1,65},{65,129},{129,193},{193,1... | collective-permute-start | bytes 1376264 | tf_op jit(solution)/shard_map/ppermute | solution.py:24
  127.4 14.9 %collective-permute-start.15 = (s16[224,1024]{1,0:T(8,128)(2,1)S(1)}, s16[224,1024]{1,0:T(8,128)(2,1)S(1)}, u32[]{:S(2)}, u32[]{:S(2)}) collective-permute-start(s16[224,1024]{1,0:T(8,128)(2,1)S(1)} %get-tuple-element.72), channel_id=1, source_target_pairs={{0,128},{64,192},{128,0},{192,64},{1,129},{65,193},{129,1},{193,65... | collective-permute-start | bytes 1376264 | tf_op jit(solution)/shard_map/ppermute | solution.py:24
  129.9 17.3 %collective-permute-start.14 = (s16[224,1024]{1,0:T(8,128)(2,1)S(1)}, s16[224,1024]{1,0:T(8,128)(2,1)S(1)}, u32[]{:S(2)}, u32[]{:S(2)}) collective-permute-start(s16[224,1024]{1,0:T(8,128)(2,1)S(1)} %get-tuple-element.73), channel_id=1, source_target_pairs={{0,192},{64,0},{128,64},{192,128},{1,193},{65,1},{129,65},{193,129... | collective-permute-start | bytes 1376264 | tf_op jit(solution)/shard_map/ppermute | solution.py:24
  130.1 2.0 copy-start.5
  150.6 2.2 %copy-start.2 = (f32[1024,1024]{1,0:T(8,128)S(1)}, f32[1024,1024]{1,0:T(8,128)}, u32[]{:S(2)}) copy-start(f32[1024,1024]{1,0:T(8,128)} %all-gather.6.cloned.1.call-done.inv_ref) | copy-start | bytes 12582916
  155.7 25.9 %collective-permute-start.20 = (s16[1040,256]{1,0:T(8,128)(2,1)S(1)}, s16[1040,256]{1,0:T(8,128)(2,1)S(1)}, u32[]{:S(2)}, u32[]{:S(2)}) collective-permute-start(s16[1040,256]{1,0:T(8,128)(2,1)S(1)} %fusion.3.e0), channel_id=1, source_target_pairs={{0,17},{2,19},{4,21},{6,23},{8,25},{10,27},{12,29},{14,31},{16,0},... | collective-permute-start | bytes 1597448 | tf_op jit(solution)/shard_map/ppermute | solution.py:285
  158.7 23.0 %collective-permute-start.19 = (s16[1040,256]{1,0:T(8,128)(2,1)S(1)}, s16[1040,256]{1,0:T(8,128)(2,1)S(1)}, u32[]{:S(2)}, u32[]{:S(2)}) collective-permute-start(s16[1040,256]{1,0:T(8,128)(2,1)S(1)} %fusion.3.e0), channel_id=1, source_target_pairs={{0,1},{2,3},{4,5},{6,7},{8,9},{10,11},{12,13},{14,15},{16,17},{18,... | collective-permute-start | bytes 1597448 | tf_op jit(solution)/shard_map/ppermute | solution.py:285
  159.8 25.6 %collective-permute-start.18 = (s16[1040,256]{1,0:T(8,128)(2,1)S(1)}, s16[1040,256]{1,0:T(8,128)(2,1)S(1)}, u32[]{:S(2)}, u32[]{:S(2)}) collective-permute-start(s16[1040,256]{1,0:T(8,128)(2,1)S(1)} %fusion.3.e0), channel_id=1, source_target_pairs={{0,16},{2,18},{4,20},{6,22},{8,24},{10,26},{12,28},{14,30},{16,1},... | collective-permute-start | bytes 1597448 | tf_op jit(solution)/shard_map/ppermute | solution.py:285
  160.1 25.2 %copy-start.3 = (bf16[1664,1024]{1,0:T(8,128)(2,1)S(1)}, bf16[1664,1024]{1,0:T(8,128)(2,1)}, u32[]{:S(2)}) copy-start(bf16[1664,1024]{1,0:T(8,128)(2,1)} %fusion.base_ref) | copy-start | bytes 10223620
  185.3 15.1 %copy-start.1 = (f32[32,1024]{1,0:T(8,128)S(1)}, f32[32,1024]{1,0:T(8,128)}, u32[]{:S(2)}) copy-start(f32[32,1024]{1,0:T(8,128)} %param.12) | copy-start | bytes 393220
Sparse Core Ops, SparseCore 0:
  10.1 96.5 all-gather.5

commit v4 on v3

--- a/solution.py
+++ b/solution.py
@@ -82,6 +82,19 @@
     from_below = (distance == 1) | (distance == 4) | (distance == 6)
     from_above = (distance == 7) | (distance == 2)
     return jnp.where(from_below, up, jnp.where(from_above, down, piece))
+
+
+def spread_from(z0, piece, z, z_owner):
+    at = lambda d: (z0 + d) % 8
+    send = lambda value, pairs: lax.ppermute(value, "z", [(at(a), at(b)) for a, b in pairs])
+    place = (z - z0) % 8
+    got = send(piece, [(0, 1), (1, 0)])
+    piece = jnp.where((place <= 1) & (z_owner != z), got, piece)
+    got = send(piece, [(0, 6), (1, 3)])
+    piece = jnp.where((place == 6) | (place == 3), got, piece)
+    got = send(piece, [(0, 7), (1, 2), (6, 5), (3, 4)])
+    odd = (place == 7) | (place == 2) | (place == 5) | (place == 4)
+    return jnp.where(odd, got, piece)
 
 
 def quantize(values):
@@ -245,11 +258,15 @@
     lanes = lambda v: jnp.repeat(v, UNIT)[None, :]
     sublanes = lambda v: jnp.repeat(v, UNIT)[:, None]
     x_piece = scatter_x(x_pieces, x, lanes(from_low))
-    x_piece, w_pieces = lax.optimization_barrier((x_piece, w_pieces))
     w_piece = scatter_x(w_pieces, x, sublanes(from_low))
-    x_piece, x_rows = reach_far(x_piece, lanes(distance), (x_rows,))
-    x_piece, w_piece = lax.optimization_barrier((x_piece, w_piece))
-    x_piece = reach_near(x_piece, lanes(distance))
+    x_piece = lax.switch(
+        (first_unit // tile_units // 2) % 8,
+        [functools.partial(spread_from, z0) for z0 in range(8)],
+        x_piece,
+        z,
+        lanes(z_owner),
+    )
+    x_piece, w_piece, x_rows = lax.optimization_barrier((x_piece, w_piece, x_rows))
 
     x_block = lax.all_gather(
         x_piece.astype(jnp.float16), ("xh", "xl", "core"), axis=0, tiled=True

time: 209 us -> 267 us (1.28)
  starting transfers between devices: 46.4 us -> 114 us
  waiting for transfers between devices: 54.6 us -> 41.8 us
  local copies, waits for them, and re-layouts: 7.62 us -> 11.6 us
    ppermute x12 -> x8, starting transfers between devices: 23.7 us -> 62.6 us  [ring(): lax.ppermute(value, axis, [(i, (i + shift) % size) for i in range(size)])]
    ppermute x3, starting transfers between devices: 4.07 us -> 25.8 us  [local(): errors.append(lax.ppermute(error, PLANE, plane_pairs(range(4), shift)))]
    ppermute x0 -> x3, waiting for transfers between devices: none -> 18.8 us  [spread_from(): lax.ppermute(value, 'z', [(at(a), at(b)) for a, b in pairs])]
    ppermute x12 -> x8, waiting for transfers between devices: 40.2 us -> 22.9 us  [ring(): lax.ppermute(value, axis, [(i, (i + shift) % size) for i in range(size)])]
    ppermute x6, waiting for transfers between devices: 9.47 us -> 0.02 us  [scatter_x(): lax.ppermute(piece, PLANE, plane_pairs((0, 2), shift))]
    ppermute x0 -> x3, starting transfers between devices: none -> 6.37 us  [spread_from(): lax.ppermute(value, 'z', [(at(a), at(b)) for a, b in pairs])]
    ppermute x3, waiting for transfers between devices: 4.87 us -> 0.01 us  [local(): errors.append(lax.ppermute(error, PLANE, plane_pairs(range(4), shift)))]
    unnamed x31 -> x35, local copies, waits for them, and re-layouts: 4.55 us -> 5.46 us
  transfers between devices with their start and end apart: 22 -> 21, of which waited for: 12 -> 6; matrix products, arithmetic and copies ran while one was open for 11% -> 9% of each run, Pallas kernels for 4% -> 3%
where the time goes in v4:
time: 267 us; the launch traced here: 264 us
  starting transfers between devices  114 us (43%)
  waiting for transfers between devices  41.8 us (16%)
  blocking collectives  37.4 us (14%)
  Pallas kernels  27 us (10%)
  other arithmetic  15.6 us (6%)
  between operations  14.6 us (5%)
  local copies, waits for them, and re-layouts  11.6 us (4%)
    ppermute x8, starting transfers between devices, ring(): lax.ppermute(value, axis, [(i, (i + shift) % size) for i in range(size)])  62.6 us
    ppermute x3, starting transfers between devices, local(): errors.append(lax.ppermute(error, PLANE, plane_pairs(range(4), shift)))  25.8 us
    ppermute x8, waiting for transfers between devices, ring(): lax.ppermute(value, axis, [(i, (i + shift) % size) for i in range(size)])  22.9 us
    all_gather x1, blocking collectives, local(): panel = lax.all_gather(quantize(total), ('y', 'core'), axis=0)  20.4 us
    ppermute x6, starting transfers between devices, scatter_x(): lax.ppermute(piece, PLANE, plane_pairs((0, 2), shift))  19.5 us
    ppermute x3, waiting for transfers between devices, spread_from(): lax.ppermute(value, 'z', [(at(a), at(b)) for a, b in pairs])  18.8 us
    all_gather x1, blocking collectives, local(): lax.all_gather(x_piece.astype(jnp.float16), ('xh', 'xl', 'core'), axis=0,...  16.9 us
    pallas_call x1, Pallas kernels, apply_update(): pl.pallas_call(update_kernel, grid_spec=pltpu.PrefetchScalarGridSpec(num_...  15.2 us
  transfers between devices with their start and end apart: 21, of which 6 were waited for; matrix products, arithmetic and copies ran while one was open for 9% of the time, Pallas kernels for 3%

profile of v4, /device:TPU:24, one launch (start us, length us, event | category | flops | bytes accessed | tf_op | source)
XLA Modules:
  0.0 264.3 jit_solution(7072897849664994314)
XLA Ops:
  6.5 0.9 copy-done
  7.4 0.6 constant_dynamic-slice_fusion.2
  8.8 0.6 pad_add_fusion.3.scalars
  9.4 4.4 %pick_columns.1 = (bf16[128,1024]{1,0:T(8,128)(2,1)}, bf16[128,1024]{1,0:T(8,128)(2,1)}, bf16[128,1024]{1,0:T(8,128)(2,1)}, bf16[128,1024]{1,0:T(8,128)(2,1)}) custom-call(s32[9]{0:T(128)} %pad_add_fusion.3.scalars, bf16[512,1664]{1,0:T(8,128)(2,1)} %src_ref.1), custom_call_target="tpu_custom_call" | custom-call | tf_op jit(solution)/shard_map/pick_columns/pallas_call | solution.py:48
  13.8 3.4 %collective-permute-start.24 = (bf16[128,1024]{1,0:T(8,128)(2,1)}, bf16[128,1024]{1,0:T(8,128)(2,1)S(1)}, u32[]{:S(2)}, u32[]{:S(2)}) collective-permute-start(bf16[128,1024]{1,0:T(8,128)(2,1)} %get-tuple-element.109), channel_id=1, source_target_pairs={{0,16},{2,18},{4,20},{6,22},{8,24},{10,26},{12,28},{14,30},{1,17},... | collective-permute-start | bytes 786440 | tf_op jit(solution)/shard_map/ppermute | solution.py:65
  17.2 4.6 %collective-permute-start.25 = (bf16[128,1024]{1,0:T(8,128)(2,1)}, bf16[128,1024]{1,0:T(8,128)(2,1)S(1)}, u32[]{:S(2)}, u32[]{:S(2)}) collective-permute-start(bf16[128,1024]{1,0:T(8,128)(2,1)} %get-tuple-element.110), channel_id=1, source_target_pairs={{0,1},{2,3},{4,5},{6,7},{8,9},{10,11},{12,13},{14,15},{1,0},{3,2},... | collective-permute-start | bytes 786440 | tf_op jit(solution)/shard_map/ppermute | solution.py:65
  21.8 1.3 collective-permute-start.26
  23.1 2.3 copy.15
  25.4 2.2 constant_dynamic-slice_fusion.1
  27.6 10.3 %collective-permute-start.30 = (bf16[512,832]{0,1:T(8,128)(2,1)}, bf16[512,832]{0,1:T(8,128)(2,1)}, u32[]{:S(2)}, u32[]{:S(2)}) collective-permute-start(bf16[512,832]{0,1:T(8,128)(2,1)} %constant_dynamic-slice_fusion.1), channel_id=1, source_target_pairs={{0,32},{32,0},{1,33},{33,1},{2,34},{34,2},{3,35},{35,3},{4,36},{36... | collective-permute-start | bytes 2555912 | tf_op jit(solution)/shard_map/ppermute | solution.py:24
  37.9 4.7 %pick_rows.1 = (bf16[1024,256]{1,0:T(8,128)(2,1)}, bf16[1024,256]{1,0:T(8,128)(2,1)}, bf16[1024,256]{1,0:T(8,128)(2,1)}, bf16[1024,256]{1,0:T(8,128)(2,1)}) custom-call(s32[9]{0:T(128)} %pad_add_fusion.3.scalars, bf16[1664,1024]{1,0:T(8,128)(2,1)} %src_ref.2), custom_call_target="tpu_custom_call" | custom-call | tf_op jit(solution)/shard_map/pick_rows/pallas_call | solution.py:48
  42.6 3.4 %collective-permute-start.27 = (bf16[1024,256]{1,0:T(8,128)(2,1)}, bf16[1024,256]{1,0:T(8,128)(2,1)S(1)}, u32[]{:S(2)}, u32[]{:S(2)}) collective-permute-start(bf16[1024,256]{1,0:T(8,128)(2,1)} %get-tuple-element.113), channel_id=1, source_target_pairs={{0,16},{2,18},{4,20},{6,22},{8,24},{10,26},{12,28},{14,30},{1,17},... | collective-permute-start | bytes 1572872 | tf_op jit(solution)/shard_map/ppermute | solution.py:65
  46.1 0.1 broadcast_bitcast_fusion.4
  46.3 4.6 %collective-permute-start.28 = (bf16[1024,256]{1,0:T(8,128)(2,1)}, bf16[1024,256]{1,0:T(8,128)(2,1)}, u32[]{:S(2)}, u32[]{:S(2)}) collective-permute-start(bf16[1024,256]{1,0:T(8,128)(2,1)} %get-tuple-element.114), channel_id=1, source_target_pairs={{0,1},{2,3},{4,5},{6,7},{8,9},{10,11},{12,13},{14,15},{1,0},{3,2},... | collective-permute-start | bytes 1572872 | tf_op jit(solution)/shard_map/ppermute | solution.py:65
  50.9 2.1 collective-permute-start.29
  53.3 25.4 %conditional.1 = (bf16[128,1024]{1,0:T(8,128)(2,1)S(1)}) conditional(s32[]{:T(128)} %clamp.4, (s32[]{:T(128)}, s32[1,1024]{1,0:T(1,128)S(1)}, bf16[128,1024]{1,0:T(8,128)(2,1)S(1)}) %tuple.63, (s32[]{:T(128)}, s32[1,1024]{1,0:T(1,128)S(1)}, bf16[128,1024]{1,0:T(8,128)(2,1)S(1)}) %tuple.64, (s32[]{:T(128)}, ...), branch_computations={%region_0.1_spmd, %region_1.2_spmd, %region_2.3_spmd, %region_3.4_... | conditional | flops 395287 | bytes 5511499 | solution.py:262
  53.3 3.8 %collective-permute-start = (bf16[128,1024]{1,0:T(8,128)(2,1)S(1)}, bf16[128,1024]{1,0:T(8,128)(2,1)S(1)}, u32[]{:S(2)}, u32[]{:S(2)}) collective-permute-start(bf16[128,1024]{1,0:T(8,128)(2,1)S(1)} %get-tuple-element.58), channel_id=1, source_target_pairs={{0,2},{2,0},{1,3},{3,1},{16,18},{18,16},{17,19},{19,17},{32,34},{3... | collective-permute-start | bytes 786440 | tf_op jit(solution)/shard_map/cond/branch_0_fun/ppermute | solution.py:89
  57.1 6.2 %collective-permute-done = bf16[128,1024]{1,0:T(8,128)(2,1)S(1)} collective-permute-done((bf16[128,1024]{1,0:T(8,128)(2,1)S(1)}, bf16[128,1024]{1,0:T(8,128)(2,1)S(1)}, u32[]{:S(2)}, u32[]{:S(2)}) %collective-permute-start) | collective-permute-done | bytes 262176 | tf_op jit(solution)/shard_map/cond/branch_0_fun/ppermute | solution.py:89
  63.4 1.3 collective-permute-start.1
  64.7 6.8 %collective-permute-done.1 = bf16[128,1024]{1,0:T(8,128)(2,1)S(1)} collective-permute-done((bf16[128,1024]{1,0:T(8,128)(2,1)S(1)}, bf16[128,1024]{1,0:T(8,128)(2,1)S(1)}, u32[]{:S(2)}, u32[]{:S(2)}) %collective-permute-start.1) | collective-permute-done | bytes 262176 | tf_op jit(solution)/shard_map/cond/branch_0_fun/ppermute | solution.py:89
  71.5 1.3 collective-permute-start.2
  72.9 5.8 %collective-permute-done.2 = bf16[128,1024]{1,0:T(8,128)(2,1)S(1)} collective-permute-done((bf16[128,1024]{1,0:T(8,128)(2,1)S(1)}, bf16[128,1024]{1,0:T(8,128)(2,1)S(1)}, u32[]{:S(2)}, u32[]{:S(2)}) %collective-permute-start.2) | collective-permute-done | bytes 262176 | tf_op jit(solution)/shard_map/cond/branch_0_fun/ppermute | solution.py:89
  78.8 1.5 select_select_fusion.2
  80.3 0.1 copy-done.7
  80.4 1.6 broadcast_select_fusion.24
  82.1 0.1 slice_dynamic-update-slice_fusion.5
  82.6 7.2 %collective-permute-start.32 = (bf16[1024,256]{1,0:T(8,128)(2,1)S(1)}, bf16[1024,256]{1,0:T(8,128)(2,1)S(1)}, u32[]{:S(2)}, u32[]{:S(2)}) collective-permute-start(bf16[1024,256]{1,0:T(8,128)(2,1)S(1)} %select_select_fusion.2), channel_id=1, source_target_pairs={{0,10},{2,12},{4,14},{6,0},{8,2},{10,4},{12,6},{14,8},{1,11},{3,13... | collective-permute-start | bytes 1572872 | tf_op jit(solution)/shard_map/ppermute | solution.py:24
  89.9 16.9 %all-gather.7 = f16[1024,1024]{1,0:T(8,128)(2,1)S(1)} all-gather(f16[128,1024]{1,0:T(8,128)(2,1)S(1)} %convert_element_type.102), channel_id=1, replica_groups=mesh['y'=4,'core'=2,'xl'=2,'z'=8,'xh'=2] {'xh','xl','core'}, dimensions={0}, use_global_device_ids=true | all-gather | bytes 2359296 | tf_op jit(solution)/shard_map/all_gather | solution.py:271
  106.8 1.9 fusion.1
  108.8 13.3 %collective-permute-done.32 = bf16[1024,256]{1,0:T(8,128)(2,1)S(1)} collective-permute-done((bf16[1024,256]{1,0:T(8,128)(2,1)S(1)}, bf16[1024,256]{1,0:T(8,128)(2,1)S(1)}, u32[]{:S(2)}, u32[]{:S(2)}) %collective-permute-start.32) | collective-permute-done | bytes 524320 | tf_op jit(solution)/shard_map/ppermute | solution.py:24
  122.1 4.0 %collective-permute-done.31 = bf16[1024,256]{1,0:T(8,128)(2,1)S(1)} collective-permute-done((bf16[1024,256]{1,0:T(8,128)(2,1)S(1)}, bf16[1024,256]{1,0:T(8,128)(2,1)S(1)}, u32[]{:S(2)}, u32[]{:S(2)}) %collective-permute-start.31) | collective-permute-done | bytes 524320 | tf_op jit(solution)/shard_map/ppermute | solution.py:24
  126.1 0.3 select_select_fusion.1
  126.5 8.7 %collective-permute-start.37 = (bf16[1024,256]{1,0:T(8,128)(2,1)S(1)}, bf16[1024,256]{1,0:T(8,128)(2,1)S(1)}, u32[]{:S(2)}, u32[]{:S(2)}) collective-permute-start(bf16[1024,256]{1,0:T(8,128)(2,1)S(1)} %select_select_fusion.1), channel_id=1, source_target_pairs={{0,14},{2,0},{4,2},{6,4},{8,6},{10,8},{12,10},{14,12},{1,15},{3,1}... | collective-permute-start | bytes 1572872 | tf_op jit(solution)/shard_map/ppermute | solution.py:24
  135.1 1.7 collective-permute-start.36
  136.9 0.3 abs_reduce_fusion
  137.2 0.1 reshape.270
  137.3 0.1 reshape.285
  137.4 2.3 convert_convert_fusion
  139.7 0.2 pad_add_fusion
  139.9 0.1 dynamic-slice_bitcast_fusion.2
  140.0 11.0 %collective-permute-start.33 = (s16[224,1024]{1,0:T(8,128)(2,1)S(1)}, s16[224,1024]{1,0:T(8,128)(2,1)S(1)}, u32[]{:S(2)}, u32[]{:S(2)}) collective-permute-start(s16[224,1024]{1,0:T(8,128)(2,1)S(1)} %get-tuple-element.138), channel_id=1, source_target_pairs={{0,64},{64,128},{128,192},{192,0},{1,65},{65,129},{129,193},{193,1... | collective-permute-start | bytes 1376264 | tf_op jit(solution)/shard_map/ppermute | solution.py:24
  151.1 11.8 %collective-permute-start.35 = (s16[224,1024]{1,0:T(8,128)(2,1)S(1)}, s16[224,1024]{1,0:T(8,128)(2,1)S(1)}, u32[]{:S(2)}, u32[]{:S(2)}) collective-permute-start(s16[224,1024]{1,0:T(8,128)(2,1)S(1)} %get-tuple-element.139), channel_id=1, source_target_pairs={{0,128},{64,192},{128,0},{192,64},{1,129},{65,193},{129,1},{193,65... | collective-permute-start | bytes 1376264 | tf_op jit(solution)/shard_map/ppermute | solution.py:24
  162.9 11.8 %collective-permute-start.34 = (s16[224,1024]{1,0:T(8,128)(2,1)S(1)}, s16[224,1024]{1,0:T(8,128)(2,1)S(1)}, u32[]{:S(2)}, u32[]{:S(2)}) collective-permute-start(s16[224,1024]{1,0:T(8,128)(2,1)S(1)} %get-tuple-element.140), channel_id=1, source_target_pairs={{0,192},{64,0},{128,64},{192,128},{1,193},{65,1},{129,65},{193,129... | collective-permute-start | bytes 1376264 | tf_op jit(solution)/shard_map/ppermute | solution.py:24
  174.7 0.2 select_reduce_fusion
  174.9 1.1 fusion.27
  176.0 0.9 copy-done.5
  176.9 3.3 %fusion.base_ref = bf16[1664,1024]{1,0:T(8,128)(2,1)} fusion(bf16[1664,1024]{1,0:T(8,128)(2,1)S(1)} %copy-done.5, s32[]{:T(128)S(6)} %min.14, bf16[1024,1024]{1,0:T(8,128)(2,1)S(1)} %get-tuple-element.128, pred[1664]{0:T(1024)(128)(4,1)S(1)} %fusion.13), kind=kLoop, calls=%fused_computation.34 | loop fusion | flops 1703936 | bytes 8914564 | tf_op jit(solution)/shard_map/jit(_where)/select_n | solution.py:309
  180.2 0.1 constant_dynamic-slice_fusion.q_ref
  180.4 5.5 %collective-permute-done.34 = s16[224,1024]{1,0:T(8,128)(2,1)S(1)} collective-permute-done((s16[224,1024]{1,0:T(8,128)(2,1)S(1)}, s16[224,1024]{1,0:T(8,128)(2,1)S(1)}, u32[]{:S(2)}, u32[]{:S(2)}) %collective-permute-start.34) | collective-permute-done | bytes 458784 | tf_op jit(solution)/shard_map/ppermute | solution.py:24
  185.9 1.7 fusion.5
  187.6 0.8 copy-done.9
  188.4 1.6 select_select_fusion.w_ref
  190.0 2.2 copy-done.2
  192.2 2.7 %block_error.1 = f32[1024,256]{1,0:T(8,128)S(1)} custom-call(f32[1024,1024]{1,0:T(8,128)S(1)} %copy-done.2, bf16[1024,256]{1,0:T(8,128)(2,1)S(1)} %select_select_fusion.w_ref, f32[1024,256]{1,0:T(8,128)S(1)} %constant_dynamic-slice_fusion.q_ref), custom_call_target="tpu_custom_call" | custom-call | flops 1610612736 | bytes 4194304 | tf_op jit(solution)/shard_map/block_error/pallas_call | solution.py:143
  194.9 0.1 multiply_round-nearest-even_fusion
  195.0 0.1 fusion.3.e0
  195.1 12.9 %collective-permute-start.40 = (s16[1040,256]{1,0:T(8,128)(2,1)S(1)}, s16[1040,256]{1,0:T(8,128)(2,1)S(1)}, u32[]{:S(2)}, u32[]{:S(2)}) collective-permute-start(s16[1040,256]{1,0:T(8,128)(2,1)S(1)} %fusion.3.e0), channel_id=1, source_target_pairs={{0,17},{2,19},{4,21},{6,23},{8,25},{10,27},{12,29},{14,31},{16,0},... | collective-permute-start | bytes 1597448 | tf_op jit(solution)/shard_map/ppermute | solution.py:302
  208.0 3.0 %collective-permute-start.39 = (s16[1040,256]{1,0:T(8,128)(2,1)S(1)}, s16[1040,256]{1,0:T(8,128)(2,1)S(1)}, u32[]{:S(2)}, u32[]{:S(2)}) collective-permute-start(s16[1040,256]{1,0:T(8,128)(2,1)S(1)} %fusion.3.e0), channel_id=1, source_target_pairs={{0,1},{2,3},{4,5},{6,7},{8,9},{10,11},{12,13},{14,15},{16,17},{18,... | collective-permute-start | bytes 1597448 | tf_op jit(solution)/shard_map/ppermute | solution.py:302
  211.0 10.0 %collective-permute-start.38 = (s16[1040,256]{1,0:T(8,128)(2,1)S(1)}, s16[1040,256]{1,0:T(8,128)(2,1)S(1)}, u32[]{:S(2)}, u32[]{:S(2)}) collective-permute-start(s16[1040,256]{1,0:T(8,128)(2,1)S(1)} %fusion.3.e0), channel_id=1, source_target_pairs={{0,16},{2,18},{4,20},{6,22},{8,24},{10,26},{12,28},{14,30},{16,1},... | collective-permute-start | bytes 1597448 | tf_op jit(solution)/shard_map/ppermute | solution.py:302
  221.0 0.1 abs_reduce_fusion.2
  221.2 0.2 convert_convert_fusion.1
  221.4 20.4 %all-gather.8 = s16[1792,1024]{1,0:T(8,128)(2,1)S(1)} all-gather(s16[224,1024]{1,0:T(8,128)(2,1)S(1)} %pad_add_fusion.1), channel_id=3, replica_groups=mesh['y'=4,'core'=2,'xl'=2,'z'=8,'xh'=2] {'y','core'}, dimensions={0}, use_global_device_ids=true | all-gather | bytes 4128768 | tf_op jit(solution)/shard_map/all_gather | solution.py:296
  241.9 0.3 mul.219.scale_ref
  242.2 15.2 %apply_update.1 = bf16[1664,1024]{1,0:T(8,128)(2,1)} custom-call(s32[2]{0:T(128)S(1)} %pad_add_fusion.2.scalars, s16[4,2,224,1024]{3,2,1,0:T(8,128)(2,1)S(1)} %bitcast.38, f32[4,2,208,1]{3,2,1,0:T(8,128)S(1)} %mul.219.scale_ref, s16[1040,256]{1,0:T(8,128)(2,1)S(1)} %fusion.3.e0, s16[1040,256]{1,0:T(8,128)(2,1)S(1)} %collective-permute-done.38.e1, ...), custom_call_target="tpu_custom_call" | custom-call | flops 10468982784 | bytes 12320768 | tf_op jit(solution)/shard_map/apply_update/pallas_call | solution.py:190
  (75 shorter events, 1.5 us)
Async XLA Ops:
  6.5 0.9 copy-start
  6.5 16.6 %copy-start.6 = (bf16[512,1664]{1,0:T(8,128)(2,1)S(1)}, bf16[512,1664]{1,0:T(8,128)(2,1)}, u32[]{:S(2)}) copy-start(bf16[512,1664]{1,0:T(8,128)(2,1)} %src_ref.1) | copy-start | bytes 5111812
  6.5 183.4 %all-gather.6.cloned.1.call-start = ((), (), s32[]{:S(2)}) async-start(), calls=%async_computation | async-start | bytes 4259840 | tf_op jit(solution)/shard_map/all_gather | solution.py:240
  13.8 32.6 %collective-permute-start.24 = (bf16[128,1024]{1,0:T(8,128)(2,1)}, bf16[128,1024]{1,0:T(8,128)(2,1)S(1)}, u32[]{:S(2)}, u32[]{:S(2)}) collective-permute-start(bf16[128,1024]{1,0:T(8,128)(2,1)} %get-tuple-element.109), channel_id=1, source_target_pairs={{0,16},{2,18},{4,20},{6,22},{8,24},{10,26},{12,28},{14,30},{1,17},... | collective-permute-start | bytes 786440 | tf_op jit(solution)/shard_map/ppermute | solution.py:65
  17.2 33.8 %collective-permute-start.25 = (bf16[128,1024]{1,0:T(8,128)(2,1)}, bf16[128,1024]{1,0:T(8,128)(2,1)S(1)}, u32[]{:S(2)}, u32[]{:S(2)}) collective-permute-start(bf16[128,1024]{1,0:T(8,128)(2,1)} %get-tuple-element.110), channel_id=1, source_target_pairs={{0,1},{2,3},{4,5},{6,7},{8,9},{10,11},{12,13},{14,15},{1,0},{3,2},... | collective-permute-start | bytes 786440 | tf_op jit(solution)/shard_map/ppermute | solution.py:65
  21.8 31.4 %collective-permute-start.26 = (bf16[128,1024]{1,0:T(8,128)(2,1)}, bf16[128,1024]{1,0:T(8,128)(2,1)S(1)}, u32[]{:S(2)}, u32[]{:S(2)}) collective-permute-start(bf16[128,1024]{1,0:T(8,128)(2,1)} %get-tuple-element.111), channel_id=1, source_target_pairs={{0,17},{2,19},{4,21},{6,23},{8,25},{10,27},{12,29},{14,31},{1,16},... | collective-permute-start | bytes 786440 | tf_op jit(solution)/shard_map/ppermute | solution.py:65
  27.6 25.6 %copy-start.11 = (bf16[128,1024]{1,0:T(8,128)(2,1)S(1)}, bf16[128,1024]{1,0:T(8,128)(2,1)}, u32[]{:S(2)}) copy-start(bf16[128,1024]{1,0:T(8,128)(2,1)} %get-tuple-element.108) | copy-start | bytes 786436
  27.6 52.7 %collective-permute-start.30 = (bf16[512,832]{0,1:T(8,128)(2,1)}, bf16[512,832]{0,1:T(8,128)(2,1)}, u32[]{:S(2)}, u32[]{:S(2)}) collective-permute-start(bf16[512,832]{0,1:T(8,128)(2,1)} %constant_dynamic-slice_fusion.1), channel_id=1, source_target_pairs={{0,32},{32,0},{1,33},{33,1},{2,34},{34,2},{3,35},{35,3},{4,36},{36... | collective-permute-start | bytes 2555912 | tf_op jit(solution)/shard_map/ppermute | solution.py:24
  42.6 36.1 %collective-permute-start.27 = (bf16[1024,256]{1,0:T(8,128)(2,1)}, bf16[1024,256]{1,0:T(8,128)(2,1)S(1)}, u32[]{:S(2)}, u32[]{:S(2)}) collective-permute-start(bf16[1024,256]{1,0:T(8,128)(2,1)} %get-tuple-element.113), channel_id=1, source_target_pairs={{0,16},{2,18},{4,20},{6,22},{8,24},{10,26},{12,28},{14,30},{1,17},... | collective-permute-start | bytes 1572872 | tf_op jit(solution)/shard_map/ppermute | solution.py:65
  46.3 32.5 %collective-permute-start.28 = (bf16[1024,256]{1,0:T(8,128)(2,1)}, bf16[1024,256]{1,0:T(8,128)(2,1)}, u32[]{:S(2)}, u32[]{:S(2)}) collective-permute-start(bf16[1024,256]{1,0:T(8,128)(2,1)} %get-tuple-element.114), channel_id=1, source_target_pairs={{0,1},{2,3},{4,5},{6,7},{8,9},{10,11},{12,13},{14,15},{1,0},{3,2},... | collective-permute-start | bytes 1572872 | tf_op jit(solution)/shard_map/ppermute | solution.py:65
  50.9 27.9 %collective-permute-start.29 = (bf16[1024,256]{1,0:T(8,128)(2,1)}, bf16[1024,256]{1,0:T(8,128)(2,1)}, u32[]{:S(2)}, u32[]{:S(2)}) collective-permute-start(bf16[1024,256]{1,0:T(8,128)(2,1)} %get-tuple-element.115), channel_id=1, source_target_pairs={{0,17},{2,19},{4,21},{6,23},{8,25},{10,27},{12,29},{14,31},{1,16},... | collective-permute-start | bytes 1572872 | tf_op jit(solution)/shard_map/ppermute | solution.py:65
  53.3 25.5 %copy-start.10 = (bf16[1024,256]{1,0:T(8,128)(2,1)S(1)}, bf16[1024,256]{1,0:T(8,128)(2,1)}, u32[]{:S(2)}) copy-start(bf16[1024,256]{1,0:T(8,128)(2,1)} %get-tuple-element.112) | copy-start | bytes 1572868
  53.3 10.0 %collective-permute-start = (bf16[128,1024]{1,0:T(8,128)(2,1)S(1)}, bf16[128,1024]{1,0:T(8,128)(2,1)S(1)}, u32[]{:S(2)}, u32[]{:S(2)}) collective-permute-start(bf16[128,1024]{1,0:T(8,128)(2,1)S(1)} %get-tuple-element.58), channel_id=1, source_target_pairs={{0,2},{2,0},{1,3},{3,1},{16,18},{18,16},{17,19},{19,17},{32,34},{3... | collective-permute-start | bytes 786440 | tf_op jit(solution)/shard_map/cond/branch_0_fun/ppermute | solution.py:89
  63.4 8.1 %collective-permute-start.1 = (bf16[128,1024]{1,0:T(8,128)(2,1)S(1)}, bf16[128,1024]{1,0:T(8,128)(2,1)S(1)}, u32[]{:S(2)}, u32[]{:S(2)}) collective-permute-start(bf16[128,1024]{1,0:T(8,128)(2,1)S(1)} %broadcast_select_fusion), channel_id=1, source_target_pairs={{0,12},{2,6},{1,13},{3,7},{16,28},{18,22},{17,29},{19,23},{32,44},... | collective-permute-start | bytes 786440 | tf_op jit(solution)/shard_map/cond/branch_0_fun/ppermute | solution.py:89
  71.5 7.2 %collective-permute-start.2 = (bf16[128,1024]{1,0:T(8,128)(2,1)S(1)}, bf16[128,1024]{1,0:T(8,128)(2,1)S(1)}, u32[]{:S(2)}, u32[]{:S(2)}) collective-permute-start(bf16[128,1024]{1,0:T(8,128)(2,1)S(1)} %broadcast_select_fusion.1), channel_id=1, source_target_pairs={{0,14},{2,4},{12,10},{6,8},{1,15},{3,5},{13,11},{7,9},{16,30},{18,... | collective-permute-start | bytes 786440 | tf_op jit(solution)/shard_map/cond/branch_0_fun/ppermute | solution.py:89
  78.8 1.7 copy-start.7
  82.6 39.5 %collective-permute-start.32 = (bf16[1024,256]{1,0:T(8,128)(2,1)S(1)}, bf16[1024,256]{1,0:T(8,128)(2,1)S(1)}, u32[]{:S(2)}, u32[]{:S(2)}) collective-permute-start(bf16[1024,256]{1,0:T(8,128)(2,1)S(1)} %select_select_fusion.2), channel_id=1, source_target_pairs={{0,10},{2,12},{4,14},{6,0},{8,2},{10,4},{12,6},{14,8},{1,11},{3,13... | collective-permute-start | bytes 1572872 | tf_op jit(solution)/shard_map/ppermute | solution.py:24
  89.8 36.3 %collective-permute-start.31 = (bf16[1024,256]{1,0:T(8,128)(2,1)S(1)}, bf16[1024,256]{1,0:T(8,128)(2,1)S(1)}, u32[]{:S(2)}, u32[]{:S(2)}) collective-permute-start(bf16[1024,256]{1,0:T(8,128)(2,1)S(1)} %select_select_fusion.2), channel_id=1, source_target_pairs={{0,6},{2,8},{4,10},{6,12},{8,14},{10,0},{12,2},{14,4},{1,7},{3,9},... | collective-permute-start | bytes 1572872 | tf_op jit(solution)/shard_map/ppermute | solution.py:24
  108.8 28.4 %copy-start.4 = (f32[832,1024]{1,0:T(8,128)}, f32[832,1024]{1,0:T(8,128)S(1)}, u32[]{:S(2)}) copy-start(f32[832,1024]{1,0:T(8,128)S(1)} %fusion.1) | copy-start | bytes 10223620
  126.5 61.1 %collective-permute-start.37 = (bf16[1024,256]{1,0:T(8,128)(2,1)S(1)}, bf16[1024,256]{1,0:T(8,128)(2,1)S(1)}, u32[]{:S(2)}, u32[]{:S(2)}) collective-permute-start(bf16[1024,256]{1,0:T(8,128)(2,1)S(1)} %select_select_fusion.1), channel_id=1, source_target_pairs={{0,14},{2,0},{4,2},{6,4},{8,6},{10,8},{12,10},{14,12},{1,15},{3,1}... | collective-permute-start | bytes 1572872 | tf_op jit(solution)/shard_map/ppermute | solution.py:24
  135.1 52.5 %collective-permute-start.36 = (bf16[1024,256]{1,0:T(8,128)(2,1)S(1)}, bf16[1024,256]{1,0:T(8,128)(2,1)}, u32[]{:S(2)}, u32[]{:S(2)}) collective-permute-start(bf16[1024,256]{1,0:T(8,128)(2,1)S(1)} %select_select_fusion.1), channel_id=1, source_target_pairs={{0,2},{2,4},{4,6},{6,8},{8,10},{10,12},{12,14},{14,0},{1,3},{3,5},... | collective-permute-start | bytes 1572872 | tf_op jit(solution)/shard_map/ppermute | solution.py:24
  139.7 35.2 %copy-start.8 = (s32[1024,1024]{1,0:T(8,128)S(1)}, s32[1024,1024]{1,0:T(8,128)}, u32[]{:S(2)}) copy-start(s32[1024,1024]{1,0:T(8,128)} %param.17) | copy-start | bytes 12582916
  139.9 34.9 %copy-start.12 = (s32[8,1024]{1,0:T(8,128)S(1)}, s32[8,1024]{1,0:T(8,128)}, u32[]{:S(2)}) copy-start(s32[8,1024]{1,0:T(8,128)} %param.18) | copy-start | bytes 98308
  139.9 34.8 %copy-start.13 = (f32[16]{0:T(128)S(1)}, f32[16]{0:T(128)}, u32[]{:S(2)}) copy-start(f32[16]{0:T(128)} %param.19) | copy-start | bytes 196
  140.0 40.3 %collective-permute-start.33 = (s16[224,1024]{1,0:T(8,128)(2,1)S(1)}, s16[224,1024]{1,0:T(8,128)(2,1)S(1)}, u32[]{:S(2)}, u32[]{:S(2)}) collective-permute-start(s16[224,1024]{1,0:T(8,128)(2,1)S(1)} %get-tuple-element.138), channel_id=1, source_target_pairs={{0,64},{64,128},{128,192},{192,0},{1,65},{65,129},{129,193},{193,1... | collective-permute-start | bytes 1376264 | tf_op jit(solution)/shard_map/ppermute | solution.py:24
  151.1 29.3 %collective-permute-start.35 = (s16[224,1024]{1,0:T(8,128)(2,1)S(1)}, s16[224,1024]{1,0:T(8,128)(2,1)S(1)}, u32[]{:S(2)}, u32[]{:S(2)}) collective-permute-start(s16[224,1024]{1,0:T(8,128)(2,1)S(1)} %get-tuple-element.139), channel_id=1, source_target_pairs={{0,128},{64,192},{128,0},{192,64},{1,129},{65,193},{129,1},{193,65... | collective-permute-start | bytes 1376264 | tf_op jit(solution)/shard_map/ppermute | solution.py:24
  162.9 23.0 %collective-permute-start.34 = (s16[224,1024]{1,0:T(8,128)(2,1)S(1)}, s16[224,1024]{1,0:T(8,128)(2,1)S(1)}, u32[]{:S(2)}, u32[]{:S(2)}) collective-permute-start(s16[224,1024]{1,0:T(8,128)(2,1)S(1)} %get-tuple-element.140), channel_id=1, source_target_pairs={{0,192},{64,0},{128,64},{192,128},{1,193},{65,1},{129,65},{193,129... | collective-permute-start | bytes 1376264 | tf_op jit(solution)/shard_map/ppermute | solution.py:24
  174.9 2.0 copy-start.5
  187.6 0.8 copy-start.9
  190.0 2.2 copy-start.2
  195.1 47.0 %collective-permute-start.40 = (s16[1040,256]{1,0:T(8,128)(2,1)S(1)}, s16[1040,256]{1,0:T(8,128)(2,1)S(1)}, u32[]{:S(2)}, u32[]{:S(2)}) collective-permute-start(s16[1040,256]{1,0:T(8,128)(2,1)S(1)} %fusion.3.e0), channel_id=1, source_target_pairs={{0,17},{2,19},{4,21},{6,23},{8,25},{10,27},{12,29},{14,31},{16,0},... | collective-permute-start | bytes 1597448 | tf_op jit(solution)/shard_map/ppermute | solution.py:302
  208.0 34.2 %collective-permute-start.39 = (s16[1040,256]{1,0:T(8,128)(2,1)S(1)}, s16[1040,256]{1,0:T(8,128)(2,1)S(1)}, u32[]{:S(2)}, u32[]{:S(2)}) collective-permute-start(s16[1040,256]{1,0:T(8,128)(2,1)S(1)} %fusion.3.e0), channel_id=1, source_target_pairs={{0,1},{2,3},{4,5},{6,7},{8,9},{10,11},{12,13},{14,15},{16,17},{18,... | collective-permute-start | bytes 1597448 | tf_op jit(solution)/shard_map/ppermute | solution.py:302
  211.0 31.2 %collective-permute-start.38 = (s16[1040,256]{1,0:T(8,128)(2,1)S(1)}, s16[1040,256]{1,0:T(8,128)(2,1)S(1)}, u32[]{:S(2)}, u32[]{:S(2)}) collective-permute-start(s16[1040,256]{1,0:T(8,128)(2,1)S(1)} %fusion.3.e0), channel_id=1, source_target_pairs={{0,16},{2,18},{4,20},{6,22},{8,24},{10,26},{12,28},{14,30},{16,1},... | collective-permute-start | bytes 1597448 | tf_op jit(solution)/shard_map/ppermute | solution.py:302
  221.4 20.8 %copy-start.3 = (bf16[1664,1024]{1,0:T(8,128)(2,1)S(1)}, bf16[1664,1024]{1,0:T(8,128)(2,1)}, u32[]{:S(2)}) copy-start(bf16[1664,1024]{1,0:T(8,128)(2,1)} %fusion.base_ref) | copy-start | bytes 10223620
  242.2 15.2 %copy-start.1 = (f32[32,1024]{1,0:T(8,128)S(1)}, f32[32,1024]{1,0:T(8,128)}, u32[]{:S(2)}) copy-start(f32[32,1024]{1,0:T(8,128)} %param.20) | copy-start | bytes 393220
Sparse Core Ops, SparseCore 0:
  10.1 86.5 all-gather.5

commit v5 on v3

--- a/solution.py
+++ b/solution.py
@@ -159,18 +159,21 @@
             level = e[BLK : BLK + 16].astype(jnp.int32).astype(F32)
             factor_ref[k] = jnp.exp2(level * (-1.0 / STEPS_PER_OCTAVE))
 
-    h_high, h_low = split(h_ref[0, 0, :rows].astype(jnp.int32).astype(F32))
+    part = rows // 2
+    h = jnp.concatenate([h_ref[j, 0, :part].astype(jnp.int32).astype(F32) for j in range(2)], axis=0)
+    scale = jnp.concatenate([scale_ref[j, 0] for j in range(2)], axis=0)
+    h_high, h_low = split(h)
     row = lax.broadcasted_iota(jnp.int32, (rows, wide), 0) + pl.program_id(0) * rows
     for k in range(4):
         cols = pl.ds(pl.multiple_of(((scalars[1] + 4 - k) % 4) * wide, wide), wide)
         update = mm(h_high, high_ref[k]) + (mm(h_high, low_ref[k]) + mm(h_low, high_ref[k]))
-        update = update * scale_ref[0, 0] * factor_ref[k, 0:1]
+        update = update * scale * factor_ref[k, 0:1]
         base = base_ref[:, cols].astype(F32)
         out_ref[:, cols] = jnp.where(row >= scalars[0], base - update, base).astype(BF16)
 
 
 def apply_update(scalars, panel, scales, errors, base):
-    rows, cols = panel.shape[2] - 16, base.shape[1]
+    rows, cols = 2 * (panel.shape[2] - 16), base.shape[1]
     wide = cols // 4
     whole = pl.BlockSpec((BLK + 16, wide), lambda i, s: (0, 0))
     stripe = pl.BlockSpec((rows, cols), lambda i, s: (i, 0))
@@ -180,8 +183,8 @@
             num_scalar_prefetch=1,
             grid=(base.shape[0] // rows,),
             in_specs=[
-                pl.BlockSpec((1, 1, rows + 16, BLK), lambda i, s: (i % 4, i // 4, 0, 0)),
-                pl.BlockSpec((1, 1, rows, 1), lambda i, s: (i % 4, i // 4, 0, 0)),
+                pl.BlockSpec((2, 1, rows // 2 + 16, BLK), lambda i, s: (i % 2, i // 2, 0, 0)),
+                pl.BlockSpec((2, 1, rows // 2, 1), lambda i, s: (i % 2, i // 2, 0, 0)),
                 whole,
                 whole,
                 whole,
@@ -245,11 +248,10 @@
     lanes = lambda v: jnp.repeat(v, UNIT)[None, :]
     sublanes = lambda v: jnp.repeat(v, UNIT)[:, None]
     x_piece = scatter_x(x_pieces, x, lanes(from_low))
-    x_piece, w_pieces = lax.optimization_barrier((x_piece, w_pieces))
     w_piece = scatter_x(w_pieces, x, sublanes(from_low))
     x_piece, x_rows = reach_far(x_piece, lanes(distance), (x_rows,))
+    x_piece = reach_near(x_piece, lanes(distance))
     x_piece, w_piece = lax.optimization_barrier((x_piece, w_piece))
-    x_piece = reach_near(x_piece, lanes(distance))
 
     x_block = lax.all_gather(
         x_piece.astype(jnp.float16), ("xh", "xl", "core"), axis=0, tiled=True

time: 209 us -> 208 us (level)
  waiting for transfers between devices: 54.6 us -> 65.1 us
  starting transfers between devices: 46.4 us -> 39.6 us
  other arithmetic: 17.1 us -> 14.3 us
    ppermute x12, waiting for transfers between devices: 40.2 us -> 61.8 us  [ring(): lax.ppermute(value, axis, [(i, (i + shift) % size) for i in range(size)])]
    ppermute x6, waiting for transfers between devices: 9.47 us -> 0.02 us  [scatter_x(): lax.ppermute(piece, PLANE, plane_pairs((0, 2), shift))]
    ppermute x12, starting transfers between devices: 23.7 us -> 20.3 us  [ring(): lax.ppermute(value, axis, [(i, (i + shift) % size) for i in range(size)])]
    ppermute x6, starting transfers between devices: 18.7 us -> 16.1 us  [scatter_x(): lax.ppermute(piece, PLANE, plane_pairs((0, 2), shift))]
    unnamed x31 -> x29, local copies, waits for them, and re-layouts: 4.55 us -> 4.53 us
  transfers between devices with their start and end apart: 22 -> 22, of which waited for: 12 -> 9; matrix products, arithmetic and copies ran while one was open for 11% -> 9% of each run, Pallas kernels for 4% -> 4%
where the time goes in v5:
time: 208 us; the launch traced here: 207 us
  waiting for transfers between devices  65.1 us (31%)
  starting transfers between devices  39.6 us (19%)
  blocking collectives  37.4 us (18%)
  Pallas kernels  26.2 us (13%)
  between operations  14.6 us (7%)
  other arithmetic  14.3 us (7%)
  local copies, waits for them, and re-layouts  7.6 us (4%)
    ppermute x12, waiting for transfers between devices, ring(): lax.ppermute(value, axis, [(i, (i + shift) % size) for i in range(size)])  61.8 us
    ppermute x12, starting transfers between devices, ring(): lax.ppermute(value, axis, [(i, (i + shift) % size) for i in range(size)])  20.3 us
    all_gather x1, blocking collectives, local(): panel = lax.all_gather(quantize(total), ('y', 'core'), axis=0)  19.9 us
    all_gather x1, blocking collectives, local(): lax.all_gather(x_piece.astype(jnp.float16), ('xh', 'xl', 'core'), axis=0,...  17.4 us
    ppermute x6, starting transfers between devices, scatter_x(): lax.ppermute(piece, PLANE, plane_pairs((0, 2), shift))  16.1 us
    pallas_call x1, Pallas kernels, apply_update(): pl.pallas_call(update_kernel, grid_spec=pltpu.PrefetchScalarGridSpec(num_...  14.6 us
    pallas_call x2, Pallas kernels, pick(): pl.pallas_call(functools.partial(pick_kernel, rows, cols), grid_spec=pltp...  8.98 us
    unnamed x29, local copies, waits for them, and re-layouts  4.53 us
  transfers between devices with their start and end apart: 22, of which 9 were waited for; matrix products, arithmetic and copies ran while one was open for 9% of the time, Pallas kernels for 4%

profile of v5, /device:TPU:24, one launch (start us, length us, event | category | flops | bytes accessed | tf_op | source)
XLA Modules:
  0.0 206.6 jit_solution(6127859977162543612)
XLA Ops:
  6.5 0.9 copy-done
  7.4 0.6 constant_dynamic-slice_fusion.2
  8.8 0.6 pad_add_fusion.3.scalars
  9.4 4.3 %pick_columns.1 = (bf16[128,1024]{1,0:T(8,128)(2,1)}, bf16[128,1024]{1,0:T(8,128)(2,1)}, bf16[128,1024]{1,0:T(8,128)(2,1)}, bf16[128,1024]{1,0:T(8,128)(2,1)}) custom-call(s32[9]{0:T(128)} %pad_add_fusion.3.scalars, bf16[512,1664]{1,0:T(8,128)(2,1)} %src_ref.1), custom_call_target="tpu_custom_call" | custom-call | tf_op jit(solution)/shard_map/pick_columns/pallas_call | solution.py:48
  13.7 4.1 %collective-permute-start = (bf16[128,1024]{1,0:T(8,128)(2,1)}, bf16[128,1024]{1,0:T(8,128)(2,1)}, u32[]{:S(2)}, u32[]{:S(2)}) collective-permute-start(bf16[128,1024]{1,0:T(8,128)(2,1)} %get-tuple-element.30), channel_id=1, source_target_pairs={{0,16},{2,18},{4,20},{6,22},{8,24},{10,26},{12,28},{14,30},{1,17},... | collective-permute-start | bytes 786440 | tf_op jit(solution)/shard_map/ppermute | solution.py:65
  17.8 4.6 %collective-permute-start.1 = (bf16[128,1024]{1,0:T(8,128)(2,1)}, bf16[128,1024]{1,0:T(8,128)(2,1)}, u32[]{:S(2)}, u32[]{:S(2)}) collective-permute-start(bf16[128,1024]{1,0:T(8,128)(2,1)} %get-tuple-element.31), channel_id=1, source_target_pairs={{0,1},{2,3},{4,5},{6,7},{8,9},{10,11},{12,13},{14,15},{1,0},{3,2},... | collective-permute-start | bytes 786440 | tf_op jit(solution)/shard_map/ppermute | solution.py:65
  22.5 2.0 collective-permute-start.2
  24.5 1.4 copy.15
  26.0 0.1 collective-permute-start.5
  26.1 4.6 %pick_rows.1 = (bf16[1024,256]{1,0:T(8,128)(2,1)}, bf16[1024,256]{1,0:T(8,128)(2,1)}, bf16[1024,256]{1,0:T(8,128)(2,1)}, bf16[1024,256]{1,0:T(8,128)(2,1)}) custom-call(s32[9]{0:T(128)} %pad_add_fusion.3.scalars, bf16[1664,1024]{1,0:T(8,128)(2,1)} %src_ref.2), custom_call_target="tpu_custom_call" | custom-call | tf_op jit(solution)/shard_map/pick_rows/pallas_call | solution.py:48
  30.7 1.3 collective-permute-start.8
  32.3 0.1 pad_add_fusion.2.scalars
  32.4 2.7 %collective-permute-start.9 = (bf16[1024,256]{1,0:T(8,128)(2,1)}, bf16[1024,256]{1,0:T(8,128)(2,1)S(1)}, u32[]{:S(2)}, u32[]{:S(2)}) collective-permute-start(bf16[1024,256]{1,0:T(8,128)(2,1)} %get-tuple-element.37), channel_id=1, source_target_pairs={{0,1},{2,3},{4,5},{6,7},{8,9},{10,11},{12,13},{14,15},{1,0},{3,2},... | collective-permute-start | bytes 1572872 | tf_op jit(solution)/shard_map/ppermute | solution.py:65
  35.1 1.3 collective-permute-start.10
  36.5 1.1 select_select_fusion.5
  37.6 7.8 %collective-permute-start.4 = (bf16[128,1024]{1,0:T(8,128)(2,1)S(1)}, bf16[128,1024]{1,0:T(8,128)(2,1)S(1)}, u32[]{:S(2)}, u32[]{:S(2)}) collective-permute-start(bf16[128,1024]{1,0:T(8,128)(2,1)S(1)} %select_select_fusion.5), channel_id=1, source_target_pairs={{0,10},{2,12},{4,14},{6,0},{8,2},{10,4},{12,6},{14,8},{1,11},{3,13... | collective-permute-start | bytes 786440 | tf_op jit(solution)/shard_map/ppermute | solution.py:24
  45.4 1.5 broadcast_select_fusion
  47.2 0.1 slice_dynamic-update-slice_fusion.3
  47.5 15.0 %collective-permute-done.4 = bf16[128,1024]{1,0:T(8,128)(2,1)S(1)} collective-permute-done((bf16[128,1024]{1,0:T(8,128)(2,1)S(1)}, bf16[128,1024]{1,0:T(8,128)(2,1)S(1)}, u32[]{:S(2)}, u32[]{:S(2)}) %collective-permute-start.4) | collective-permute-done | bytes 262176 | tf_op jit(solution)/shard_map/ppermute | solution.py:24
  62.5 3.5 %collective-permute-done.3 = bf16[128,1024]{1,0:T(8,128)(2,1)S(1)} collective-permute-done((bf16[128,1024]{1,0:T(8,128)(2,1)S(1)}, bf16[128,1024]{1,0:T(8,128)(2,1)S(1)}, u32[]{:S(2)}, u32[]{:S(2)}) %collective-permute-start.3) | collective-permute-done | bytes 262176 | tf_op jit(solution)/shard_map/ppermute | solution.py:24
  66.1 0.1 collective-permute-start.7
  66.2 2.0 collective-permute-start.6
  68.2 0.2 select_select_fusion.2
  68.4 8.0 %collective-permute-done.7 = bf16[128,1024]{1,0:T(8,128)(2,1)S(1)} collective-permute-done((bf16[128,1024]{1,0:T(8,128)(2,1)S(1)}, bf16[128,1024]{1,0:T(8,128)(2,1)S(1)}, u32[]{:S(2)}, u32[]{:S(2)}) %collective-permute-start.7) | collective-permute-done | bytes 262176 | tf_op jit(solution)/shard_map/ppermute | solution.py:24
  76.4 1.0 collective-permute-done.6
  77.4 0.4 collective-permute-start.12
  77.8 3.5 %collective-permute-start.11 = (bf16[1024,256]{1,0:T(8,128)(2,1)S(1)}, bf16[1024,256]{1,0:T(8,128)(2,1)S(1)}, u32[]{:S(2)}, u32[]{:S(2)}) collective-permute-start(bf16[1024,256]{1,0:T(8,128)(2,1)S(1)} %select_select_fusion.2), channel_id=1, source_target_pairs={{0,6},{2,8},{4,10},{6,12},{8,14},{10,0},{12,2},{14,4},{1,7},{3,9},... | collective-permute-start | bytes 1572872 | tf_op jit(solution)/shard_map/ppermute | solution.py:24
  81.4 17.4 %all-gather.7 = f16[1024,1024]{1,0:T(8,128)(2,1)S(1)} all-gather(f16[128,1024]{1,0:T(8,128)(2,1)S(1)} %convert_element_type.102), channel_id=1, replica_groups=mesh['y'=4,'core'=2,'xl'=2,'z'=8,'xh'=2] {'xh','xl','core'}, dimensions={0}, use_global_device_ids=true | all-gather | bytes 2359296 | tf_op jit(solution)/shard_map/all_gather | solution.py:256
  98.8 1.9 fusion.1
  100.8 17.3 %collective-permute-done.12 = bf16[1024,256]{1,0:T(8,128)(2,1)S(1)} collective-permute-done((bf16[1024,256]{1,0:T(8,128)(2,1)S(1)}, bf16[1024,256]{1,0:T(8,128)(2,1)S(1)}, u32[]{:S(2)}, u32[]{:S(2)}) %collective-permute-start.12) | collective-permute-done | bytes 524320 | tf_op jit(solution)/shard_map/ppermute | solution.py:24
  118.1 3.0 %collective-permute-done.11 = bf16[1024,256]{1,0:T(8,128)(2,1)S(1)} collective-permute-done((bf16[1024,256]{1,0:T(8,128)(2,1)S(1)}, bf16[1024,256]{1,0:T(8,128)(2,1)S(1)}, u32[]{:S(2)}, u32[]{:S(2)}) %collective-permute-start.11) | collective-permute-done | bytes 524320 | tf_op jit(solution)/shard_map/ppermute | solution.py:24
  121.1 1.2 select_select_fusion.1
  122.3 2.4 %collective-permute-start.17 = (bf16[1024,256]{1,0:T(8,128)(2,1)}, bf16[1024,256]{1,0:T(8,128)(2,1)}, u32[]{:S(2)}, u32[]{:S(2)}) collective-permute-start(bf16[1024,256]{1,0:T(8,128)(2,1)} %select_select_fusion.1), channel_id=1, source_target_pairs={{0,14},{2,0},{4,2},{6,4},{8,6},{10,8},{12,10},{14,12},{1,15},{3,1}... | collective-permute-start | bytes 1572872 | tf_op jit(solution)/shard_map/ppermute | solution.py:24
  124.7 0.3 abs_reduce_fusion
  125.1 0.1 reshape.325
  125.2 0.1 reshape.332
  125.3 0.3 convert_convert_fusion
  125.6 0.2 pad_add_fusion
  125.8 0.1 dynamic-slice_bitcast_fusion.2
  125.9 1.6 collective-permute-start.13
  127.5 1.3 collective-permute-start.15
  128.9 1.1 collective-permute-start.14
  129.9 0.2 select_reduce_fusion
  130.1 1.0 fusion.28
  131.2 0.9 copy-done.5
  132.1 3.3 %fusion.base_ref = bf16[1664,1024]{1,0:T(8,128)(2,1)} fusion(bf16[1664,1024]{1,0:T(8,128)(2,1)S(1)} %copy-done.5, s32[]{:T(128)S(6)} %min.14, bf16[1024,1024]{1,0:T(8,128)(2,1)S(1)} %get-tuple-element.51, pred[1664]{0:T(1024)(128)(4,1)S(1)} %fusion.13), kind=kLoop, calls=%fused_computation.2 | loop fusion | flops 1703936 | bytes 8914564 | tf_op jit(solution)/shard_map/jit(_where)/select_n | solution.py:294
  135.4 0.1 constant_dynamic-slice_fusion.q_ref
  135.5 10.3 %collective-permute-done.13 = s16[224,1024]{1,0:T(8,128)(2,1)S(1)} collective-permute-done((s16[224,1024]{1,0:T(8,128)(2,1)S(1)}, s16[224,1024]{1,0:T(8,128)(2,1)S(1)}, u32[]{:S(2)}, u32[]{:S(2)}) %collective-permute-start.13) | collective-permute-done | bytes 458784 | tf_op jit(solution)/shard_map/ppermute | solution.py:24
  145.9 3.6 %collective-permute-done.14 = s16[224,1024]{1,0:T(8,128)(2,1)S(1)} collective-permute-done((s16[224,1024]{1,0:T(8,128)(2,1)S(1)}, s16[224,1024]{1,0:T(8,128)(2,1)S(1)}, u32[]{:S(2)}, u32[]{:S(2)}) %collective-permute-start.14) | collective-permute-done | bytes 458784 | tf_op jit(solution)/shard_map/ppermute | solution.py:24
  149.5 1.7 fusion.5
  151.2 1.7 select_select_fusion.w_ref
  153.0 2.2 %copy-done.2 = f32[1024,1024]{1,0:T(8,128)S(1)} copy-done((f32[1024,1024]{1,0:T(8,128)S(1)}, f32[1024,1024]{1,0:T(8,128)}, u32[]{:S(2)}) %copy-start.2) | copy-done | bytes 4194328
  155.2 2.6 %block_error.1 = f32[1024,256]{1,0:T(8,128)S(1)} custom-call(f32[1024,1024]{1,0:T(8,128)S(1)} %copy-done.2, bf16[1024,256]{1,0:T(8,128)(2,1)S(1)} %select_select_fusion.w_ref, f32[1024,256]{1,0:T(8,128)S(1)} %constant_dynamic-slice_fusion.q_ref), custom_call_target="tpu_custom_call" | custom-call | flops 1610612736 | bytes 4194304 | tf_op jit(solution)/shard_map/block_error/pallas_call | solution.py:130
  157.8 0.1 multiply_round-nearest-even_fusion
  157.9 0.1 fusion.3.e0
  158.0 0.1 collective-permute-start.20
  158.1 1.8 collective-permute-start.19
  159.9 1.3 collective-permute-start.18
  161.2 0.1 abs_reduce_fusion.2
  161.4 0.2 convert_convert_fusion.1
  161.6 19.9 %all-gather.8 = s16[1792,1024]{1,0:T(8,128)(2,1)S(1)} all-gather(s16[224,1024]{1,0:T(8,128)(2,1)S(1)} %pad_add_fusion.1), channel_id=3, replica_groups=mesh['y'=4,'core'=2,'xl'=2,'z'=8,'xh'=2] {'y','core'}, dimensions={0}, use_global_device_ids=true | all-gather | bytes 4128768 | tf_op jit(solution)/shard_map/all_gather | solution.py:281
  181.6 0.3 mul.219.scale_ref
  181.9 3.3 %collective-permute-done.18.e1 = s16[1040,256]{1,0:T(8,128)(2,1)S(1)} collective-permute-done((s16[1040,256]{1,0:T(8,128)(2,1)S(1)}, s16[1040,256]{1,0:T(8,128)(2,1)S(1)}, u32[]{:S(2)}, u32[]{:S(2)}) %collective-permute-start.18) | collective-permute-done | bytes 532512 | tf_op jit(solution)/shard_map/ppermute | solution.py:287
  185.2 14.6 %apply_update.1 = bf16[1664,1024]{1,0:T(8,128)(2,1)} custom-call(s32[2]{0:T(128)S(1)} %pad_add_fusion.2.scalars, s16[4,2,224,1024]{3,2,1,0:T(8,128)(2,1)S(1)} %bitcast.37, f32[4,2,208,1]{3,2,1,0:T(8,128)S(1)} %mul.219.scale_ref, s16[1040,256]{1,0:T(8,128)(2,1)S(1)} %fusion.3.e0, s16[1040,256]{1,0:T(8,128)(2,1)S(1)} %collective-permute-done.18.e1, ...), custom_call_target="tpu_custom_call" | custom-call | flops 10468982784 | bytes 12320768 | tf_op jit(solution)/shard_map/apply_update/pallas_call | solution.py:180
  (67 shorter events, 1.4 us)
Async XLA Ops:
  6.5 0.9 copy-start
  6.5 18.0 %copy-start.6 = (bf16[512,1664]{1,0:T(8,128)(2,1)S(1)}, bf16[512,1664]{1,0:T(8,128)(2,1)}, u32[]{:S(2)}) copy-start(bf16[512,1664]{1,0:T(8,128)(2,1)} %src_ref.1) | copy-start | bytes 5111812
  6.5 146.4 %all-gather.6.cloned.1.call-start = ((), (), s32[]{:S(2)}) async-start(), calls=%async_computation | async-start | bytes 4259840 | tf_op jit(solution)/shard_map/all_gather | solution.py:230
  13.7 18.7 %collective-permute-start = (bf16[128,1024]{1,0:T(8,128)(2,1)}, bf16[128,1024]{1,0:T(8,128)(2,1)}, u32[]{:S(2)}, u32[]{:S(2)}) collective-permute-start(bf16[128,1024]{1,0:T(8,128)(2,1)} %get-tuple-element.30), channel_id=1, source_target_pairs={{0,16},{2,18},{4,20},{6,22},{8,24},{10,26},{12,28},{14,30},{1,17},... | collective-permute-start | bytes 786440 | tf_op jit(solution)/shard_map/ppermute | solution.py:65
  17.8 17.3 %collective-permute-start.1 = (bf16[128,1024]{1,0:T(8,128)(2,1)}, bf16[128,1024]{1,0:T(8,128)(2,1)}, u32[]{:S(2)}, u32[]{:S(2)}) collective-permute-start(bf16[128,1024]{1,0:T(8,128)(2,1)} %get-tuple-element.31), channel_id=1, source_target_pairs={{0,1},{2,3},{4,5},{6,7},{8,9},{10,11},{12,13},{14,15},{1,0},{3,2},... | collective-permute-start | bytes 786440 | tf_op jit(solution)/shard_map/ppermute | solution.py:65
  22.5 14.0 %collective-permute-start.2 = (bf16[128,1024]{1,0:T(8,128)(2,1)}, bf16[128,1024]{1,0:T(8,128)(2,1)}, u32[]{:S(2)}, u32[]{:S(2)}) collective-permute-start(bf16[128,1024]{1,0:T(8,128)(2,1)} %get-tuple-element.32), channel_id=1, source_target_pairs={{0,17},{2,19},{4,21},{6,23},{8,25},{10,27},{12,29},{14,31},{1,16},... | collective-permute-start | bytes 786440 | tf_op jit(solution)/shard_map/ppermute | solution.py:65
  26.0 19.4 %collective-permute-start.5 = (bf16[512,832]{0,1:T(8,128)(2,1)S(1)}, bf16[512,832]{0,1:T(8,128)(2,1)}, u32[]{:S(2)}, u32[]{:S(2)}) collective-permute-start(bf16[512,832]{0,1:T(8,128)(2,1)S(1)} %constant_dynamic-slice_fusion.1), channel_id=1, source_target_pairs={{0,32},{32,0},{1,33},{33,1},{2,34},{34,2},{3,35},{35,3},{4,36},{36... | collective-permute-start | bytes 2555912 | tf_op jit(solution)/shard_map/ppermute | solution.py:24
  30.7 37.5 %collective-permute-start.8 = (bf16[1024,256]{1,0:T(8,128)(2,1)}, bf16[1024,256]{1,0:T(8,128)(2,1)S(1)}, u32[]{:S(2)}, u32[]{:S(2)}) collective-permute-start(bf16[1024,256]{1,0:T(8,128)(2,1)} %get-tuple-element.36), channel_id=1, source_target_pairs={{0,16},{2,18},{4,20},{6,22},{8,24},{10,26},{12,28},{14,30},{1,17},... | collective-permute-start | bytes 1572872 | tf_op jit(solution)/shard_map/ppermute | solution.py:65
  32.4 35.8 %collective-permute-start.9 = (bf16[1024,256]{1,0:T(8,128)(2,1)}, bf16[1024,256]{1,0:T(8,128)(2,1)S(1)}, u32[]{:S(2)}, u32[]{:S(2)}) collective-permute-start(bf16[1024,256]{1,0:T(8,128)(2,1)} %get-tuple-element.37), channel_id=1, source_target_pairs={{0,1},{2,3},{4,5},{6,7},{8,9},{10,11},{12,13},{14,15},{1,0},{3,2},... | collective-permute-start | bytes 1572872 | tf_op jit(solution)/shard_map/ppermute | solution.py:65
  35.1 33.1 %collective-permute-start.10 = (bf16[1024,256]{1,0:T(8,128)(2,1)}, bf16[1024,256]{1,0:T(8,128)(2,1)S(1)}, u32[]{:S(2)}, u32[]{:S(2)}) collective-permute-start(bf16[1024,256]{1,0:T(8,128)(2,1)} %get-tuple-element.38), channel_id=1, source_target_pairs={{0,17},{2,19},{4,21},{6,23},{8,25},{10,27},{12,29},{14,31},{1,16},... | collective-permute-start | bytes 1572872 | tf_op jit(solution)/shard_map/ppermute | solution.py:65
  37.6 25.0 %collective-permute-start.4 = (bf16[128,1024]{1,0:T(8,128)(2,1)S(1)}, bf16[128,1024]{1,0:T(8,128)(2,1)S(1)}, u32[]{:S(2)}, u32[]{:S(2)}) collective-permute-start(bf16[128,1024]{1,0:T(8,128)(2,1)S(1)} %select_select_fusion.5), channel_id=1, source_target_pairs={{0,10},{2,12},{4,14},{6,0},{8,2},{10,4},{12,6},{14,8},{1,11},{3,13... | collective-permute-start | bytes 786440 | tf_op jit(solution)/shard_map/ppermute | solution.py:24
  45.4 20.6 %collective-permute-start.3 = (bf16[128,1024]{1,0:T(8,128)(2,1)S(1)}, bf16[128,1024]{1,0:T(8,128)(2,1)S(1)}, u32[]{:S(2)}, u32[]{:S(2)}) collective-permute-start(bf16[128,1024]{1,0:T(8,128)(2,1)S(1)} %select_select_fusion.5), channel_id=1, source_target_pairs={{0,6},{2,8},{4,10},{6,12},{8,14},{10,0},{12,2},{14,4},{1,7},{3,9},... | collective-permute-start | bytes 786440 | tf_op jit(solution)/shard_map/ppermute | solution.py:24
  47.0 21.2 %copy-start.8 = (bf16[1024,256]{1,0:T(8,128)(2,1)S(1)}, bf16[1024,256]{1,0:T(8,128)(2,1)}, u32[]{:S(2)}) copy-start(bf16[1024,256]{1,0:T(8,128)(2,1)} %get-tuple-element.35) | copy-start | bytes 1572868
  66.1 10.3 %collective-permute-start.7 = (bf16[128,1024]{1,0:T(8,128)(2,1)S(1)}, bf16[128,1024]{1,0:T(8,128)(2,1)S(1)}, u32[]{:S(2)}, u32[]{:S(2)}) collective-permute-start(bf16[128,1024]{1,0:T(8,128)(2,1)S(1)} %select_select_fusion.4), channel_id=1, source_target_pairs={{0,14},{2,0},{4,2},{6,4},{8,6},{10,8},{12,10},{14,12},{1,15},{3,1}... | collective-permute-start | bytes 786440 | tf_op jit(solution)/shard_map/ppermute | solution.py:24
  66.2 11.2 %collective-permute-start.6 = (bf16[128,1024]{1,0:T(8,128)(2,1)S(1)}, bf16[128,1024]{1,0:T(8,128)(2,1)S(1)}, u32[]{:S(2)}, u32[]{:S(2)}) collective-permute-start(bf16[128,1024]{1,0:T(8,128)(2,1)S(1)} %select_select_fusion.4), channel_id=1, source_target_pairs={{0,2},{2,4},{4,6},{6,8},{8,10},{10,12},{12,14},{14,0},{1,3},{3,5},... | collective-permute-start | bytes 786440 | tf_op jit(solution)/shard_map/ppermute | solution.py:24
  77.4 40.7 %collective-permute-start.12 = (bf16[1024,256]{1,0:T(8,128)(2,1)S(1)}, bf16[1024,256]{1,0:T(8,128)(2,1)S(1)}, u32[]{:S(2)}, u32[]{:S(2)}) collective-permute-start(bf16[1024,256]{1,0:T(8,128)(2,1)S(1)} %select_select_fusion.2), channel_id=1, source_target_pairs={{0,10},{2,12},{4,14},{6,0},{8,2},{10,4},{12,6},{14,8},{1,11},{3,13... | collective-permute-start | bytes 1572872 | tf_op jit(solution)/shard_map/ppermute | solution.py:24
  77.8 43.3 %collective-permute-start.11 = (bf16[1024,256]{1,0:T(8,128)(2,1)S(1)}, bf16[1024,256]{1,0:T(8,128)(2,1)S(1)}, u32[]{:S(2)}, u32[]{:S(2)}) collective-permute-start(bf16[1024,256]{1,0:T(8,128)(2,1)S(1)} %select_select_fusion.2), channel_id=1, source_target_pairs={{0,6},{2,8},{4,10},{6,12},{8,14},{10,0},{12,2},{14,4},{1,7},{3,9},... | collective-permute-start | bytes 1572872 | tf_op jit(solution)/shard_map/ppermute | solution.py:24
  100.7 24.5 %copy-start.4 = (f32[832,1024]{1,0:T(8,128)}, f32[832,1024]{1,0:T(8,128)S(1)}, u32[]{:S(2)}) copy-start(f32[832,1024]{1,0:T(8,128)S(1)} %fusion.1) | copy-start | bytes 10223620
  122.3 28.9 %collective-permute-start.17 = (bf16[1024,256]{1,0:T(8,128)(2,1)}, bf16[1024,256]{1,0:T(8,128)(2,1)}, u32[]{:S(2)}, u32[]{:S(2)}) collective-permute-start(bf16[1024,256]{1,0:T(8,128)(2,1)} %select_select_fusion.1), channel_id=1, source_target_pairs={{0,14},{2,0},{4,2},{6,4},{8,6},{10,8},{12,10},{14,12},{1,15},{3,1}... | collective-permute-start | bytes 1572872 | tf_op jit(solution)/shard_map/ppermute | solution.py:24
  124.7 26.5 %collective-permute-start.16 = (bf16[1024,256]{1,0:T(8,128)(2,1)}, bf16[1024,256]{1,0:T(8,128)(2,1)}, u32[]{:S(2)}, u32[]{:S(2)}) collective-permute-start(bf16[1024,256]{1,0:T(8,128)(2,1)} %select_select_fusion.1), channel_id=1, source_target_pairs={{0,2},{2,4},{4,6},{6,8},{8,10},{10,12},{12,14},{14,0},{1,3},{3,5},... | collective-permute-start | bytes 1572872 | tf_op jit(solution)/shard_map/ppermute | solution.py:24
  125.6 4.5 %copy-start.7 = (s32[1024,1024]{1,0:T(8,128)S(1)}, s32[1024,1024]{1,0:T(8,128)}, u32[]{:S(2)}) copy-start(s32[1024,1024]{1,0:T(8,128)} %param.9) | copy-start | bytes 12582916
  125.8 4.1 %copy-start.9 = (s32[8,1024]{1,0:T(8,128)S(1)}, s32[8,1024]{1,0:T(8,128)}, u32[]{:S(2)}) copy-start(s32[8,1024]{1,0:T(8,128)} %param.10) | copy-start | bytes 98308
  125.8 4.1 %copy-start.10 = (f32[16]{0:T(128)S(1)}, f32[16]{0:T(128)}, u32[]{:S(2)}) copy-start(f32[16]{0:T(128)} %param.11) | copy-start | bytes 196
  125.9 19.9 %collective-permute-start.13 = (s16[224,1024]{1,0:T(8,128)(2,1)S(1)}, s16[224,1024]{1,0:T(8,128)(2,1)S(1)}, u32[]{:S(2)}, u32[]{:S(2)}) collective-permute-start(s16[224,1024]{1,0:T(8,128)(2,1)S(1)} %get-tuple-element.61), channel_id=1, source_target_pairs={{0,64},{64,128},{128,192},{192,0},{1,65},{65,129},{129,193},{193,1... | collective-permute-start | bytes 1376264 | tf_op jit(solution)/shard_map/ppermute | solution.py:24
  127.5 18.3 %collective-permute-start.15 = (s16[224,1024]{1,0:T(8,128)(2,1)S(1)}, s16[224,1024]{1,0:T(8,128)(2,1)S(1)}, u32[]{:S(2)}, u32[]{:S(2)}) collective-permute-start(s16[224,1024]{1,0:T(8,128)(2,1)S(1)} %get-tuple-element.62), channel_id=1, source_target_pairs={{0,128},{64,192},{128,0},{192,64},{1,129},{65,193},{129,1},{193,65... | collective-permute-start | bytes 1376264 | tf_op jit(solution)/shard_map/ppermute | solution.py:24
  128.9 20.7 %collective-permute-start.14 = (s16[224,1024]{1,0:T(8,128)(2,1)S(1)}, s16[224,1024]{1,0:T(8,128)(2,1)S(1)}, u32[]{:S(2)}, u32[]{:S(2)}) collective-permute-start(s16[224,1024]{1,0:T(8,128)(2,1)S(1)} %get-tuple-element.63), channel_id=1, source_target_pairs={{0,192},{64,0},{128,64},{192,128},{1,193},{65,1},{129,65},{193,129... | collective-permute-start | bytes 1376264 | tf_op jit(solution)/shard_map/ppermute | solution.py:24
  130.1 2.0 copy-start.5
  153.0 2.2 %copy-start.2 = (f32[1024,1024]{1,0:T(8,128)S(1)}, f32[1024,1024]{1,0:T(8,128)}, u32[]{:S(2)}) copy-start(f32[1024,1024]{1,0:T(8,128)} %all-gather.6.cloned.1.call-done.inv_ref) | copy-start | bytes 12582916
  158.0 23.8 %collective-permute-start.20 = (s16[1040,256]{1,0:T(8,128)(2,1)S(1)}, s16[1040,256]{1,0:T(8,128)(2,1)S(1)}, u32[]{:S(2)}, u32[]{:S(2)}) collective-permute-start(s16[1040,256]{1,0:T(8,128)(2,1)S(1)} %fusion.3.e0), channel_id=1, source_target_pairs={{0,17},{2,19},{4,21},{6,23},{8,25},{10,27},{12,29},{14,31},{16,0},... | collective-permute-start | bytes 1597448 | tf_op jit(solution)/shard_map/ppermute | solution.py:287
  158.1 23.8 %collective-permute-start.19 = (s16[1040,256]{1,0:T(8,128)(2,1)S(1)}, s16[1040,256]{1,0:T(8,128)(2,1)S(1)}, u32[]{:S(2)}, u32[]{:S(2)}) collective-permute-start(s16[1040,256]{1,0:T(8,128)(2,1)S(1)} %fusion.3.e0), channel_id=1, source_target_pairs={{0,1},{2,3},{4,5},{6,7},{8,9},{10,11},{12,13},{14,15},{16,17},{18,... | collective-permute-start | bytes 1597448 | tf_op jit(solution)/shard_map/ppermute | solution.py:287
  159.9 25.3 %collective-permute-start.18 = (s16[1040,256]{1,0:T(8,128)(2,1)S(1)}, s16[1040,256]{1,0:T(8,128)(2,1)S(1)}, u32[]{:S(2)}, u32[]{:S(2)}) collective-permute-start(s16[1040,256]{1,0:T(8,128)(2,1)S(1)} %fusion.3.e0), channel_id=1, source_target_pairs={{0,16},{2,18},{4,20},{6,22},{8,24},{10,26},{12,28},{14,30},{16,1},... | collective-permute-start | bytes 1597448 | tf_op jit(solution)/shard_map/ppermute | solution.py:287
  161.6 23.6 %copy-start.3 = (bf16[1664,1024]{1,0:T(8,128)(2,1)S(1)}, bf16[1664,1024]{1,0:T(8,128)(2,1)}, u32[]{:S(2)}) copy-start(bf16[1664,1024]{1,0:T(8,128)(2,1)} %fusion.base_ref) | copy-start | bytes 10223620
  185.2 14.6 %copy-start.1 = (f32[32,1024]{1,0:T(8,128)S(1)}, f32[32,1024]{1,0:T(8,128)}, u32[]{:S(2)}) copy-start(f32[32,1024]{1,0:T(8,128)} %param.12) | copy-start | bytes 393220
Sparse Core Ops, SparseCore 0:
  10.1 101.6 all-gather.5

commit v6 on v5

--- a/solution.py
+++ b/solution.py
@@ -260,7 +260,7 @@
     partial_panel = lax.dot_general(
         x_rows, x_block, (((1,), (0,)), ((), ())), preferred_element_type=F32
     )
-    w_piece, partial_panel = reach_far(w_piece, sublanes(distance), (partial_panel,))
+    w_piece, = reach_far(w_piece, sublanes(distance))
     w_piece = reach_near(w_piece, sublanes(distance))
     quarter = half // 4
     parts = partial_panel.reshape(4, quarter, BLK)
@@ -269,7 +269,10 @@
     total = lax.dynamic_index_in_dim(parts, y, 0, False)
     for shift in (1, 3, 2):
         sent = lax.dynamic_index_in_dim(message, (y + shift) % 4, 0, False)
-        total = total + dequantize(ring("y", 4, shift, sent))
+        got = ring("y", 4, shift, sent)
+        if shift == 1:
+            got, inverse = lax.optimization_barrier((got, inverse))
+        total = total + dequantize(got)
     chosen = (scale_index[:, :, None] == jnp.arange(LEVELS, dtype=jnp.int32)).astype(F32)
     group_scale = jnp.sum(chosen * scale_table, axis=2)
     quantized = jnp.repeat(group_scale, GROUP, axis=0) * (codes.astype(F32) - 7.5)

time: 208 us -> 197 us (0.947)
  waiting for transfers between devices: 65.1 us -> 52.8 us
    ppermute x12, waiting for transfers between devices: 61.8 us -> 51.6 us  [ring(): lax.ppermute(value, axis, [(i, (i + shift) % size) for i in range(size)])]
    ppermute x3, waiting for transfers between devices: 3.26 us -> 1.18 us  [local(): errors.append(lax.ppermute(error, PLANE, plane_pairs(range(4), shift)))]
  transfers between devices with their start and end apart: 22 -> 22, of which waited for: 9 -> 10; matrix products, arithmetic and copies ran while one was open for 9% -> 8% of each run, Pallas kernels for 4% -> 5%
where the time goes in v6:
time: 197 us; the launch traced here: 195 us
  waiting for transfers between devices  52.8 us (27%)
  starting transfers between devices  40 us (20%)
  blocking collectives  37.1 us (19%)
  Pallas kernels  26.3 us (13%)
  between operations  14.6 us (7%)
  other arithmetic  12.9 us (7%)
  local copies, waits for them, and re-layouts  8.79 us (4%)
  matrix products  2.02 us (1%)
    ppermute x12, waiting for transfers between devices, ring(): lax.ppermute(value, axis, [(i, (i + shift) % size) for i in range(size)])  51.6 us
    all_gather x1, blocking collectives, local(): panel = lax.all_gather(quantize(total), ('y', 'core'), axis=0)  19.7 us
    ppermute x12, starting transfers between devices, ring(): lax.ppermute(value, axis, [(i, (i + shift) % size) for i in range(size)])  18.9 us
    all_gather x1, blocking collectives, local(): lax.all_gather(x_piece.astype(jnp.float16), ('xh', 'xl', 'core'), axis=0,...  17.4 us
    ppermute x6, starting transfers between devices, scatter_x(): lax.ppermute(piece, PLANE, plane_pairs((0, 2), shift))  16.9 us
    pallas_call x1, Pallas kernels, apply_update(): pl.pallas_call(update_kernel, grid_spec=pltpu.PrefetchScalarGridSpec(num_...  14.6 us
    pallas_call x2, Pallas kernels, pick(): pl.pallas_call(functools.partial(pick_kernel, rows, cols), grid_spec=pltp...  8.99 us
    unnamed x29, local copies, waits for them, and re-layouts  5.72 us
  transfers between devices with their start and end apart: 22, of which 10 were waited for; matrix products, arithmetic and copies ran while one was open for 8% of the time, Pallas kernels for 5%

profile of v6, /device:TPU:24, one launch (start us, length us, event | category | flops | bytes accessed | tf_op | source)
XLA Modules:
  0.0 194.5 jit_solution(16861708852427303753)
XLA Ops:
  6.5 0.9 copy-done
  7.4 0.6 constant_dynamic-slice_fusion.2
  8.8 0.7 pad_add_fusion.3.scalars
  9.4 4.4 %pick_columns.1 = (bf16[128,1024]{1,0:T(8,128)(2,1)}, bf16[128,1024]{1,0:T(8,128)(2,1)}, bf16[128,1024]{1,0:T(8,128)(2,1)}, bf16[128,1024]{1,0:T(8,128)(2,1)}) custom-call(s32[9]{0:T(128)} %pad_add_fusion.3.scalars, bf16[512,1664]{1,0:T(8,128)(2,1)} %src_ref.1), custom_call_target="tpu_custom_call" | custom-call | tf_op jit(solution)/shard_map/pick_columns/pallas_call | solution.py:48
  13.8 4.1 %collective-permute-start = (bf16[128,1024]{1,0:T(8,128)(2,1)}, bf16[128,1024]{1,0:T(8,128)(2,1)}, u32[]{:S(2)}, u32[]{:S(2)}) collective-permute-start(bf16[128,1024]{1,0:T(8,128)(2,1)} %get-tuple-element.31), channel_id=1, source_target_pairs={{0,16},{2,18},{4,20},{6,22},{8,24},{10,26},{12,28},{14,30},{1,17},... | collective-permute-start | bytes 786440 | tf_op jit(solution)/shard_map/ppermute | solution.py:65
  17.9 4.6 %collective-permute-start.1 = (bf16[128,1024]{1,0:T(8,128)(2,1)}, bf16[128,1024]{1,0:T(8,128)(2,1)}, u32[]{:S(2)}, u32[]{:S(2)}) collective-permute-start(bf16[128,1024]{1,0:T(8,128)(2,1)} %get-tuple-element.32), channel_id=1, source_target_pairs={{0,1},{2,3},{4,5},{6,7},{8,9},{10,11},{12,13},{14,15},{1,0},{3,2},... | collective-permute-start | bytes 786440 | tf_op jit(solution)/shard_map/ppermute | solution.py:65
  22.6 2.0 %collective-permute-start.2 = (bf16[128,1024]{1,0:T(8,128)(2,1)}, bf16[128,1024]{1,0:T(8,128)(2,1)}, u32[]{:S(2)}, u32[]{:S(2)}) collective-permute-start(bf16[128,1024]{1,0:T(8,128)(2,1)} %get-tuple-element.33), channel_id=1, source_target_pairs={{0,17},{2,19},{4,21},{6,23},{8,25},{10,27},{12,29},{14,31},{1,16},... | collective-permute-start | bytes 786440 | tf_op jit(solution)/shard_map/ppermute | solution.py:65
  24.6 1.4 copy.15
  26.1 0.1 collective-permute-start.5
  26.2 4.6 %pick_rows.1 = (bf16[1024,256]{1,0:T(8,128)(2,1)}, bf16[1024,256]{1,0:T(8,128)(2,1)}, bf16[1024,256]{1,0:T(8,128)(2,1)}, bf16[1024,256]{1,0:T(8,128)(2,1)}) custom-call(s32[9]{0:T(128)} %pad_add_fusion.3.scalars, bf16[1664,1024]{1,0:T(8,128)(2,1)} %src_ref.2), custom_call_target="tpu_custom_call" | custom-call | tf_op jit(solution)/shard_map/pick_rows/pallas_call | solution.py:48
  30.8 2.1 %collective-permute-start.8 = (bf16[1024,256]{1,0:T(8,128)(2,1)}, bf16[1024,256]{1,0:T(8,128)(2,1)}, u32[]{:S(2)}, u32[]{:S(2)}) collective-permute-start(bf16[1024,256]{1,0:T(8,128)(2,1)} %get-tuple-element.38), channel_id=1, source_target_pairs={{0,16},{2,18},{4,20},{6,22},{8,24},{10,26},{12,28},{14,30},{1,17},... | collective-permute-start | bytes 1572872 | tf_op jit(solution)/shard_map/ppermute | solution.py:65
  33.2 2.7 %collective-permute-start.9 = (bf16[1024,256]{1,0:T(8,128)(2,1)}, bf16[1024,256]{1,0:T(8,128)(2,1)S(1)}, u32[]{:S(2)}, u32[]{:S(2)}) collective-permute-start(bf16[1024,256]{1,0:T(8,128)(2,1)} %get-tuple-element.39), channel_id=1, source_target_pairs={{0,1},{2,3},{4,5},{6,7},{8,9},{10,11},{12,13},{14,15},{1,0},{3,2},... | collective-permute-start | bytes 1572872 | tf_op jit(solution)/shard_map/ppermute | solution.py:65
  36.0 1.3 collective-permute-start.10
  37.3 1.1 select_select_fusion.5
  38.4 7.8 %collective-permute-start.4 = (bf16[128,1024]{1,0:T(8,128)(2,1)S(1)}, bf16[128,1024]{1,0:T(8,128)(2,1)S(1)}, u32[]{:S(2)}, u32[]{:S(2)}) collective-permute-start(bf16[128,1024]{1,0:T(8,128)(2,1)S(1)} %select_select_fusion.5), channel_id=1, source_target_pairs={{0,10},{2,12},{4,14},{6,0},{8,2},{10,4},{12,6},{14,8},{1,11},{3,13... | collective-permute-start | bytes 786440 | tf_op jit(solution)/shard_map/ppermute | solution.py:24
  46.3 0.4 broadcast_select_fusion
  46.7 0.1 slice_dynamic-update-slice_fusion.6
  47.3 16.1 %collective-permute-done.4 = bf16[128,1024]{1,0:T(8,128)(2,1)S(1)} collective-permute-done((bf16[128,1024]{1,0:T(8,128)(2,1)S(1)}, bf16[128,1024]{1,0:T(8,128)(2,1)S(1)}, u32[]{:S(2)}, u32[]{:S(2)}) %collective-permute-start.4) | collective-permute-done | bytes 262176 | tf_op jit(solution)/shard_map/ppermute | solution.py:24
  63.4 3.4 %collective-permute-done.3 = bf16[128,1024]{1,0:T(8,128)(2,1)S(1)} collective-permute-done((bf16[128,1024]{1,0:T(8,128)(2,1)S(1)}, bf16[128,1024]{1,0:T(8,128)(2,1)S(1)}, u32[]{:S(2)}, u32[]{:S(2)}) %collective-permute-start.3) | collective-permute-done | bytes 262176 | tf_op jit(solution)/shard_map/ppermute | solution.py:24
  66.8 0.1 collective-permute-start.7
  66.9 2.0 %collective-permute-start.6 = (bf16[128,1024]{1,0:T(8,128)(2,1)S(1)}, bf16[128,1024]{1,0:T(8,128)(2,1)S(1)}, u32[]{:S(2)}, u32[]{:S(2)}) collective-permute-start(bf16[128,1024]{1,0:T(8,128)(2,1)S(1)} %select_select_fusion.4), channel_id=1, source_target_pairs={{0,2},{2,4},{4,6},{6,8},{8,10},{10,12},{12,14},{14,0},{1,3},{3,5},... | collective-permute-start | bytes 786440 | tf_op jit(solution)/shard_map/ppermute | solution.py:24
  68.9 1.1 select_select_fusion.2
  70.0 7.9 %collective-permute-done.7 = bf16[128,1024]{1,0:T(8,128)(2,1)S(1)} collective-permute-done((bf16[128,1024]{1,0:T(8,128)(2,1)S(1)}, bf16[128,1024]{1,0:T(8,128)(2,1)S(1)}, u32[]{:S(2)}, u32[]{:S(2)}) %collective-permute-start.7) | collective-permute-done | bytes 262176 | tf_op jit(solution)/shard_map/ppermute | solution.py:24
  77.9 1.2 collective-permute-done.6
  79.1 0.2 collective-permute-start.15
  79.3 3.7 %collective-permute-start.14 = (bf16[1024,256]{1,0:T(8,128)(2,1)}, bf16[1024,256]{1,0:T(8,128)(2,1)}, u32[]{:S(2)}, u32[]{:S(2)}) collective-permute-start(bf16[1024,256]{1,0:T(8,128)(2,1)} %select_select_fusion.2), channel_id=1, source_target_pairs={{0,6},{2,8},{4,10},{6,12},{8,14},{10,0},{12,2},{14,4},{1,7},{3,9},... | collective-permute-start | bytes 1572872 | tf_op jit(solution)/shard_map/ppermute | solution.py:24
  83.1 17.4 %all-gather.7 = f16[1024,1024]{1,0:T(8,128)(2,1)S(1)} all-gather(f16[128,1024]{1,0:T(8,128)(2,1)S(1)} %convert_element_type.102), channel_id=1, replica_groups=mesh['y'=4,'core'=2,'xl'=2,'z'=8,'xh'=2] {'xh','xl','core'}, dimensions={0}, use_global_device_ids=true | all-gather | bytes 2359296 | tf_op jit(solution)/shard_map/all_gather | solution.py:256
  100.5 2.0 %abs_reduce_fusion = (f32[832]{0:T(1024)S(1)}, f32[832,1024]{1,0:T(8,128)S(1)}) fusion(bf16[832,1024]{1,0:T(8,128)(2,1)S(1)} %bitcast.40, f16[1024,1024]{1,0:T(8,128)(2,1)S(1)} %all-gather.7), kind=kOutput, calls=%fused_computation.4 | convolution fusion | flops 1747582208 | bytes 7212288 | tf_op jit(solution)/shard_map/dot_general | solution.py:260
  102.6 0.1 reshape.325
  102.6 0.1 reshape.332
  102.7 0.4 convert_convert_fusion
  103.1 1.2 copy-done.6
  104.3 0.1 pad_add_fusion
  104.5 0.1 dynamic-slice_bitcast_fusion.2
  104.6 0.1 collective-permute-start.11
  104.7 2.7 %collective-permute-start.13 = (s16[224,1024]{1,0:T(8,128)(2,1)S(1)}, s16[224,1024]{1,0:T(8,128)(2,1)S(1)}, u32[]{:S(2)}, u32[]{:S(2)}) collective-permute-start(s16[224,1024]{1,0:T(8,128)(2,1)S(1)} %get-tuple-element.64), channel_id=1, source_target_pairs={{0,128},{64,192},{128,0},{192,64},{1,129},{65,193},{129,1},{193,65... | collective-permute-start | bytes 1376264 | tf_op jit(solution)/shard_map/ppermute | solution.py:24
  107.4 0.2 select_reduce_fusion
  107.6 1.1 fusion.25
  108.7 0.9 copy-done.4
  109.6 3.3 %fusion.base_ref = bf16[1664,1024]{1,0:T(8,128)(2,1)} fusion(bf16[1664,1024]{1,0:T(8,128)(2,1)S(1)} %copy-done.4, s32[]{:T(128)S(6)} %min.14, bf16[1024,1024]{1,0:T(8,128)(2,1)S(1)} %get-tuple-element.53, pred[1664]{0:T(1024)(128)(4,1)S(1)} %fusion.13), kind=kLoop, calls=%fused_computation.2 | loop fusion | flops 1703936 | bytes 8914564 | tf_op jit(solution)/shard_map/jit(_where)/select_n | solution.py:297
  112.9 7.4 %collective-permute-done.15 = bf16[1024,256]{1,0:T(8,128)(2,1)} collective-permute-done((bf16[1024,256]{1,0:T(8,128)(2,1)}, bf16[1024,256]{1,0:T(8,128)(2,1)}, u32[]{:S(2)}, u32[]{:S(2)}) %collective-permute-start.15) | collective-permute-done | bytes 524320 | tf_op jit(solution)/shard_map/ppermute | solution.py:24
  120.3 2.9 %collective-permute-done.14 = bf16[1024,256]{1,0:T(8,128)(2,1)} collective-permute-done((bf16[1024,256]{1,0:T(8,128)(2,1)}, bf16[1024,256]{1,0:T(8,128)(2,1)}, u32[]{:S(2)}, u32[]{:S(2)}) %collective-permute-start.14) | collective-permute-done | bytes 524320 | tf_op jit(solution)/shard_map/ppermute | solution.py:24
  123.2 1.7 select_select_fusion.1
  124.9 0.1 collective-permute-start.17
  125.0 2.0 %collective-permute-start.16 = (bf16[1024,256]{1,0:T(8,128)(2,1)S(1)}, bf16[1024,256]{1,0:T(8,128)(2,1)S(1)}, u32[]{:S(2)}, u32[]{:S(2)}) collective-permute-start(bf16[1024,256]{1,0:T(8,128)(2,1)S(1)} %select_select_fusion.1), channel_id=1, source_target_pairs={{0,2},{2,4},{4,6},{6,8},{8,10},{10,12},{12,14},{14,0},{1,3},{3,5},... | collective-permute-start | bytes 1572872 | tf_op jit(solution)/shard_map/ppermute | solution.py:24
  127.0 0.1 constant_dynamic-slice_fusion.q_ref
  127.2 1.9 collective-permute-done.12
  129.1 9.5 %collective-permute-done.17 = bf16[1024,256]{1,0:T(8,128)(2,1)S(1)} collective-permute-done((bf16[1024,256]{1,0:T(8,128)(2,1)S(1)}, bf16[1024,256]{1,0:T(8,128)(2,1)S(1)}, u32[]{:S(2)}, u32[]{:S(2)}) %collective-permute-start.17) | collective-permute-done | bytes 524320 | tf_op jit(solution)/shard_map/ppermute | solution.py:24
  138.6 1.3 collective-permute-done.16
  139.9 0.3 select_select_fusion.w_ref
  140.3 2.2 %copy-done.2 = f32[1024,1024]{1,0:T(8,128)S(1)} copy-done((f32[1024,1024]{1,0:T(8,128)S(1)}, f32[1024,1024]{1,0:T(8,128)}, u32[]{:S(2)}) %copy-start.2) | copy-done | bytes 4194328
  142.4 2.7 %block_error.1 = f32[1024,256]{1,0:T(8,128)S(1)} custom-call(f32[1024,1024]{1,0:T(8,128)S(1)} %copy-done.2, bf16[1024,256]{1,0:T(8,128)(2,1)S(1)} %select_select_fusion.w_ref, f32[1024,256]{1,0:T(8,128)S(1)} %constant_dynamic-slice_fusion.q_ref), custom_call_target="tpu_custom_call" | custom-call | flops 1610612736 | bytes 4194304 | tf_op jit(solution)/shard_map/block_error/pallas_call | solution.py:130
  145.2 0.1 multiply_round-nearest-even_fusion
  145.3 0.1 fusion.3.e0
  145.4 1.7 fusion.5
  147.1 0.1 collective-permute-start.20
  147.2 2.9 %collective-permute-start.19 = (s16[1040,256]{1,0:T(8,128)(2,1)S(1)}, s16[1040,256]{1,0:T(8,128)(2,1)S(1)}, u32[]{:S(2)}, u32[]{:S(2)}) collective-permute-start(s16[1040,256]{1,0:T(8,128)(2,1)S(1)} %fusion.3.e0), channel_id=1, source_target_pairs={{0,1},{2,3},{4,5},{6,7},{8,9},{10,11},{12,13},{14,15},{16,17},{18,... | collective-permute-start | bytes 1597448 | tf_op jit(solution)/shard_map/ppermute | solution.py:290
  150.1 1.3 collective-permute-start.18
  151.4 0.1 abs_reduce_fusion.2
  151.6 0.2 convert_convert_fusion.1
  151.8 19.7 %all-gather.8 = s16[1792,1024]{1,0:T(8,128)(2,1)S(1)} all-gather(s16[224,1024]{1,0:T(8,128)(2,1)S(1)} %pad_add_fusion.1), channel_id=3, replica_groups=mesh['y'=4,'core'=2,'xl'=2,'z'=8,'xh'=2] {'y','core'}, dimensions={0}, use_global_device_ids=true | all-gather | bytes 4128768 | tf_op jit(solution)/shard_map/all_gather | solution.py:284
  171.6 0.3 mul.219.scale_ref
  171.9 1.2 collective-permute-done.18.e1
  173.0 14.6 %apply_update.1 = bf16[1664,1024]{1,0:T(8,128)(2,1)} custom-call(s32[2]{0:T(128)S(1)} %pad_add_fusion.2.scalars, s16[4,2,224,1024]{3,2,1,0:T(8,128)(2,1)S(1)} %bitcast.37, f32[4,2,208,1]{3,2,1,0:T(8,128)S(1)} %mul.219.scale_ref, s16[1040,256]{1,0:T(8,128)(2,1)S(1)} %fusion.3.e0, s16[1040,256]{1,0:T(8,128)(2,1)S(1)} %collective-permute-done.18.e1, ...), custom_call_target="tpu_custom_call" | custom-call | flops 10468982784 | bytes 12320768 | tf_op jit(solution)/shard_map/apply_update/pallas_call | solution.py:180
  (66 shorter events, 1.4 us)
Async XLA Ops:
  6.5 0.9 copy-start
  6.5 18.1 %copy-start.5 = (bf16[512,1664]{1,0:T(8,128)(2,1)S(1)}, bf16[512,1664]{1,0:T(8,128)(2,1)}, u32[]{:S(2)}) copy-start(bf16[512,1664]{1,0:T(8,128)(2,1)} %src_ref.1) | copy-start | bytes 5111812
  6.5 133.7 %all-gather.6.cloned.1.call-start = ((), (), s32[]{:S(2)}) async-start(), calls=%async_computation | async-start | bytes 4259840 | tf_op jit(solution)/shard_map/all_gather | solution.py:230
  13.8 19.4 %collective-permute-start = (bf16[128,1024]{1,0:T(8,128)(2,1)}, bf16[128,1024]{1,0:T(8,128)(2,1)}, u32[]{:S(2)}, u32[]{:S(2)}) collective-permute-start(bf16[128,1024]{1,0:T(8,128)(2,1)} %get-tuple-element.31), channel_id=1, source_target_pairs={{0,16},{2,18},{4,20},{6,22},{8,24},{10,26},{12,28},{14,30},{1,17},... | collective-permute-start | bytes 786440 | tf_op jit(solution)/shard_map/ppermute | solution.py:65
  17.9 18.0 %collective-permute-start.1 = (bf16[128,1024]{1,0:T(8,128)(2,1)}, bf16[128,1024]{1,0:T(8,128)(2,1)}, u32[]{:S(2)}, u32[]{:S(2)}) collective-permute-start(bf16[128,1024]{1,0:T(8,128)(2,1)} %get-tuple-element.32), channel_id=1, source_target_pairs={{0,1},{2,3},{4,5},{6,7},{8,9},{10,11},{12,13},{14,15},{1,0},{3,2},... | collective-permute-start | bytes 786440 | tf_op jit(solution)/shard_map/ppermute | solution.py:65
  22.6 14.7 %collective-permute-start.2 = (bf16[128,1024]{1,0:T(8,128)(2,1)}, bf16[128,1024]{1,0:T(8,128)(2,1)}, u32[]{:S(2)}, u32[]{:S(2)}) collective-permute-start(bf16[128,1024]{1,0:T(8,128)(2,1)} %get-tuple-element.33), channel_id=1, source_target_pairs={{0,17},{2,19},{4,21},{6,23},{8,25},{10,27},{12,29},{14,31},{1,16},... | collective-permute-start | bytes 786440 | tf_op jit(solution)/shard_map/ppermute | solution.py:65
  26.1 20.2 %collective-permute-start.5 = (bf16[512,832]{0,1:T(8,128)(2,1)S(1)}, bf16[512,832]{0,1:T(8,128)(2,1)S(1)}, u32[]{:S(2)}, u32[]{:S(2)}) collective-permute-start(bf16[512,832]{0,1:T(8,128)(2,1)S(1)} %constant_dynamic-slice_fusion.1), channel_id=1, source_target_pairs={{0,32},{32,0},{1,33},{33,1},{2,34},{34,2},{3,35},{35,3},{4,36},{36... | collective-permute-start | bytes 2555912 | tf_op jit(solution)/shard_map/ppermute | solution.py:24
  30.8 38.2 %collective-permute-start.8 = (bf16[1024,256]{1,0:T(8,128)(2,1)}, bf16[1024,256]{1,0:T(8,128)(2,1)}, u32[]{:S(2)}, u32[]{:S(2)}) collective-permute-start(bf16[1024,256]{1,0:T(8,128)(2,1)} %get-tuple-element.38), channel_id=1, source_target_pairs={{0,16},{2,18},{4,20},{6,22},{8,24},{10,26},{12,28},{14,30},{1,17},... | collective-permute-start | bytes 1572872 | tf_op jit(solution)/shard_map/ppermute | solution.py:65
  33.2 35.7 %collective-permute-start.9 = (bf16[1024,256]{1,0:T(8,128)(2,1)}, bf16[1024,256]{1,0:T(8,128)(2,1)S(1)}, u32[]{:S(2)}, u32[]{:S(2)}) collective-permute-start(bf16[1024,256]{1,0:T(8,128)(2,1)} %get-tuple-element.39), channel_id=1, source_target_pairs={{0,1},{2,3},{4,5},{6,7},{8,9},{10,11},{12,13},{14,15},{1,0},{3,2},... | collective-permute-start | bytes 1572872 | tf_op jit(solution)/shard_map/ppermute | solution.py:65
  36.0 32.9 %collective-permute-start.10 = (bf16[1024,256]{1,0:T(8,128)(2,1)}, bf16[1024,256]{1,0:T(8,128)(2,1)S(1)}, u32[]{:S(2)}, u32[]{:S(2)}) collective-permute-start(bf16[1024,256]{1,0:T(8,128)(2,1)} %get-tuple-element.40), channel_id=1, source_target_pairs={{0,17},{2,19},{4,21},{6,23},{8,25},{10,27},{12,29},{14,31},{1,16},... | collective-permute-start | bytes 1572872 | tf_op jit(solution)/shard_map/ppermute | solution.py:65
  38.4 25.0 %collective-permute-start.4 = (bf16[128,1024]{1,0:T(8,128)(2,1)S(1)}, bf16[128,1024]{1,0:T(8,128)(2,1)S(1)}, u32[]{:S(2)}, u32[]{:S(2)}) collective-permute-start(bf16[128,1024]{1,0:T(8,128)(2,1)S(1)} %select_select_fusion.5), channel_id=1, source_target_pairs={{0,10},{2,12},{4,14},{6,0},{8,2},{10,4},{12,6},{14,8},{1,11},{3,13... | collective-permute-start | bytes 786440 | tf_op jit(solution)/shard_map/ppermute | solution.py:24
  46.3 20.5 %collective-permute-start.3 = (bf16[128,1024]{1,0:T(8,128)(2,1)S(1)}, bf16[128,1024]{1,0:T(8,128)(2,1)S(1)}, u32[]{:S(2)}, u32[]{:S(2)}) collective-permute-start(bf16[128,1024]{1,0:T(8,128)(2,1)S(1)} %select_select_fusion.5), channel_id=1, source_target_pairs={{0,6},{2,8},{4,10},{6,12},{8,14},{10,0},{12,2},{14,4},{1,7},{3,9},... | collective-permute-start | bytes 786440 | tf_op jit(solution)/shard_map/ppermute | solution.py:24
  46.8 22.1 %copy-start.8 = (bf16[1024,256]{1,0:T(8,128)(2,1)S(1)}, bf16[1024,256]{1,0:T(8,128)(2,1)}, u32[]{:S(2)}) copy-start(bf16[1024,256]{1,0:T(8,128)(2,1)} %get-tuple-element.37) | copy-start | bytes 1572868
  66.8 11.1 %collective-permute-start.7 = (bf16[128,1024]{1,0:T(8,128)(2,1)S(1)}, bf16[128,1024]{1,0:T(8,128)(2,1)S(1)}, u32[]{:S(2)}, u32[]{:S(2)}) collective-permute-start(bf16[128,1024]{1,0:T(8,128)(2,1)S(1)} %select_select_fusion.4), channel_id=1, source_target_pairs={{0,14},{2,0},{4,2},{6,4},{8,6},{10,8},{12,10},{14,12},{1,15},{3,1}... | collective-permute-start | bytes 786440 | tf_op jit(solution)/shard_map/ppermute | solution.py:24
  66.9 12.2 %collective-permute-start.6 = (bf16[128,1024]{1,0:T(8,128)(2,1)S(1)}, bf16[128,1024]{1,0:T(8,128)(2,1)S(1)}, u32[]{:S(2)}, u32[]{:S(2)}) collective-permute-start(bf16[128,1024]{1,0:T(8,128)(2,1)S(1)} %select_select_fusion.4), channel_id=1, source_target_pairs={{0,2},{2,4},{4,6},{6,8},{8,10},{10,12},{12,14},{14,0},{1,3},{3,5},... | collective-permute-start | bytes 786440 | tf_op jit(solution)/shard_map/ppermute | solution.py:24
  79.1 41.2 %collective-permute-start.15 = (bf16[1024,256]{1,0:T(8,128)(2,1)}, bf16[1024,256]{1,0:T(8,128)(2,1)}, u32[]{:S(2)}, u32[]{:S(2)}) collective-permute-start(bf16[1024,256]{1,0:T(8,128)(2,1)} %select_select_fusion.2), channel_id=1, source_target_pairs={{0,10},{2,12},{4,14},{6,0},{8,2},{10,4},{12,6},{14,8},{1,11},{3,13... | collective-permute-start | bytes 1572872 | tf_op jit(solution)/shard_map/ppermute | solution.py:24
  79.3 43.9 %collective-permute-start.14 = (bf16[1024,256]{1,0:T(8,128)(2,1)}, bf16[1024,256]{1,0:T(8,128)(2,1)}, u32[]{:S(2)}, u32[]{:S(2)}) collective-permute-start(bf16[1024,256]{1,0:T(8,128)(2,1)} %select_select_fusion.2), channel_id=1, source_target_pairs={{0,6},{2,8},{4,10},{6,12},{8,14},{10,0},{12,2},{14,4},{1,7},{3,9},... | collective-permute-start | bytes 1572872 | tf_op jit(solution)/shard_map/ppermute | solution.py:24
  102.5 1.8 copy-start.6
  104.3 3.3 %copy-start.7 = (s32[1024,1024]{1,0:T(8,128)S(1)}, s32[1024,1024]{1,0:T(8,128)}, u32[]{:S(2)}) copy-start(s32[1024,1024]{1,0:T(8,128)} %param.9) | copy-start | bytes 12582916
  104.4 3.0 %copy-start.9 = (s32[8,1024]{1,0:T(8,128)S(1)}, s32[8,1024]{1,0:T(8,128)}, u32[]{:S(2)}) copy-start(s32[8,1024]{1,0:T(8,128)} %param.10) | copy-start | bytes 98308
  104.4 3.0 %copy-start.10 = (f32[16]{0:T(128)S(1)}, f32[16]{0:T(128)}, u32[]{:S(2)}) copy-start(f32[16]{0:T(128)} %param.11) | copy-start | bytes 196
  104.6 35.6 %collective-permute-start.11 = (s16[224,1024]{1,0:T(8,128)(2,1)S(1)}, s16[224,1024]{1,0:T(8,128)(2,1)S(1)}, u32[]{:S(2)}, u32[]{:S(2)}) collective-permute-start(s16[224,1024]{1,0:T(8,128)(2,1)S(1)} %get-tuple-element.63), channel_id=1, source_target_pairs={{0,64},{64,128},{128,192},{192,0},{1,65},{65,129},{129,193},{193,1... | collective-permute-start | bytes 1376264 | tf_op jit(solution)/shard_map/ppermute | solution.py:24
  104.7 22.5 %collective-permute-start.13 = (s16[224,1024]{1,0:T(8,128)(2,1)S(1)}, s16[224,1024]{1,0:T(8,128)(2,1)S(1)}, u32[]{:S(2)}, u32[]{:S(2)}) collective-permute-start(s16[224,1024]{1,0:T(8,128)(2,1)S(1)} %get-tuple-element.64), channel_id=1, source_target_pairs={{0,128},{64,192},{128,0},{192,64},{1,129},{65,193},{129,1},{193,65... | collective-permute-start | bytes 1376264 | tf_op jit(solution)/shard_map/ppermute | solution.py:24
  107.4 21.6 %collective-permute-start.12 = (s16[224,1024]{1,0:T(8,128)(2,1)S(1)}, s16[224,1024]{1,0:T(8,128)(2,1)S(1)}, u32[]{:S(2)}, u32[]{:S(2)}) collective-permute-start(s16[224,1024]{1,0:T(8,128)(2,1)S(1)} %get-tuple-element.65), channel_id=1, source_target_pairs={{0,192},{64,0},{128,64},{192,128},{1,193},{65,1},{129,65},{193,129... | collective-permute-start | bytes 1376264 | tf_op jit(solution)/shard_map/ppermute | solution.py:24
  107.6 2.0 %copy-start.4 = (bf16[1664,1024]{1,0:T(8,128)(2,1)S(1)}, bf16[1664,1024]{1,0:T(8,128)(2,1)}, u32[]{:S(2)}) copy-start(bf16[1664,1024]{1,0:T(8,128)(2,1)} %src_ref.2) | copy-start | bytes 10223620
  124.9 13.6 %collective-permute-start.17 = (bf16[1024,256]{1,0:T(8,128)(2,1)S(1)}, bf16[1024,256]{1,0:T(8,128)(2,1)S(1)}, u32[]{:S(2)}, u32[]{:S(2)}) collective-permute-start(bf16[1024,256]{1,0:T(8,128)(2,1)S(1)} %select_select_fusion.1), channel_id=1, source_target_pairs={{0,14},{2,0},{4,2},{6,4},{8,6},{10,8},{12,10},{14,12},{1,15},{3,1}... | collective-permute-start | bytes 1572872 | tf_op jit(solution)/shard_map/ppermute | solution.py:24
  125.0 14.8 %collective-permute-start.16 = (bf16[1024,256]{1,0:T(8,128)(2,1)S(1)}, bf16[1024,256]{1,0:T(8,128)(2,1)S(1)}, u32[]{:S(2)}, u32[]{:S(2)}) collective-permute-start(bf16[1024,256]{1,0:T(8,128)(2,1)S(1)} %select_select_fusion.1), channel_id=1, source_target_pairs={{0,2},{2,4},{4,6},{6,8},{8,10},{10,12},{12,14},{14,0},{1,3},{3,5},... | collective-permute-start | bytes 1572872 | tf_op jit(solution)/shard_map/ppermute | solution.py:24
  140.3 2.2 %copy-start.2 = (f32[1024,1024]{1,0:T(8,128)S(1)}, f32[1024,1024]{1,0:T(8,128)}, u32[]{:S(2)}) copy-start(f32[1024,1024]{1,0:T(8,128)} %all-gather.6.cloned.1.call-done.inv_ref) | copy-start | bytes 12582916
  147.1 24.7 %collective-permute-start.20 = (s16[1040,256]{1,0:T(8,128)(2,1)S(1)}, s16[1040,256]{1,0:T(8,128)(2,1)S(1)}, u32[]{:S(2)}, u32[]{:S(2)}) collective-permute-start(s16[1040,256]{1,0:T(8,128)(2,1)S(1)} %fusion.3.e0), channel_id=1, source_target_pairs={{0,17},{2,19},{4,21},{6,23},{8,25},{10,27},{12,29},{14,31},{16,0},... | collective-permute-start | bytes 1597448 | tf_op jit(solution)/shard_map/ppermute | solution.py:290
  147.2 24.7 %collective-permute-start.19 = (s16[1040,256]{1,0:T(8,128)(2,1)S(1)}, s16[1040,256]{1,0:T(8,128)(2,1)S(1)}, u32[]{:S(2)}, u32[]{:S(2)}) collective-permute-start(s16[1040,256]{1,0:T(8,128)(2,1)S(1)} %fusion.3.e0), channel_id=1, source_target_pairs={{0,1},{2,3},{4,5},{6,7},{8,9},{10,11},{12,13},{14,15},{16,17},{18,... | collective-permute-start | bytes 1597448 | tf_op jit(solution)/shard_map/ppermute | solution.py:290
  150.1 22.9 %collective-permute-start.18 = (s16[1040,256]{1,0:T(8,128)(2,1)S(1)}, s16[1040,256]{1,0:T(8,128)(2,1)S(1)}, u32[]{:S(2)}, u32[]{:S(2)}) collective-permute-start(s16[1040,256]{1,0:T(8,128)(2,1)S(1)} %fusion.3.e0), channel_id=1, source_target_pairs={{0,16},{2,18},{4,20},{6,22},{8,24},{10,26},{12,28},{14,30},{16,1},... | collective-permute-start | bytes 1597448 | tf_op jit(solution)/shard_map/ppermute | solution.py:290
  151.8 21.2 %copy-start.3 = (bf16[1664,1024]{1,0:T(8,128)(2,1)S(1)}, bf16[1664,1024]{1,0:T(8,128)(2,1)}, u32[]{:S(2)}) copy-start(bf16[1664,1024]{1,0:T(8,128)(2,1)} %fusion.base_ref) | copy-start | bytes 10223620
  173.0 14.6 %copy-start.1 = (f32[32,1024]{1,0:T(8,128)S(1)}, f32[32,1024]{1,0:T(8,128)}, u32[]{:S(2)}) copy-start(f32[32,1024]{1,0:T(8,128)} %param.12) | copy-start | bytes 393220
Sparse Core Ops, SparseCore 0:
  10.1 98.1 all-gather.5

commit v7 on v6

--- a/solution.py
+++ b/solution.py
@@ -250,8 +250,8 @@
     x_piece = scatter_x(x_pieces, x, lanes(from_low))
     w_piece = scatter_x(w_pieces, x, sublanes(from_low))
     x_piece, x_rows = reach_far(x_piece, lanes(distance), (x_rows,))
+    x_piece, w_piece = lax.optimization_barrier((x_piece, w_piece))
     x_piece = reach_near(x_piece, lanes(distance))
-    x_piece, w_piece = lax.optimization_barrier((x_piece, w_piece))
 
     x_block = lax.all_gather(
         x_piece.astype(jnp.float16), ("xh", "xl", "core"), axis=0, tiled=True
@@ -260,7 +260,7 @@
     partial_panel = lax.dot_general(
         x_rows, x_block, (((1,), (0,)), ((), ())), preferred_element_type=F32
     )
-    w_piece, = reach_far(w_piece, sublanes(distance))
+    w_piece, inverse = reach_far(w_piece, sublanes(distance), (inverse,))
     w_piece = reach_near(w_piece, sublanes(distance))
     quarter = half // 4
     parts = partial_panel.reshape(4, quarter, BLK)
@@ -271,7 +271,7 @@
         sent = lax.dynamic_index_in_dim(message, (y + shift) % 4, 0, False)
         got = ring("y", 4, shift, sent)
         if shift == 1:
-            got, inverse = lax.optimization_barrier((got, inverse))
+            got, w_piece = lax.optimization_barrier((got, w_piece))
         total = total + dequantize(got)
     chosen = (scale_index[:, :, None] == jnp.arange(LEVELS, dtype=jnp.int32)).astype(F32)
     group_scale = jnp.sum(chosen * scale_table, axis=2)

time: 197 us -> 203 us (1.030)
  waiting for transfers between devices: 52.8 us -> 43.7 us
  blocking collectives: 37.1 us -> 42.2 us
  other arithmetic: 12.9 us -> 17.3 us
  starting transfers between devices: 40 us -> 44 us
    ppermute x12, waiting for transfers between devices: 51.6 us -> 33.3 us  [ring(): lax.ppermute(value, axis, [(i, (i + shift) % size) for i in range(size)])]
    ppermute x6, waiting for transfers between devices: 0.02 us -> 7.82 us  [scatter_x(): lax.ppermute(piece, PLANE, plane_pairs((0, 2), shift))]
    ppermute x12, starting transfers between devices: 18.9 us -> 23.4 us  [ring(): lax.ppermute(value, axis, [(i, (i + shift) % size) for i in range(size)])]
    all_gather x1, blocking collectives: 17.4 us -> 21.3 us  [local(): lax.all_gather(x_piece.astype(jnp.float16), ('xh', 'xl', 'core'), axis=0,...]
    unnamed x29 -> x27, local copies, waits for them, and re-layouts: 5.72 us -> 2.64 us
    exp2 x3, other arithmetic: 0.03 us -> 2.18 us  [scales_of(): return jnp.swapaxes(jnp.exp2(-level / STEPS_PER_OCTAVE), -1, -2)]
  transfers between devices with their start and end apart: 22 -> 22, of which waited for: 10 -> 8; matrix products, arithmetic and copies ran while one was open for 8% -> 12% of each run, Pallas kernels for 5% -> 5%
where the time goes in v7:
time: 203 us; the launch traced here: 200 us
  starting transfers between devices  44 us (22%)
  waiting for transfers between devices  43.7 us (22%)
  blocking collectives  42.2 us (21%)
  Pallas kernels  26.2 us (13%)
  other arithmetic  17.3 us (9%)
  between operations  14.5 us (7%)
  local copies, waits for them, and re-layouts  8.13 us (4%)
  matrix products  3.48 us (2%)
    ppermute x12, waiting for transfers between devices, ring(): lax.ppermute(value, axis, [(i, (i + shift) % size) for i in range(size)])  33.3 us
    ppermute x12, starting transfers between devices, ring(): lax.ppermute(value, axis, [(i, (i + shift) % size) for i in range(size)])  23.4 us
    all_gather x1, blocking collectives, local(): lax.all_gather(x_piece.astype(jnp.float16), ('xh', 'xl', 'core'), axis=0,...  21.3 us
    all_gather x1, blocking collectives, local(): panel = lax.all_gather(quantize(total), ('y', 'core'), axis=0)  20.9 us
    ppermute x6, starting transfers between devices, scatter_x(): lax.ppermute(piece, PLANE, plane_pairs((0, 2), shift))  17.6 us
    pallas_call x1, Pallas kernels, apply_update(): pl.pallas_call(update_kernel, grid_spec=pltpu.PrefetchScalarGridSpec(num_...  14.6 us
    pallas_call x2, Pallas kernels, pick(): pl.pallas_call(functools.partial(pick_kernel, rows, cols), grid_spec=pltp...  9.05 us
    ppermute x6, waiting for transfers between devices, scatter_x(): lax.ppermute(piece, PLANE, plane_pairs((0, 2), shift))  7.82 us
  transfers between devices with their start and end apart: 22, of which 8 were waited for; matrix products, arithmetic and copies ran while one was open for 12% of the time, Pallas kernels for 5%

profile of v7, /device:TPU:24, one launch (start us, length us, event | category | flops | bytes accessed | tf_op | source)
XLA Modules:
  0.0 199.6 jit_solution(13275088011580611809)
XLA Ops:
  6.5 0.9 copy-done
  7.4 0.6 constant_dynamic-slice_fusion.2
  8.8 0.7 pad_add_fusion.3.scalars
  9.4 4.4 %pick_columns.1 = (bf16[128,1024]{1,0:T(8,128)(2,1)}, bf16[128,1024]{1,0:T(8,128)(2,1)}, bf16[128,1024]{1,0:T(8,128)(2,1)}, bf16[128,1024]{1,0:T(8,128)(2,1)}) custom-call(s32[9]{0:T(128)} %pad_add_fusion.3.scalars, bf16[512,1664]{1,0:T(8,128)(2,1)} %src_ref.1), custom_call_target="tpu_custom_call" | custom-call | tf_op jit(solution)/shard_map/pick_columns/pallas_call | solution.py:48
  13.8 4.1 %collective-permute-start = (bf16[128,1024]{1,0:T(8,128)(2,1)}, bf16[128,1024]{1,0:T(8,128)(2,1)}, u32[]{:S(2)}, u32[]{:S(2)}) collective-permute-start(bf16[128,1024]{1,0:T(8,128)(2,1)} %get-tuple-element.32), channel_id=1, source_target_pairs={{0,16},{2,18},{4,20},{6,22},{8,24},{10,26},{12,28},{14,30},{1,17},... | collective-permute-start | bytes 786440 | tf_op jit(solution)/shard_map/ppermute | solution.py:65
  18.0 4.6 %collective-permute-start.1 = (bf16[128,1024]{1,0:T(8,128)(2,1)}, bf16[128,1024]{1,0:T(8,128)(2,1)}, u32[]{:S(2)}, u32[]{:S(2)}) collective-permute-start(bf16[128,1024]{1,0:T(8,128)(2,1)} %get-tuple-element.33), channel_id=1, source_target_pairs={{0,1},{2,3},{4,5},{6,7},{8,9},{10,11},{12,13},{14,15},{1,0},{3,2},... | collective-permute-start | bytes 786440 | tf_op jit(solution)/shard_map/ppermute | solution.py:65
  22.6 2.0 %collective-permute-start.2 = (bf16[128,1024]{1,0:T(8,128)(2,1)}, bf16[128,1024]{1,0:T(8,128)(2,1)}, u32[]{:S(2)}, u32[]{:S(2)}) collective-permute-start(bf16[128,1024]{1,0:T(8,128)(2,1)} %get-tuple-element.34), channel_id=1, source_target_pairs={{0,17},{2,19},{4,21},{6,23},{8,25},{10,27},{12,29},{14,31},{1,16},... | collective-permute-start | bytes 786440 | tf_op jit(solution)/shard_map/ppermute | solution.py:65
  24.6 1.4 copy.15
  26.1 0.1 collective-permute-start.5
  26.2 4.6 %pick_rows.1 = (bf16[1024,256]{1,0:T(8,128)(2,1)}, bf16[1024,256]{1,0:T(8,128)(2,1)}, bf16[1024,256]{1,0:T(8,128)(2,1)}, bf16[1024,256]{1,0:T(8,128)(2,1)}) custom-call(s32[9]{0:T(128)} %pad_add_fusion.3.scalars, bf16[1664,1024]{1,0:T(8,128)(2,1)} %src_ref.2), custom_call_target="tpu_custom_call" | custom-call | tf_op jit(solution)/shard_map/pick_rows/pallas_call | solution.py:48
  30.8 2.1 %collective-permute-start.6 = (bf16[1024,256]{1,0:T(8,128)(2,1)}, bf16[1024,256]{1,0:T(8,128)(2,1)}, u32[]{:S(2)}, u32[]{:S(2)}) collective-permute-start(bf16[1024,256]{1,0:T(8,128)(2,1)} %get-tuple-element.39), channel_id=1, source_target_pairs={{0,16},{2,18},{4,20},{6,22},{8,24},{10,26},{12,28},{14,30},{1,17},... | collective-permute-start | bytes 1572872 | tf_op jit(solution)/shard_map/ppermute | solution.py:65
  32.9 0.1 broadcast_bitcast_fusion.4
  33.1 2.7 %collective-permute-start.7 = (bf16[1024,256]{1,0:T(8,128)(2,1)}, bf16[1024,256]{1,0:T(8,128)(2,1)}, u32[]{:S(2)}, u32[]{:S(2)}) collective-permute-start(bf16[1024,256]{1,0:T(8,128)(2,1)} %get-tuple-element.40), channel_id=1, source_target_pairs={{0,1},{2,3},{4,5},{6,7},{8,9},{10,11},{12,13},{14,15},{1,0},{3,2},... | collective-permute-start | bytes 1572872 | tf_op jit(solution)/shard_map/ppermute | solution.py:65
  35.8 2.1 %collective-permute-start.8 = (bf16[1024,256]{1,0:T(8,128)(2,1)}, bf16[1024,256]{1,0:T(8,128)(2,1)}, u32[]{:S(2)}, u32[]{:S(2)}) collective-permute-start(bf16[1024,256]{1,0:T(8,128)(2,1)} %get-tuple-element.41), channel_id=1, source_target_pairs={{0,17},{2,19},{4,21},{6,23},{8,25},{10,27},{12,29},{14,31},{1,16},... | collective-permute-start | bytes 1572872 | tf_op jit(solution)/shard_map/ppermute | solution.py:65
  38.0 1.1 select_select_fusion.4
  39.1 8.6 %collective-permute-start.4 = (bf16[128,1024]{1,0:T(8,128)(2,1)S(1)}, bf16[128,1024]{1,0:T(8,128)(2,1)S(1)}, u32[]{:S(2)}, u32[]{:S(2)}) collective-permute-start(bf16[128,1024]{1,0:T(8,128)(2,1)S(1)} %select_select_fusion.4), channel_id=1, source_target_pairs={{0,10},{2,12},{4,14},{6,0},{8,2},{10,4},{12,6},{14,8},{1,11},{3,13... | collective-permute-start | bytes 786440 | tf_op jit(solution)/shard_map/ppermute | solution.py:24
  47.6 2.1 %collective-permute-start.3 = (bf16[128,1024]{1,0:T(8,128)(2,1)S(1)}, bf16[128,1024]{1,0:T(8,128)(2,1)S(1)}, u32[]{:S(2)}, u32[]{:S(2)}) collective-permute-start(bf16[128,1024]{1,0:T(8,128)(2,1)S(1)} %select_select_fusion.4), channel_id=1, source_target_pairs={{0,6},{2,8},{4,10},{6,12},{8,14},{10,0},{12,2},{14,4},{1,7},{3,9},... | collective-permute-start | bytes 786440 | tf_op jit(solution)/shard_map/ppermute | solution.py:24
  49.7 7.8 %collective-permute-done.7 = bf16[1024,256]{1,0:T(8,128)(2,1)} collective-permute-done((bf16[1024,256]{1,0:T(8,128)(2,1)}, bf16[1024,256]{1,0:T(8,128)(2,1)}, u32[]{:S(2)}, u32[]{:S(2)}) %collective-permute-start.7) | collective-permute-done | bytes 524320 | tf_op jit(solution)/shard_map/ppermute | solution.py:65
  57.5 2.3 %select_select_fusion.2 = bf16[1024,256]{1,0:T(8,128)(2,1)} fusion(bf16[1024,256]{1,0:T(8,128)(2,1)} %collective-permute-done.7, bf16[1024,256]{1,0:T(8,128)(2,1)} %collective-permute-done.8, bf16[1024,256]{1,0:T(8,128)(2,1)} %get-tuple-element.38, bf16[1024,256]{1,0:T(8,128)(2,1)} %collective-permute-done.6, ...), kind=kLoop, calls=%fused_computation.23 | loop fusion | flops 786432 | bytes 2622465 | tf_op jit(solution)/shard_map/jit(_where)/select_n | solution.py:71
  59.8 0.4 broadcast_select_fusion
  60.2 0.1 slice_dynamic-update-slice_fusion.6
  60.5 0.1 slice_dynamic-update-slice_fusion.3
  60.6 0.1 slice_dynamic-update-slice_fusion.1
  60.8 3.1 %collective-permute-done.4 = bf16[128,1024]{1,0:T(8,128)(2,1)S(1)} collective-permute-done((bf16[128,1024]{1,0:T(8,128)(2,1)S(1)}, bf16[128,1024]{1,0:T(8,128)(2,1)S(1)}, u32[]{:S(2)}, u32[]{:S(2)}) %collective-permute-start.4) | collective-permute-done | bytes 262176 | tf_op jit(solution)/shard_map/ppermute | solution.py:24
  63.9 5.5 %collective-permute-done.3 = bf16[128,1024]{1,0:T(8,128)(2,1)S(1)} collective-permute-done((bf16[128,1024]{1,0:T(8,128)(2,1)S(1)}, bf16[128,1024]{1,0:T(8,128)(2,1)S(1)}, u32[]{:S(2)}, u32[]{:S(2)}) %collective-permute-start.3) | collective-permute-done | bytes 262176 | tf_op jit(solution)/shard_map/ppermute | solution.py:24
  69.4 1.6 collective-permute-start.10
  71.0 0.5 collective-permute-start.9
  71.7 3.8 %collective-permute-start.13 = (bf16[1024,256]{1,0:T(8,128)(2,1)}, bf16[1024,256]{1,0:T(8,128)(2,1)}, u32[]{:S(2)}, u32[]{:S(2)}) collective-permute-start(bf16[1024,256]{1,0:T(8,128)(2,1)} %select_select_fusion.2), channel_id=1, source_target_pairs={{0,10},{2,12},{4,14},{6,0},{8,2},{10,4},{12,6},{14,8},{1,11},{3,13... | collective-permute-start | bytes 1572872 | tf_op jit(solution)/shard_map/ppermute | solution.py:24
  75.5 11.8 %collective-permute-done.10 = bf16[128,1024]{1,0:T(8,128)(2,1)S(1)} collective-permute-done((bf16[128,1024]{1,0:T(8,128)(2,1)S(1)}, bf16[128,1024]{1,0:T(8,128)(2,1)S(1)}, u32[]{:S(2)}, u32[]{:S(2)}) %collective-permute-start.10) | collective-permute-done | bytes 262176 | tf_op jit(solution)/shard_map/ppermute | solution.py:24
  87.3 1.4 collective-permute-done.9
  88.7 21.3 %all-gather.7 = f16[1024,1024]{1,0:T(8,128)(2,1)S(1)} all-gather(f16[128,1024]{1,0:T(8,128)(2,1)S(1)} %select_convert_fusion), channel_id=1, replica_groups=mesh['y'=4,'core'=2,'xl'=2,'z'=8,'xh'=2] {'xh','xl','core'}, dimensions={0}, use_global_device_ids=true | all-gather | bytes 2359296 | tf_op jit(solution)/shard_map/all_gather | solution.py:256
  110.0 3.5 %abs_reduce_fusion = (f32[832]{0:T(1024)S(1)}, f32[832,1024]{1,0:T(8,128)S(1)}) fusion(bf16[832,1024]{1,0:T(8,128)(2,1)} %bitcast.40, f16[1024,1024]{1,0:T(8,128)(2,1)S(1)} %all-gather.7), kind=kOutput, calls=%fused_computation.4 | convolution fusion | flops 1747582208 | bytes 7212288 | tf_op jit(solution)/shard_map/dot_general | solution.py:260
  113.6 0.1 reshape.325
  113.6 0.1 reshape.332
  113.7 0.3 convert_convert_fusion
  114.1 1.2 copy-done.5
  115.3 0.2 pad_add_fusion
  115.5 1.2 dynamic-slice_bitcast_fusion.2
  116.7 2.6 %collective-permute-start.17 = (s16[224,1024]{1,0:T(8,128)(2,1)}, s16[224,1024]{1,0:T(8,128)(2,1)}, u32[]{:S(2)}, u32[]{:S(2)}) collective-permute-start(s16[224,1024]{1,0:T(8,128)(2,1)} %get-tuple-element.66), channel_id=1, source_target_pairs={{0,128},{64,192},{128,0},{192,64},{1,129},{65,193},{129,1},{193,65... | collective-permute-start | bytes 1376264 | tf_op jit(solution)/shard_map/ppermute | solution.py:24
  119.3 0.2 select_reduce_fusion
  119.5 2.9 %fusion.25 = (bf16[1024,1024]{1,0:T(8,128)(2,1)S(1)}, f32[1024,1024]{1,0:T(8,128)}) fusion(s32[1024,1024]{1,0:T(8,128)S(1)} %copy-done.6, f32[8,1024]{1,0:T(8,128)S(1)} %select_reduce_fusion), kind=kLoop, calls=%fused_computation.99 | loop fusion | flops 4194304 | bytes 10518528 | tf_op jit(solution)/shard_map/convert_element_type | solution.py:293
  122.5 2.1 %fusion.base_ref = bf16[1664,1024]{1,0:T(8,128)(2,1)S(1)} fusion(bf16[1664,1024]{1,0:T(8,128)(2,1)S(1)} %copy-done.3, s32[]{:T(128)S(6)} %min.14, bf16[1024,1024]{1,0:T(8,128)(2,1)S(1)} %get-tuple-element.55, pred[1664]{0:T(1024)(128)(4,1)S(1)} %fusion.13), kind=kLoop, calls=%fused_computation.2 | loop fusion | flops 1703936 | bytes 8914564 | tf_op jit(solution)/shard_map/jit(_where)/select_n | solution.py:297
  124.6 1.7 select_select_fusion.1
  126.3 4.1 %collective-permute-start.15 = (bf16[1024,256]{1,0:T(8,128)(2,1)S(1)}, bf16[1024,256]{1,0:T(8,128)(2,1)S(1)}, u32[]{:S(2)}, u32[]{:S(2)}) collective-permute-start(bf16[1024,256]{1,0:T(8,128)(2,1)S(1)} %select_select_fusion.1), channel_id=1, source_target_pairs={{0,14},{2,0},{4,2},{6,4},{8,6},{10,8},{12,10},{14,12},{1,15},{3,1}... | collective-permute-start | bytes 1572872 | tf_op jit(solution)/shard_map/ppermute | solution.py:24
  130.5 1.4 constant_dynamic-slice_fusion.q_ref
  131.9 0.8 fusion.16
  132.8 8.4 %collective-permute-done.16 = s16[224,1024]{1,0:T(8,128)(2,1)} collective-permute-done((s16[224,1024]{1,0:T(8,128)(2,1)}, s16[224,1024]{1,0:T(8,128)(2,1)}, u32[]{:S(2)}, u32[]{:S(2)}) %collective-permute-start.16) | collective-permute-done | bytes 458784 | tf_op jit(solution)/shard_map/ppermute | solution.py:24
  141.1 0.7 fusion.19
  141.8 3.2 %collective-permute-done.14 = bf16[1024,256]{1,0:T(8,128)(2,1)S(1)} collective-permute-done((bf16[1024,256]{1,0:T(8,128)(2,1)S(1)}, bf16[1024,256]{1,0:T(8,128)(2,1)S(1)}, u32[]{:S(2)}, u32[]{:S(2)}) %collective-permute-start.14) | collective-permute-done | bytes 524320 | tf_op jit(solution)/shard_map/ppermute | solution.py:24
  145.0 0.3 select_select_fusion.w_ref
  145.4 0.7 multiply_exponential_fusion.3
  146.1 2.6 %block_error.1 = f32[1024,256]{1,0:T(8,128)S(1)} custom-call(f32[1024,1024]{1,0:T(8,128)S(1)} %copy-done.2, bf16[1024,256]{1,0:T(8,128)(2,1)S(1)} %select_select_fusion.w_ref, f32[1024,256]{1,0:T(8,128)S(1)} %constant_dynamic-slice_fusion.q_ref), custom_call_target="tpu_custom_call" | custom-call | flops 1610612736 | bytes 4194304 | tf_op jit(solution)/shard_map/block_error/pallas_call | solution.py:130
  148.8 0.1 multiply_round-nearest-even_fusion
  148.9 0.1 fusion.3.e0
  149.0 2.1 %fusion.5 = f32[208,1024]{1,0:T(8,128)S(1)} fusion(f32[4,208,1024]{2,1,0:T(8,128)} %bitcast.39, s32[]{:T(128)S(6)} %select_n.177, s16[224,1024]{1,0:T(8,128)(2,1)} %collective-permute-done.17, s16[224,1024]{1,0:T(8,128)(2,1)} %collective-permute-done.16, f32[208]{0:T(256)S(1)} %bitcast.41, f32[208]{0:T(256)S(1)} %bitcast.42, f32[208]{0:T(256)S(1)} %bitcast.43, ...), kind=kLoop, calls=%fused_computation.14 | loop fusion | flops 1916928 | bytes 2984388 | tf_op jit(solution)/shard_map/add | solution.py:275
  151.0 1.9 collective-permute-start.20
  152.9 0.8 collective-permute-start.19
  153.7 0.3 collective-permute-start.18
  154.0 0.1 abs_reduce_fusion.2
  154.2 0.2 convert_convert_fusion.1
  154.4 20.9 %all-gather.8 = s16[1792,1024]{1,0:T(8,128)(2,1)S(1)} all-gather(s16[224,1024]{1,0:T(8,128)(2,1)S(1)} %pad_add_fusion.1), channel_id=3, replica_groups=mesh['y'=4,'core'=2,'xl'=2,'z'=8,'xh'=2] {'y','core'}, dimensions={0}, use_global_device_ids=true | all-gather | bytes 4128768 | tf_op jit(solution)/shard_map/all_gather | solution.py:284
  175.3 0.3 mul.219.scale_ref
  175.6 2.5 %collective-permute-done.18.e1 = s16[1040,256]{1,0:T(8,128)(2,1)S(1)} collective-permute-done((s16[1040,256]{1,0:T(8,128)(2,1)S(1)}, s16[1040,256]{1,0:T(8,128)(2,1)S(1)}, u32[]{:S(2)}, u32[]{:S(2)}) %collective-permute-start.18) | collective-permute-done | bytes 532512 | tf_op jit(solution)/shard_map/ppermute | solution.py:290
  178.1 14.6 %apply_update.1 = bf16[1664,1024]{1,0:T(8,128)(2,1)} custom-call(s32[2]{0:T(128)S(1)} %pad_add_fusion.2.scalars, s16[4,2,224,1024]{3,2,1,0:T(8,128)(2,1)S(1)} %bitcast.37, f32[4,2,208,1]{3,2,1,0:T(8,128)S(1)} %mul.219.scale_ref, s16[1040,256]{1,0:T(8,128)(2,1)S(1)} %fusion.3.e0, s16[1040,256]{1,0:T(8,128)(2,1)S(1)} %collective-permute-done.18.e1, ...), custom_call_target="tpu_custom_call" | custom-call | flops 10468982784 | bytes 12320768 | tf_op jit(solution)/shard_map/apply_update/pallas_call | solution.py:180
  (63 shorter events, 1.2 us)
Async XLA Ops:
  6.5 0.9 copy-start
  6.5 18.1 %copy-start.4 = (bf16[512,1664]{1,0:T(8,128)(2,1)S(1)}, bf16[512,1664]{1,0:T(8,128)(2,1)}, u32[]{:S(2)}) copy-start(bf16[512,1664]{1,0:T(8,128)(2,1)} %src_ref.1) | copy-start | bytes 5111812
  6.5 118.1 %all-gather.6.cloned.1.call-start = ((), (), s32[]{:S(2)}) async-start(), calls=%async_computation | async-start | bytes 4259840 | tf_op jit(solution)/shard_map/all_gather | solution.py:230
  13.8 19.2 %collective-permute-start = (bf16[128,1024]{1,0:T(8,128)(2,1)}, bf16[128,1024]{1,0:T(8,128)(2,1)}, u32[]{:S(2)}, u32[]{:S(2)}) collective-permute-start(bf16[128,1024]{1,0:T(8,128)(2,1)} %get-tuple-element.32), channel_id=1, source_target_pairs={{0,16},{2,18},{4,20},{6,22},{8,24},{10,26},{12,28},{14,30},{1,17},... | collective-permute-start | bytes 786440 | tf_op jit(solution)/shard_map/ppermute | solution.py:65
  18.0 17.8 %collective-permute-start.1 = (bf16[128,1024]{1,0:T(8,128)(2,1)}, bf16[128,1024]{1,0:T(8,128)(2,1)}, u32[]{:S(2)}, u32[]{:S(2)}) collective-permute-start(bf16[128,1024]{1,0:T(8,128)(2,1)} %get-tuple-element.33), channel_id=1, source_target_pairs={{0,1},{2,3},{4,5},{6,7},{8,9},{10,11},{12,13},{14,15},{1,0},{3,2},... | collective-permute-start | bytes 786440 | tf_op jit(solution)/shard_map/ppermute | solution.py:65
  22.6 15.4 %collective-permute-start.2 = (bf16[128,1024]{1,0:T(8,128)(2,1)}, bf16[128,1024]{1,0:T(8,128)(2,1)}, u32[]{:S(2)}, u32[]{:S(2)}) collective-permute-start(bf16[128,1024]{1,0:T(8,128)(2,1)} %get-tuple-element.34), channel_id=1, source_target_pairs={{0,17},{2,19},{4,21},{6,23},{8,25},{10,27},{12,29},{14,31},{1,16},... | collective-permute-start | bytes 786440 | tf_op jit(solution)/shard_map/ppermute | solution.py:65
  26.1 33.7 %collective-permute-start.5 = (bf16[512,832]{0,1:T(8,128)(2,1)S(1)}, bf16[512,832]{0,1:T(8,128)(2,1)S(1)}, u32[]{:S(2)}, u32[]{:S(2)}) collective-permute-start(bf16[512,832]{0,1:T(8,128)(2,1)S(1)} %constant_dynamic-slice_fusion.1), channel_id=1, source_target_pairs={{0,32},{32,0},{1,33},{33,1},{2,34},{34,2},{3,35},{35,3},{4,36},{36... | collective-permute-start | bytes 2555912 | tf_op jit(solution)/shard_map/ppermute | solution.py:24
  30.8 16.8 %collective-permute-start.6 = (bf16[1024,256]{1,0:T(8,128)(2,1)}, bf16[1024,256]{1,0:T(8,128)(2,1)}, u32[]{:S(2)}, u32[]{:S(2)}) collective-permute-start(bf16[1024,256]{1,0:T(8,128)(2,1)} %get-tuple-element.39), channel_id=1, source_target_pairs={{0,16},{2,18},{4,20},{6,22},{8,24},{10,26},{12,28},{14,30},{1,17},... | collective-permute-start | bytes 1572872 | tf_op jit(solution)/shard_map/ppermute | solution.py:65
  33.1 24.4 %collective-permute-start.7 = (bf16[1024,256]{1,0:T(8,128)(2,1)}, bf16[1024,256]{1,0:T(8,128)(2,1)}, u32[]{:S(2)}, u32[]{:S(2)}) collective-permute-start(bf16[1024,256]{1,0:T(8,128)(2,1)} %get-tuple-element.40), channel_id=1, source_target_pairs={{0,1},{2,3},{4,5},{6,7},{8,9},{10,11},{12,13},{14,15},{1,0},{3,2},... | collective-permute-start | bytes 1572872 | tf_op jit(solution)/shard_map/ppermute | solution.py:65
  35.8 21.7 %collective-permute-start.8 = (bf16[1024,256]{1,0:T(8,128)(2,1)}, bf16[1024,256]{1,0:T(8,128)(2,1)}, u32[]{:S(2)}, u32[]{:S(2)}) collective-permute-start(bf16[1024,256]{1,0:T(8,128)(2,1)} %get-tuple-element.41), channel_id=1, source_target_pairs={{0,17},{2,19},{4,21},{6,23},{8,25},{10,27},{12,29},{14,31},{1,16},... | collective-permute-start | bytes 1572872 | tf_op jit(solution)/shard_map/ppermute | solution.py:65
  39.1 24.8 %collective-permute-start.4 = (bf16[128,1024]{1,0:T(8,128)(2,1)S(1)}, bf16[128,1024]{1,0:T(8,128)(2,1)S(1)}, u32[]{:S(2)}, u32[]{:S(2)}) collective-permute-start(bf16[128,1024]{1,0:T(8,128)(2,1)S(1)} %select_select_fusion.4), channel_id=1, source_target_pairs={{0,10},{2,12},{4,14},{6,0},{8,2},{10,4},{12,6},{14,8},{1,11},{3,13... | collective-permute-start | bytes 786440 | tf_op jit(solution)/shard_map/ppermute | solution.py:24
  47.6 21.8 %collective-permute-start.3 = (bf16[128,1024]{1,0:T(8,128)(2,1)S(1)}, bf16[128,1024]{1,0:T(8,128)(2,1)S(1)}, u32[]{:S(2)}, u32[]{:S(2)}) collective-permute-start(bf16[128,1024]{1,0:T(8,128)(2,1)S(1)} %select_select_fusion.4), channel_id=1, source_target_pairs={{0,6},{2,8},{4,10},{6,12},{8,14},{10,0},{12,2},{14,4},{1,7},{3,9},... | collective-permute-start | bytes 786440 | tf_op jit(solution)/shard_map/ppermute | solution.py:24
  60.8 8.6 %copy-start.8 = (bf16[1024,832]{0,1:T(8,128)(2,1)}, bf16[1024,832]{0,1:T(8,128)(2,1)S(1)}, u32[]{:S(2)}) copy-start(bf16[1024,832]{0,1:T(8,128)(2,1)S(1)} %slice_dynamic-update-slice_fusion) | copy-start | bytes 5111812
  69.4 17.8 %collective-permute-start.10 = (bf16[128,1024]{1,0:T(8,128)(2,1)S(1)}, bf16[128,1024]{1,0:T(8,128)(2,1)S(1)}, u32[]{:S(2)}, u32[]{:S(2)}) collective-permute-start(bf16[128,1024]{1,0:T(8,128)(2,1)S(1)} %select_select_fusion.3), channel_id=1, source_target_pairs={{0,14},{2,0},{4,2},{6,4},{8,6},{10,8},{12,10},{14,12},{1,15},{3,1}... | collective-permute-start | bytes 786440 | tf_op jit(solution)/shard_map/ppermute | solution.py:24
  71.0 17.6 %collective-permute-start.9 = (bf16[128,1024]{1,0:T(8,128)(2,1)S(1)}, bf16[128,1024]{1,0:T(8,128)(2,1)S(1)}, u32[]{:S(2)}, u32[]{:S(2)}) collective-permute-start(bf16[128,1024]{1,0:T(8,128)(2,1)S(1)} %select_select_fusion.3), channel_id=1, source_target_pairs={{0,2},{2,4},{4,6},{6,8},{8,10},{10,12},{12,14},{14,0},{1,3},{3,5},... | collective-permute-start | bytes 786440 | tf_op jit(solution)/shard_map/ppermute | solution.py:24
  71.7 52.9 %collective-permute-start.13 = (bf16[1024,256]{1,0:T(8,128)(2,1)}, bf16[1024,256]{1,0:T(8,128)(2,1)}, u32[]{:S(2)}, u32[]{:S(2)}) collective-permute-start(bf16[1024,256]{1,0:T(8,128)(2,1)} %select_select_fusion.2), channel_id=1, source_target_pairs={{0,10},{2,12},{4,14},{6,0},{8,2},{10,4},{12,6},{14,8},{1,11},{3,13... | collective-permute-start | bytes 1572872 | tf_op jit(solution)/shard_map/ppermute | solution.py:24
  75.5 49.1 %collective-permute-start.12 = (bf16[1024,256]{1,0:T(8,128)(2,1)}, bf16[1024,256]{1,0:T(8,128)(2,1)}, u32[]{:S(2)}, u32[]{:S(2)}) collective-permute-start(bf16[1024,256]{1,0:T(8,128)(2,1)} %select_select_fusion.2), channel_id=1, source_target_pairs={{0,6},{2,8},{4,10},{6,12},{8,14},{10,0},{12,2},{14,4},{1,7},{3,9},... | collective-permute-start | bytes 1572872 | tf_op jit(solution)/shard_map/ppermute | solution.py:24
  113.5 1.8 copy-start.5
  115.3 4.2 %copy-start.6 = (s32[1024,1024]{1,0:T(8,128)S(1)}, s32[1024,1024]{1,0:T(8,128)}, u32[]{:S(2)}) copy-start(s32[1024,1024]{1,0:T(8,128)} %param.9) | copy-start | bytes 12582916
  115.4 3.9 %copy-start.7 = (s32[8,1024]{1,0:T(8,128)S(1)}, s32[8,1024]{1,0:T(8,128)}, u32[]{:S(2)}) copy-start(s32[8,1024]{1,0:T(8,128)} %param.10) | copy-start | bytes 98308
  115.5 3.9 %copy-start.9 = (f32[16]{0:T(128)S(1)}, f32[16]{0:T(128)}, u32[]{:S(2)}) copy-start(f32[16]{0:T(128)} %param.11) | copy-start | bytes 196
  116.7 28.7 %collective-permute-start.11 = (s16[224,1024]{1,0:T(8,128)(2,1)}, s16[224,1024]{1,0:T(8,128)(2,1)}, u32[]{:S(2)}, u32[]{:S(2)}) collective-permute-start(s16[224,1024]{1,0:T(8,128)(2,1)} %get-tuple-element.65), channel_id=1, source_target_pairs={{0,64},{64,128},{128,192},{192,0},{1,65},{65,129},{129,193},{193,1... | collective-permute-start | bytes 1376264 | tf_op jit(solution)/shard_map/ppermute | solution.py:24
  116.7 15.2 %collective-permute-start.17 = (s16[224,1024]{1,0:T(8,128)(2,1)}, s16[224,1024]{1,0:T(8,128)(2,1)}, u32[]{:S(2)}, u32[]{:S(2)}) collective-permute-start(s16[224,1024]{1,0:T(8,128)(2,1)} %get-tuple-element.66), channel_id=1, source_target_pairs={{0,128},{64,192},{128,0},{192,64},{1,129},{65,193},{129,1},{193,65... | collective-permute-start | bytes 1376264 | tf_op jit(solution)/shard_map/ppermute | solution.py:24
  119.3 21.8 %collective-permute-start.16 = (s16[224,1024]{1,0:T(8,128)(2,1)}, s16[224,1024]{1,0:T(8,128)(2,1)}, u32[]{:S(2)}, u32[]{:S(2)}) collective-permute-start(s16[224,1024]{1,0:T(8,128)(2,1)} %get-tuple-element.67), channel_id=1, source_target_pairs={{0,192},{64,0},{128,64},{192,128},{1,193},{65,1},{129,65},{193,129... | collective-permute-start | bytes 1376264 | tf_op jit(solution)/shard_map/ppermute | solution.py:24
  119.5 2.9 %copy-start.3 = (bf16[1664,1024]{1,0:T(8,128)(2,1)S(1)}, bf16[1664,1024]{1,0:T(8,128)(2,1)}, u32[]{:S(2)}) copy-start(bf16[1664,1024]{1,0:T(8,128)(2,1)} %src_ref.2) | copy-start | bytes 10223620
  126.3 15.5 %collective-permute-start.15 = (bf16[1024,256]{1,0:T(8,128)(2,1)S(1)}, bf16[1024,256]{1,0:T(8,128)(2,1)S(1)}, u32[]{:S(2)}, u32[]{:S(2)}) collective-permute-start(bf16[1024,256]{1,0:T(8,128)(2,1)S(1)} %select_select_fusion.1), channel_id=1, source_target_pairs={{0,14},{2,0},{4,2},{6,4},{8,6},{10,8},{12,10},{14,12},{1,15},{3,1}... | collective-permute-start | bytes 1572872 | tf_op jit(solution)/shard_map/ppermute | solution.py:24
  130.5 14.6 %collective-permute-start.14 = (bf16[1024,256]{1,0:T(8,128)(2,1)S(1)}, bf16[1024,256]{1,0:T(8,128)(2,1)S(1)}, u32[]{:S(2)}, u32[]{:S(2)}) collective-permute-start(bf16[1024,256]{1,0:T(8,128)(2,1)S(1)} %select_select_fusion.1), channel_id=1, source_target_pairs={{0,2},{2,4},{4,6},{6,8},{8,10},{10,12},{12,14},{14,0},{1,3},{3,5},... | collective-permute-start | bytes 1572872 | tf_op jit(solution)/shard_map/ppermute | solution.py:24
  130.5 15.6 %copy-start.2 = (f32[1024,1024]{1,0:T(8,128)S(1)}, f32[1024,1024]{1,0:T(8,128)}, u32[]{:S(2)}) copy-start(f32[1024,1024]{1,0:T(8,128)} %all-gather.6.cloned.1.call-done.inv_ref) | copy-start | bytes 12582916
  151.0 24.6 %collective-permute-start.20 = (s16[1040,256]{1,0:T(8,128)(2,1)S(1)}, s16[1040,256]{1,0:T(8,128)(2,1)S(1)}, u32[]{:S(2)}, u32[]{:S(2)}) collective-permute-start(s16[1040,256]{1,0:T(8,128)(2,1)S(1)} %fusion.3.e0), channel_id=1, source_target_pairs={{0,17},{2,19},{4,21},{6,23},{8,25},{10,27},{12,29},{14,31},{16,0},... | collective-permute-start | bytes 1597448 | tf_op jit(solution)/shard_map/ppermute | solution.py:290
  152.9 22.7 %collective-permute-start.19 = (s16[1040,256]{1,0:T(8,128)(2,1)S(1)}, s16[1040,256]{1,0:T(8,128)(2,1)S(1)}, u32[]{:S(2)}, u32[]{:S(2)}) collective-permute-start(s16[1040,256]{1,0:T(8,128)(2,1)S(1)} %fusion.3.e0), channel_id=1, source_target_pairs={{0,1},{2,3},{4,5},{6,7},{8,9},{10,11},{12,13},{14,15},{16,17},{18,... | collective-permute-start | bytes 1597448 | tf_op jit(solution)/shard_map/ppermute | solution.py:290
  153.7 24.4 %collective-permute-start.18 = (s16[1040,256]{1,0:T(8,128)(2,1)S(1)}, s16[1040,256]{1,0:T(8,128)(2,1)S(1)}, u32[]{:S(2)}, u32[]{:S(2)}) collective-permute-start(s16[1040,256]{1,0:T(8,128)(2,1)S(1)} %fusion.3.e0), channel_id=1, source_target_pairs={{0,16},{2,18},{4,20},{6,22},{8,24},{10,26},{12,28},{14,30},{16,1},... | collective-permute-start | bytes 1597448 | tf_op jit(solution)/shard_map/ppermute | solution.py:290
  178.1 14.6 %copy-start.1 = (f32[32,1024]{1,0:T(8,128)S(1)}, f32[32,1024]{1,0:T(8,128)}, u32[]{:S(2)}) copy-start(f32[32,1024]{1,0:T(8,128)} %param.12) | copy-start | bytes 393220
Sparse Core Ops, SparseCore 0:
  10.1 96.7 all-gather.5

commit v8 on v7

--- a/solution.py
+++ b/solution.py
@@ -250,8 +250,8 @@
     x_piece = scatter_x(x_pieces, x, lanes(from_low))
     w_piece = scatter_x(w_pieces, x, sublanes(from_low))
     x_piece, x_rows = reach_far(x_piece, lanes(distance), (x_rows,))
+    x_piece = reach_near(x_piece, lanes(distance))
     x_piece, w_piece = lax.optimization_barrier((x_piece, w_piece))
-    x_piece = reach_near(x_piece, lanes(distance))
 
     x_block = lax.all_gather(
         x_piece.astype(jnp.float16), ("xh", "xl", "core"), axis=0, tiled=True

time: 203 us -> 196 us (0.966)
  waiting for transfers between devices: 43.7 us -> 51.5 us
  starting transfers between devices: 44 us -> 37.6 us
  blocking collectives: 42.2 us -> 37.8 us
    ppermute x12, waiting for transfers between devices: 33.3 us -> 49 us  [ring(): lax.ppermute(value, axis, [(i, (i + shift) % size) for i in range(size)])]
    ppermute x6, waiting for transfers between devices: 7.82 us -> 0.02 us  [scatter_x(): lax.ppermute(piece, PLANE, plane_pairs((0, 2), shift))]
    ppermute x12, starting transfers between devices: 23.4 us -> 17.1 us  [ring(): lax.ppermute(value, axis, [(i, (i + shift) % size) for i in range(size)])]
    all_gather x1, blocking collectives: 21.3 us -> 18.7 us  [local(): lax.all_gather(x_piece.astype(jnp.float16), ('xh', 'xl', 'core'), axis=0,...]
  transfers between devices with their start and end apart: 22 -> 22, of which waited for: 8 -> 9; matrix products, arithmetic and copies ran while one was open for 12% -> 11% of each run, Pallas kernels for 5% -> 5%
where the time goes in v8:
time: 196 us; the launch traced here: 194 us
  waiting for transfers between devices  51.5 us (26%)
  blocking collectives  37.8 us (19%)
  starting transfers between devices  37.6 us (19%)
  Pallas kernels  26.4 us (13%)
  other arithmetic  16.2 us (8%)
  between operations  14.5 us (7%)
  local copies, waits for them, and re-layouts  8.14 us (4%)
  matrix products  2.02 us (1%)
    ppermute x12, waiting for transfers between devices, ring(): lax.ppermute(value, axis, [(i, (i + shift) % size) for i in range(size)])  49 us
    all_gather x1, blocking collectives, local(): panel = lax.all_gather(quantize(total), ('y', 'core'), axis=0)  19.1 us
    all_gather x1, blocking collectives, local(): lax.all_gather(x_piece.astype(jnp.float16), ('xh', 'xl', 'core'), axis=0,...  18.7 us
    ppermute x12, starting transfers between devices, ring(): lax.ppermute(value, axis, [(i, (i + shift) % size) for i in range(size)])  17.1 us
    ppermute x6, starting transfers between devices, scatter_x(): lax.ppermute(piece, PLANE, plane_pairs((0, 2), shift))  16.9 us
    pallas_call x1, Pallas kernels, apply_update(): pl.pallas_call(update_kernel, grid_spec=pltpu.PrefetchScalarGridSpec(num_...  14.6 us
    pallas_call x2, Pallas kernels, pick(): pl.pallas_call(functools.partial(pick_kernel, rows, cols), grid_spec=pltp...  9.03 us
  transfers between devices with their start and end apart: 22, of which 9 were waited for; matrix products, arithmetic and copies ran while one was open for 11% of the time, Pallas kernels for 5%

profile of v8, /device:TPU:24, one launch (start us, length us, event | category | flops | bytes accessed | tf_op | source)
XLA Modules:
  0.0 194.1 jit_solution(7170548496917882020)
XLA Ops:
  6.5 0.9 copy-done
  7.4 0.6 constant_dynamic-slice_fusion.2
  8.8 0.6 pad_add_fusion.3.scalars
  9.4 4.4 %pick_columns.1 = (bf16[128,1024]{1,0:T(8,128)(2,1)}, bf16[128,1024]{1,0:T(8,128)(2,1)}, bf16[128,1024]{1,0:T(8,128)(2,1)}, bf16[128,1024]{1,0:T(8,128)(2,1)}) custom-call(s32[9]{0:T(128)} %pad_add_fusion.3.scalars, bf16[512,1664]{1,0:T(8,128)(2,1)} %src_ref.1), custom_call_target="tpu_custom_call" | custom-call | tf_op jit(solution)/shard_map/pick_columns/pallas_call | solution.py:48
  13.8 4.1 %collective-permute-start = (bf16[128,1024]{1,0:T(8,128)(2,1)}, bf16[128,1024]{1,0:T(8,128)(2,1)}, u32[]{:S(2)}, u32[]{:S(2)}) collective-permute-start(bf16[128,1024]{1,0:T(8,128)(2,1)} %get-tuple-element.32), channel_id=1, source_target_pairs={{0,16},{2,18},{4,20},{6,22},{8,24},{10,26},{12,28},{14,30},{1,17},... | collective-permute-start | bytes 786440 | tf_op jit(solution)/shard_map/ppermute | solution.py:65
  17.9 4.6 %collective-permute-start.1 = (bf16[128,1024]{1,0:T(8,128)(2,1)}, bf16[128,1024]{1,0:T(8,128)(2,1)}, u32[]{:S(2)}, u32[]{:S(2)}) collective-permute-start(bf16[128,1024]{1,0:T(8,128)(2,1)} %get-tuple-element.33), channel_id=1, source_target_pairs={{0,1},{2,3},{4,5},{6,7},{8,9},{10,11},{12,13},{14,15},{1,0},{3,2},... | collective-permute-start | bytes 786440 | tf_op jit(solution)/shard_map/ppermute | solution.py:65
  22.5 2.0 %collective-permute-start.2 = (bf16[128,1024]{1,0:T(8,128)(2,1)}, bf16[128,1024]{1,0:T(8,128)(2,1)}, u32[]{:S(2)}, u32[]{:S(2)}) collective-permute-start(bf16[128,1024]{1,0:T(8,128)(2,1)} %get-tuple-element.34), channel_id=1, source_target_pairs={{0,17},{2,19},{4,21},{6,23},{8,25},{10,27},{12,29},{14,31},{1,16},... | collective-permute-start | bytes 786440 | tf_op jit(solution)/shard_map/ppermute | solution.py:65
  24.6 1.4 copy.15
  26.0 0.1 collective-permute-start.5
  26.1 4.6 %pick_rows.1 = (bf16[1024,256]{1,0:T(8,128)(2,1)}, bf16[1024,256]{1,0:T(8,128)(2,1)}, bf16[1024,256]{1,0:T(8,128)(2,1)}, bf16[1024,256]{1,0:T(8,128)(2,1)}) custom-call(s32[9]{0:T(128)} %pad_add_fusion.3.scalars, bf16[1664,1024]{1,0:T(8,128)(2,1)} %src_ref.2), custom_call_target="tpu_custom_call" | custom-call | tf_op jit(solution)/shard_map/pick_rows/pallas_call | solution.py:48
  30.8 2.1 %collective-permute-start.8 = (bf16[1024,256]{1,0:T(8,128)(2,1)}, bf16[1024,256]{1,0:T(8,128)(2,1)}, u32[]{:S(2)}, u32[]{:S(2)}) collective-permute-start(bf16[1024,256]{1,0:T(8,128)(2,1)} %get-tuple-element.39), channel_id=1, source_target_pairs={{0,16},{2,18},{4,20},{6,22},{8,24},{10,26},{12,28},{14,30},{1,17},... | collective-permute-start | bytes 1572872 | tf_op jit(solution)/shard_map/ppermute | solution.py:65
  33.2 2.7 %collective-permute-start.9 = (bf16[1024,256]{1,0:T(8,128)(2,1)}, bf16[1024,256]{1,0:T(8,128)(2,1)S(1)}, u32[]{:S(2)}, u32[]{:S(2)}) collective-permute-start(bf16[1024,256]{1,0:T(8,128)(2,1)} %get-tuple-element.40), channel_id=1, source_target_pairs={{0,1},{2,3},{4,5},{6,7},{8,9},{10,11},{12,13},{14,15},{1,0},{3,2},... | collective-permute-start | bytes 1572872 | tf_op jit(solution)/shard_map/ppermute | solution.py:65
  36.0 1.3 collective-permute-start.10
  37.3 1.1 select_select_fusion.5
  38.4 6.8 %collective-permute-start.4 = (bf16[128,1024]{1,0:T(8,128)(2,1)S(1)}, bf16[128,1024]{1,0:T(8,128)(2,1)S(1)}, u32[]{:S(2)}, u32[]{:S(2)}) collective-permute-start(bf16[128,1024]{1,0:T(8,128)(2,1)S(1)} %select_select_fusion.5), channel_id=1, source_target_pairs={{0,10},{2,12},{4,14},{6,0},{8,2},{10,4},{12,6},{14,8},{1,11},{3,13... | collective-permute-start | bytes 786440 | tf_op jit(solution)/shard_map/ppermute | solution.py:24
  45.2 0.4 broadcast_select_fusion
  45.7 0.1 slice_dynamic-update-slice_fusion.6
  45.9 0.1 slice_dynamic-update-slice_fusion.4
  46.3 16.6 %collective-permute-done.4 = bf16[128,1024]{1,0:T(8,128)(2,1)S(1)} collective-permute-done((bf16[128,1024]{1,0:T(8,128)(2,1)S(1)}, bf16[128,1024]{1,0:T(8,128)(2,1)S(1)}, u32[]{:S(2)}, u32[]{:S(2)}) %collective-permute-start.4) | collective-permute-done | bytes 262176 | tf_op jit(solution)/shard_map/ppermute | solution.py:24
  62.9 4.3 %collective-permute-done.3 = bf16[128,1024]{1,0:T(8,128)(2,1)S(1)} collective-permute-done((bf16[128,1024]{1,0:T(8,128)(2,1)S(1)}, bf16[128,1024]{1,0:T(8,128)(2,1)S(1)}, u32[]{:S(2)}, u32[]{:S(2)}) %collective-permute-start.3) | collective-permute-done | bytes 262176 | tf_op jit(solution)/shard_map/ppermute | solution.py:24
  67.2 0.5 collective-permute-start.7
  67.7 1.6 collective-permute-start.6
  69.4 1.1 select_select_fusion.2
  70.4 7.1 %collective-permute-done.7 = bf16[128,1024]{1,0:T(8,128)(2,1)S(1)} collective-permute-done((bf16[128,1024]{1,0:T(8,128)(2,1)S(1)}, bf16[128,1024]{1,0:T(8,128)(2,1)S(1)}, u32[]{:S(2)}, u32[]{:S(2)}) %collective-permute-start.7) | collective-permute-done | bytes 262176 | tf_op jit(solution)/shard_map/ppermute | solution.py:24
  77.6 1.0 collective-permute-start.13
  78.6 2.9 %collective-permute-start.12 = (bf16[1024,256]{1,0:T(8,128)(2,1)}, bf16[1024,256]{1,0:T(8,128)(2,1)}, u32[]{:S(2)}, u32[]{:S(2)}) collective-permute-start(bf16[1024,256]{1,0:T(8,128)(2,1)} %select_select_fusion.2), channel_id=1, source_target_pairs={{0,6},{2,8},{4,10},{6,12},{8,14},{10,0},{12,2},{14,4},{1,7},{3,9},... | collective-permute-start | bytes 1572872 | tf_op jit(solution)/shard_map/ppermute | solution.py:24
  81.5 18.7 %all-gather.7 = f16[1024,1024]{1,0:T(8,128)(2,1)S(1)} all-gather(f16[128,1024]{1,0:T(8,128)(2,1)S(1)} %convert_element_type.102), channel_id=1, replica_groups=mesh['y'=4,'core'=2,'xl'=2,'z'=8,'xh'=2] {'xh','xl','core'}, dimensions={0}, use_global_device_ids=true | all-gather | bytes 2359296 | tf_op jit(solution)/shard_map/all_gather | solution.py:256
  100.2 2.0 %abs_reduce_fusion = (f32[832]{0:T(1024)S(1)}, f32[832,1024]{1,0:T(8,128)S(1)}) fusion(bf16[832,1024]{1,0:T(8,128)(2,1)S(1)} %bitcast.40, f16[1024,1024]{1,0:T(8,128)(2,1)S(1)} %all-gather.7), kind=kOutput, calls=%fused_computation.4 | convolution fusion | flops 1747582208 | bytes 7212288 | tf_op jit(solution)/shard_map/dot_general | solution.py:260
  102.2 0.1 reshape.325
  102.3 0.1 reshape.332
  102.4 0.4 convert_convert_fusion
  102.8 1.2 copy-done.5
  104.0 0.2 pad_add_fusion
  104.2 1.2 dynamic-slice_bitcast_fusion.2
  105.4 0.9 collective-permute-start.17
  106.3 1.1 collective-permute-start.16
  107.4 0.2 select_reduce_fusion
  107.6 2.9 %fusion.25 = (bf16[1024,1024]{1,0:T(8,128)(2,1)S(1)}, f32[1024,1024]{1,0:T(8,128)}) fusion(s32[1024,1024]{1,0:T(8,128)S(1)} %copy-done.6, f32[8,1024]{1,0:T(8,128)S(1)} %select_reduce_fusion), kind=kLoop, calls=%fused_computation.99 | loop fusion | flops 4194304 | bytes 10518528 | tf_op jit(solution)/shard_map/convert_element_type | solution.py:293
  110.6 2.1 %fusion.base_ref = bf16[1664,1024]{1,0:T(8,128)(2,1)S(1)} fusion(bf16[1664,1024]{1,0:T(8,128)(2,1)S(1)} %copy-done.3, s32[]{:T(128)S(6)} %min.14, bf16[1024,1024]{1,0:T(8,128)(2,1)S(1)} %get-tuple-element.55, pred[1664]{0:T(1024)(128)(4,1)S(1)} %fusion.13), kind=kLoop, calls=%fused_computation.2 | loop fusion | flops 1703936 | bytes 8914564 | tf_op jit(solution)/shard_map/jit(_where)/select_n | solution.py:297
  112.7 6.4 %collective-permute-done.13 = bf16[1024,256]{1,0:T(8,128)(2,1)} collective-permute-done((bf16[1024,256]{1,0:T(8,128)(2,1)}, bf16[1024,256]{1,0:T(8,128)(2,1)}, u32[]{:S(2)}, u32[]{:S(2)}) %collective-permute-start.13) | collective-permute-done | bytes 524320 | tf_op jit(solution)/shard_map/ppermute | solution.py:24
  119.1 4.5 %collective-permute-done.12 = bf16[1024,256]{1,0:T(8,128)(2,1)} collective-permute-done((bf16[1024,256]{1,0:T(8,128)(2,1)}, bf16[1024,256]{1,0:T(8,128)(2,1)}, u32[]{:S(2)}, u32[]{:S(2)}) %collective-permute-start.12) | collective-permute-done | bytes 524320 | tf_op jit(solution)/shard_map/ppermute | solution.py:24
  123.7 1.7 select_select_fusion.1
  125.4 0.1 collective-permute-start.15
  125.5 2.0 %collective-permute-start.14 = (bf16[1024,256]{1,0:T(8,128)(2,1)S(1)}, bf16[1024,256]{1,0:T(8,128)(2,1)S(1)}, u32[]{:S(2)}, u32[]{:S(2)}) collective-permute-start(bf16[1024,256]{1,0:T(8,128)(2,1)S(1)} %select_select_fusion.1), channel_id=1, source_target_pairs={{0,2},{2,4},{4,6},{6,8},{8,10},{10,12},{12,14},{14,0},{1,3},{3,5},... | collective-permute-start | bytes 1572872 | tf_op jit(solution)/shard_map/ppermute | solution.py:24
  127.5 1.4 constant_dynamic-slice_fusion.q_ref
  128.9 0.8 fusion.16
  129.8 0.7 fusion.19
  130.5 8.6 %collective-permute-done.15 = bf16[1024,256]{1,0:T(8,128)(2,1)S(1)} collective-permute-done((bf16[1024,256]{1,0:T(8,128)(2,1)S(1)}, bf16[1024,256]{1,0:T(8,128)(2,1)S(1)}, u32[]{:S(2)}, u32[]{:S(2)}) %collective-permute-start.15) | collective-permute-done | bytes 524320 | tf_op jit(solution)/shard_map/ppermute | solution.py:24
  139.1 1.3 collective-permute-done.14
  140.5 0.3 select_select_fusion.w_ref
  140.8 0.7 multiply_exponential_fusion.3
  141.5 2.7 %block_error.1 = f32[1024,256]{1,0:T(8,128)S(1)} custom-call(f32[1024,1024]{1,0:T(8,128)S(1)} %copy-done.2, bf16[1024,256]{1,0:T(8,128)(2,1)S(1)} %select_select_fusion.w_ref, f32[1024,256]{1,0:T(8,128)S(1)} %constant_dynamic-slice_fusion.q_ref), custom_call_target="tpu_custom_call" | custom-call | flops 1610612736 | bytes 4194304 | tf_op jit(solution)/shard_map/block_error/pallas_call | solution.py:130
  144.3 0.1 multiply_round-nearest-even_fusion
  144.4 0.1 fusion.3.e0
  144.5 2.1 %fusion.5 = f32[208,1024]{1,0:T(8,128)S(1)} fusion(f32[4,208,1024]{2,1,0:T(8,128)} %bitcast.39, s32[]{:T(128)S(6)} %select_n.177, s16[224,1024]{1,0:T(8,128)(2,1)} %collective-permute-done.17, s16[224,1024]{1,0:T(8,128)(2,1)} %collective-permute-done.16, f32[208]{0:T(256)S(1)} %bitcast.41, f32[208]{0:T(256)S(1)} %bitcast.42, f32[208]{0:T(256)S(1)} %bitcast.43, ...), kind=kLoop, calls=%fused_computation.14 | loop fusion | flops 1916928 | bytes 2984388 | tf_op jit(solution)/shard_map/add | solution.py:275
  146.6 0.1 collective-permute-start.20
  146.6 2.3 %collective-permute-start.19 = (s16[1040,256]{1,0:T(8,128)(2,1)S(1)}, s16[1040,256]{1,0:T(8,128)(2,1)S(1)}, u32[]{:S(2)}, u32[]{:S(2)}) collective-permute-start(s16[1040,256]{1,0:T(8,128)(2,1)S(1)} %fusion.3.e0), channel_id=1, source_target_pairs={{0,1},{2,3},{4,5},{6,7},{8,9},{10,11},{12,13},{14,15},{16,17},{18,... | collective-permute-start | bytes 1597448 | tf_op jit(solution)/shard_map/ppermute | solution.py:290
  148.9 1.3 collective-permute-start.18
  150.2 0.1 abs_reduce_fusion.2
  150.4 0.2 convert_convert_fusion.1
  150.6 19.1 %all-gather.8 = s16[1792,1024]{1,0:T(8,128)(2,1)S(1)} all-gather(s16[224,1024]{1,0:T(8,128)(2,1)S(1)} %pad_add_fusion.1), channel_id=3, replica_groups=mesh['y'=4,'core'=2,'xl'=2,'z'=8,'xh'=2] {'y','core'}, dimensions={0}, use_global_device_ids=true | all-gather | bytes 4128768 | tf_op jit(solution)/shard_map/all_gather | solution.py:284
  169.8 0.3 mul.219.scale_ref
  170.1 2.5 %collective-permute-done.18.e1 = s16[1040,256]{1,0:T(8,128)(2,1)S(1)} collective-permute-done((s16[1040,256]{1,0:T(8,128)(2,1)S(1)}, s16[1040,256]{1,0:T(8,128)(2,1)S(1)}, u32[]{:S(2)}, u32[]{:S(2)}) %collective-permute-start.18) | collective-permute-done | bytes 532512 | tf_op jit(solution)/shard_map/ppermute | solution.py:290
  172.6 14.6 %apply_update.1 = bf16[1664,1024]{1,0:T(8,128)(2,1)} custom-call(s32[2]{0:T(128)S(1)} %pad_add_fusion.2.scalars, s16[4,2,224,1024]{3,2,1,0:T(8,128)(2,1)S(1)} %bitcast.37, f32[4,2,208,1]{3,2,1,0:T(8,128)S(1)} %mul.219.scale_ref, s16[1040,256]{1,0:T(8,128)(2,1)S(1)} %fusion.3.e0, s16[1040,256]{1,0:T(8,128)(2,1)S(1)} %collective-permute-done.18.e1, ...), custom_call_target="tpu_custom_call" | custom-call | flops 10468982784 | bytes 12320768 | tf_op jit(solution)/shard_map/apply_update/pallas_call | solution.py:180
  (64 shorter events, 1.4 us)
Async XLA Ops:
  6.5 0.9 copy-start
  6.5 18.0 %copy-start.4 = (bf16[512,1664]{1,0:T(8,128)(2,1)S(1)}, bf16[512,1664]{1,0:T(8,128)(2,1)}, u32[]{:S(2)}) copy-start(bf16[512,1664]{1,0:T(8,128)(2,1)} %src_ref.1) | copy-start | bytes 5111812
  6.5 117.1 %all-gather.6.cloned.1.call-start = ((), (), s32[]{:S(2)}) async-start(), calls=%async_computation | async-start | bytes 4259840 | tf_op jit(solution)/shard_map/all_gather | solution.py:230
  13.8 19.5 %collective-permute-start = (bf16[128,1024]{1,0:T(8,128)(2,1)}, bf16[128,1024]{1,0:T(8,128)(2,1)}, u32[]{:S(2)}, u32[]{:S(2)}) collective-permute-start(bf16[128,1024]{1,0:T(8,128)(2,1)} %get-tuple-element.32), channel_id=1, source_target_pairs={{0,16},{2,18},{4,20},{6,22},{8,24},{10,26},{12,28},{14,30},{1,17},... | collective-permute-start | bytes 786440 | tf_op jit(solution)/shard_map/ppermute | solution.py:65
  17.9 18.0 %collective-permute-start.1 = (bf16[128,1024]{1,0:T(8,128)(2,1)}, bf16[128,1024]{1,0:T(8,128)(2,1)}, u32[]{:S(2)}, u32[]{:S(2)}) collective-permute-start(bf16[128,1024]{1,0:T(8,128)(2,1)} %get-tuple-element.33), channel_id=1, source_target_pairs={{0,1},{2,3},{4,5},{6,7},{8,9},{10,11},{12,13},{14,15},{1,0},{3,2},... | collective-permute-start | bytes 786440 | tf_op jit(solution)/shard_map/ppermute | solution.py:65
  22.5 14.8 %collective-permute-start.2 = (bf16[128,1024]{1,0:T(8,128)(2,1)}, bf16[128,1024]{1,0:T(8,128)(2,1)}, u32[]{:S(2)}, u32[]{:S(2)}) collective-permute-start(bf16[128,1024]{1,0:T(8,128)(2,1)} %get-tuple-element.34), channel_id=1, source_target_pairs={{0,17},{2,19},{4,21},{6,23},{8,25},{10,27},{12,29},{14,31},{1,16},... | collective-permute-start | bytes 786440 | tf_op jit(solution)/shard_map/ppermute | solution.py:65
  26.0 19.2 %collective-permute-start.5 = (bf16[512,832]{0,1:T(8,128)(2,1)S(1)}, bf16[512,832]{0,1:T(8,128)(2,1)S(1)}, u32[]{:S(2)}, u32[]{:S(2)}) collective-permute-start(bf16[512,832]{0,1:T(8,128)(2,1)S(1)} %constant_dynamic-slice_fusion.1), channel_id=1, source_target_pairs={{0,32},{32,0},{1,33},{33,1},{2,34},{34,2},{3,35},{35,3},{4,36},{36... | collective-permute-start | bytes 2555912 | tf_op jit(solution)/shard_map/ppermute | solution.py:24
  30.8 38.6 %collective-permute-start.8 = (bf16[1024,256]{1,0:T(8,128)(2,1)}, bf16[1024,256]{1,0:T(8,128)(2,1)}, u32[]{:S(2)}, u32[]{:S(2)}) collective-permute-start(bf16[1024,256]{1,0:T(8,128)(2,1)} %get-tuple-element.39), channel_id=1, source_target_pairs={{0,16},{2,18},{4,20},{6,22},{8,24},{10,26},{12,28},{14,30},{1,17},... | collective-permute-start | bytes 1572872 | tf_op jit(solution)/shard_map/ppermute | solution.py:65
  33.2 36.1 %collective-permute-start.9 = (bf16[1024,256]{1,0:T(8,128)(2,1)}, bf16[1024,256]{1,0:T(8,128)(2,1)S(1)}, u32[]{:S(2)}, u32[]{:S(2)}) collective-permute-start(bf16[1024,256]{1,0:T(8,128)(2,1)} %get-tuple-element.40), channel_id=1, source_target_pairs={{0,1},{2,3},{4,5},{6,7},{8,9},{10,11},{12,13},{14,15},{1,0},{3,2},... | collective-permute-start | bytes 1572872 | tf_op jit(solution)/shard_map/ppermute | solution.py:65
  36.0 33.4 %collective-permute-start.10 = (bf16[1024,256]{1,0:T(8,128)(2,1)}, bf16[1024,256]{1,0:T(8,128)(2,1)S(1)}, u32[]{:S(2)}, u32[]{:S(2)}) collective-permute-start(bf16[1024,256]{1,0:T(8,128)(2,1)} %get-tuple-element.41), channel_id=1, source_target_pairs={{0,17},{2,19},{4,21},{6,23},{8,25},{10,27},{12,29},{14,31},{1,16},... | collective-permute-start | bytes 1572872 | tf_op jit(solution)/shard_map/ppermute | solution.py:65
  38.4 24.5 %collective-permute-start.4 = (bf16[128,1024]{1,0:T(8,128)(2,1)S(1)}, bf16[128,1024]{1,0:T(8,128)(2,1)S(1)}, u32[]{:S(2)}, u32[]{:S(2)}) collective-permute-start(bf16[128,1024]{1,0:T(8,128)(2,1)S(1)} %select_select_fusion.5), channel_id=1, source_target_pairs={{0,10},{2,12},{4,14},{6,0},{8,2},{10,4},{12,6},{14,8},{1,11},{3,13... | collective-permute-start | bytes 786440 | tf_op jit(solution)/shard_map/ppermute | solution.py:24
  45.2 22.0 %collective-permute-start.3 = (bf16[128,1024]{1,0:T(8,128)(2,1)S(1)}, bf16[128,1024]{1,0:T(8,128)(2,1)S(1)}, u32[]{:S(2)}, u32[]{:S(2)}) collective-permute-start(bf16[128,1024]{1,0:T(8,128)(2,1)S(1)} %select_select_fusion.5), channel_id=1, source_target_pairs={{0,6},{2,8},{4,10},{6,12},{8,14},{10,0},{12,2},{14,4},{1,7},{3,9},... | collective-permute-start | bytes 786440 | tf_op jit(solution)/shard_map/ppermute | solution.py:24
  45.8 23.6 %copy-start.7 = (bf16[1024,256]{1,0:T(8,128)(2,1)S(1)}, bf16[1024,256]{1,0:T(8,128)(2,1)}, u32[]{:S(2)}) copy-start(bf16[1024,256]{1,0:T(8,128)(2,1)} %get-tuple-element.38) | copy-start | bytes 1572868
  67.2 10.3 %collective-permute-start.7 = (bf16[128,1024]{1,0:T(8,128)(2,1)S(1)}, bf16[128,1024]{1,0:T(8,128)(2,1)S(1)}, u32[]{:S(2)}, u32[]{:S(2)}) collective-permute-start(bf16[128,1024]{1,0:T(8,128)(2,1)S(1)} %select_select_fusion.4), channel_id=1, source_target_pairs={{0,14},{2,0},{4,2},{6,4},{8,6},{10,8},{12,10},{14,12},{1,15},{3,1}... | collective-permute-start | bytes 786440 | tf_op jit(solution)/shard_map/ppermute | solution.py:24
  67.7 9.8 %collective-permute-start.6 = (bf16[128,1024]{1,0:T(8,128)(2,1)S(1)}, bf16[128,1024]{1,0:T(8,128)(2,1)S(1)}, u32[]{:S(2)}, u32[]{:S(2)}) collective-permute-start(bf16[128,1024]{1,0:T(8,128)(2,1)S(1)} %select_select_fusion.4), channel_id=1, source_target_pairs={{0,2},{2,4},{4,6},{6,8},{8,10},{10,12},{12,14},{14,0},{1,3},{3,5},... | collective-permute-start | bytes 786440 | tf_op jit(solution)/shard_map/ppermute | solution.py:24
  77.6 41.6 %collective-permute-start.13 = (bf16[1024,256]{1,0:T(8,128)(2,1)}, bf16[1024,256]{1,0:T(8,128)(2,1)}, u32[]{:S(2)}, u32[]{:S(2)}) collective-permute-start(bf16[1024,256]{1,0:T(8,128)(2,1)} %select_select_fusion.2), channel_id=1, source_target_pairs={{0,10},{2,12},{4,14},{6,0},{8,2},{10,4},{12,6},{14,8},{1,11},{3,13... | collective-permute-start | bytes 1572872 | tf_op jit(solution)/shard_map/ppermute | solution.py:24
  78.6 45.1 %collective-permute-start.12 = (bf16[1024,256]{1,0:T(8,128)(2,1)}, bf16[1024,256]{1,0:T(8,128)(2,1)}, u32[]{:S(2)}, u32[]{:S(2)}) collective-permute-start(bf16[1024,256]{1,0:T(8,128)(2,1)} %select_select_fusion.2), channel_id=1, source_target_pairs={{0,6},{2,8},{4,10},{6,12},{8,14},{10,0},{12,2},{14,4},{1,7},{3,9},... | collective-permute-start | bytes 1572872 | tf_op jit(solution)/shard_map/ppermute | solution.py:24
  102.2 1.8 copy-start.5
  104.0 3.6 %copy-start.6 = (s32[1024,1024]{1,0:T(8,128)S(1)}, s32[1024,1024]{1,0:T(8,128)}, u32[]{:S(2)}) copy-start(s32[1024,1024]{1,0:T(8,128)} %param.9) | copy-start | bytes 12582916
  104.1 3.3 %copy-start.8 = (s32[8,1024]{1,0:T(8,128)S(1)}, s32[8,1024]{1,0:T(8,128)}, u32[]{:S(2)}) copy-start(s32[8,1024]{1,0:T(8,128)} %param.10) | copy-start | bytes 98308
  104.1 3.3 %copy-start.9 = (f32[16]{0:T(128)S(1)}, f32[16]{0:T(128)}, u32[]{:S(2)}) copy-start(f32[16]{0:T(128)} %param.11) | copy-start | bytes 196
  105.4 35.4 %collective-permute-start.11 = (s16[224,1024]{1,0:T(8,128)(2,1)}, s16[224,1024]{1,0:T(8,128)(2,1)}, u32[]{:S(2)}, u32[]{:S(2)}) collective-permute-start(s16[224,1024]{1,0:T(8,128)(2,1)} %get-tuple-element.65), channel_id=1, source_target_pairs={{0,64},{64,128},{128,192},{192,0},{1,65},{65,129},{129,193},{193,1... | collective-permute-start | bytes 1376264 | tf_op jit(solution)/shard_map/ppermute | solution.py:24
  105.4 23.5 %collective-permute-start.17 = (s16[224,1024]{1,0:T(8,128)(2,1)}, s16[224,1024]{1,0:T(8,128)(2,1)}, u32[]{:S(2)}, u32[]{:S(2)}) collective-permute-start(s16[224,1024]{1,0:T(8,128)(2,1)} %get-tuple-element.66), channel_id=1, source_target_pairs={{0,128},{64,192},{128,0},{192,64},{1,129},{65,193},{129,1},{193,65... | collective-permute-start | bytes 1376264 | tf_op jit(solution)/shard_map/ppermute | solution.py:24
  106.3 23.5 %collective-permute-start.16 = (s16[224,1024]{1,0:T(8,128)(2,1)}, s16[224,1024]{1,0:T(8,128)(2,1)}, u32[]{:S(2)}, u32[]{:S(2)}) collective-permute-start(s16[224,1024]{1,0:T(8,128)(2,1)} %get-tuple-element.67), channel_id=1, source_target_pairs={{0,192},{64,0},{128,64},{192,128},{1,193},{65,1},{129,65},{193,129... | collective-permute-start | bytes 1376264 | tf_op jit(solution)/shard_map/ppermute | solution.py:24
  107.6 3.0 %copy-start.3 = (bf16[1664,1024]{1,0:T(8,128)(2,1)S(1)}, bf16[1664,1024]{1,0:T(8,128)(2,1)}, u32[]{:S(2)}) copy-start(bf16[1664,1024]{1,0:T(8,128)(2,1)} %src_ref.2) | copy-start | bytes 10223620
  125.4 13.8 %collective-permute-start.15 = (bf16[1024,256]{1,0:T(8,128)(2,1)S(1)}, bf16[1024,256]{1,0:T(8,128)(2,1)S(1)}, u32[]{:S(2)}, u32[]{:S(2)}) collective-permute-start(bf16[1024,256]{1,0:T(8,128)(2,1)S(1)} %select_select_fusion.1), channel_id=1, source_target_pairs={{0,14},{2,0},{4,2},{6,4},{8,6},{10,8},{12,10},{14,12},{1,15},{3,1}... | collective-permute-start | bytes 1572872 | tf_op jit(solution)/shard_map/ppermute | solution.py:24
  125.5 15.0 %collective-permute-start.14 = (bf16[1024,256]{1,0:T(8,128)(2,1)S(1)}, bf16[1024,256]{1,0:T(8,128)(2,1)S(1)}, u32[]{:S(2)}, u32[]{:S(2)}) collective-permute-start(bf16[1024,256]{1,0:T(8,128)(2,1)S(1)} %select_select_fusion.1), channel_id=1, source_target_pairs={{0,2},{2,4},{4,6},{6,8},{8,10},{10,12},{12,14},{14,0},{1,3},{3,5},... | collective-permute-start | bytes 1572872 | tf_op jit(solution)/shard_map/ppermute | solution.py:24
  127.5 14.0 %copy-start.2 = (f32[1024,1024]{1,0:T(8,128)S(1)}, f32[1024,1024]{1,0:T(8,128)}, u32[]{:S(2)}) copy-start(f32[1024,1024]{1,0:T(8,128)} %all-gather.6.cloned.1.call-done.inv_ref) | copy-start | bytes 12582916
  146.6 23.5 %collective-permute-start.20 = (s16[1040,256]{1,0:T(8,128)(2,1)S(1)}, s16[1040,256]{1,0:T(8,128)(2,1)S(1)}, u32[]{:S(2)}, u32[]{:S(2)}) collective-permute-start(s16[1040,256]{1,0:T(8,128)(2,1)S(1)} %fusion.3.e0), channel_id=1, source_target_pairs={{0,17},{2,19},{4,21},{6,23},{8,25},{10,27},{12,29},{14,31},{16,0},... | collective-permute-start | bytes 1597448 | tf_op jit(solution)/shard_map/ppermute | solution.py:290
  146.6 23.5 %collective-permute-start.19 = (s16[1040,256]{1,0:T(8,128)(2,1)S(1)}, s16[1040,256]{1,0:T(8,128)(2,1)S(1)}, u32[]{:S(2)}, u32[]{:S(2)}) collective-permute-start(s16[1040,256]{1,0:T(8,128)(2,1)S(1)} %fusion.3.e0), channel_id=1, source_target_pairs={{0,1},{2,3},{4,5},{6,7},{8,9},{10,11},{12,13},{14,15},{16,17},{18,... | collective-permute-start | bytes 1597448 | tf_op jit(solution)/shard_map/ppermute | solution.py:290
  148.9 23.7 %collective-permute-start.18 = (s16[1040,256]{1,0:T(8,128)(2,1)S(1)}, s16[1040,256]{1,0:T(8,128)(2,1)S(1)}, u32[]{:S(2)}, u32[]{:S(2)}) collective-permute-start(s16[1040,256]{1,0:T(8,128)(2,1)S(1)} %fusion.3.e0), channel_id=1, source_target_pairs={{0,16},{2,18},{4,20},{6,22},{8,24},{10,26},{12,28},{14,30},{16,1},... | collective-permute-start | bytes 1597448 | tf_op jit(solution)/shard_map/ppermute | solution.py:290
  172.6 14.6 %copy-start.1 = (f32[32,1024]{1,0:T(8,128)S(1)}, f32[32,1024]{1,0:T(8,128)}, u32[]{:S(2)}) copy-start(f32[32,1024]{1,0:T(8,128)} %param.12) | copy-start | bytes 393220
Sparse Core Ops, SparseCore 0:
  10.1 97.9 all-gather.5
